TPU v7x, 256 devices: a whole 4x4x8 slice. The times are simulated.
256 devices in a mesh: tiles: 64 (over y, x_hi, z), lev: 4 (over x_lo, core).
Axes of the slice: x: 4 (x_hi: 2, x_lo: 2; x = x_hi * 2 + x_lo), y: 4, z: 8, core: 2. Of those that a mesh axis runs over, the one named last changes fastest.
Arguments:
- air_state: float32 [4, 8, 1048576], P(None, 'lev', 'tiles'), may hold values from -6 to 6
- sea_state: float32 [4, 8, 1048576], P(None, 'lev', 'tiles'), may hold values from -6 to 6
- air_courant: float32 [8, 1048576], P('lev', 'tiles'), may hold values from -0.9 to 0.9
- sea_courant: float32 [8, 1048576], P('lev', 'tiles'), may hold values from -0.9 to 0.9
- air_mixing: float32 [8, 1048576], P(None, 'tiles'), may hold values from 0.2 to 3
- sea_mixing: float32 [8, 1048576], P(None, 'tiles'), may hold values from 0.2 to 3
- upward_weight: bfloat16 [16384, 2, 4096], P('tiles'), may hold values from 0 to 0.03125
- upward_target: int32 [16384, 2], P('tiles'), may hold values from 0 to 63, all different within a row; in each aligned block of 256 rows (0 to 255, 256 to 511, ...) at most 16 rows name the same one
- upward_block: int32 [16384, 2], P('tiles'), may hold values from 0 to 255
- downward_weight: bfloat16 [16384, 2, 4096], P('tiles'), may hold values from 0 to 0.03125
- downward_target: int32 [16384, 2], P('tiles'), may hold values from 0 to 63, all different within a row; in each aligned block of 256 rows (0 to 255, 256 to 511, ...) at most 16 rows name the same one
- downward_block: int32 [16384, 2], P('tiles'), may hold values from 0 to 255
- sea_mask: int32 [16384], P('tiles'), may hold values 0 or 1
Outputs:
- air_out: float32 [4, 8, 1048576], P('lev', None, 'tiles')
- sea_out: float32 [4, 8, 1048576], P('lev', None, 'tiles')
Inputs may be any that keep to these rules, and one draw needn't show every extreme that they name: `upward_target`: each row names 2 different tiles indices; among the 256 rows of one tiles index no tiles index is named more than 16 times, a bound that some block reaches. `downward_target`: each row names 2 different tiles indices; among the 256 rows of one tiles index no tiles index is named more than 16 times, a bound that some block reaches.
All inputs are finite; a program needn't handle non-finite values. No bound on the sum of `sea_mask` on one device may be relied on, other than what follows from the above.
Results may differ from a plain program's by a relative error of at most 0.0003.
Values sent between devices are 32-bit elements; how exact they have to be, the bound alone decides.
No kernel may reach another device: no remote copies, remote signals or barrier semaphores. Data moves between devices by JAX's collectives and lax.ppermute only.
A program may use at most 128 MiB of HBM per device.

v0:
```python
import functools

import jax
import jax.numpy as jnp
from jax import lax
from jax.experimental import pallas as pl
from jax.experimental.pallas import tpu as pltpu
from jax.sharding import PartitionSpec as P

BLOCK = 64
LANES = 128
SLOTS = 16
F32 = jnp.float32
BF16 = jnp.bfloat16
NT = (((1,), (1,)), ((), ()))
NN = (((1,), (0,)), ((), ()))


def dot(a, b, dims=NN):
    return lax.dot_general(a, b, dims, preferred_element_type=F32)


def split(x):
    high = x.astype(BF16)
    return high, (x - high.astype(F32)).astype(BF16)


def iota(shape, dim):
    return lax.broadcasted_iota(jnp.int32, shape, dim)


def low_half(shape):
    return iota(shape, len(shape) - 1) < BLOCK


def swap(x):
    return pltpu.roll(x, BLOCK, x.ndim - 1)


class Fetched:
    def __init__(self, source, buf, sem):
        self.copy = pltpu.make_async_copy(source, buf, sem)
        self.shape = source.shape
        self.buf = buf
        self.waiting = True
        self.copy.start()

    def get(self):
        if self.waiting:
            self.copy.wait()
            self.waiting = False
        return self.buf


def onehot(condition):
    return jnp.where(condition, 1.0, 0.0).astype(BF16)


def prepare_kernel(tiles, ut, ub, dt, db, mask, up_out, down_out, label_out, mask_out, order_out):
    blocks = ut.shape[1]
    groups = blocks // 2
    entries = 2 * blocks
    source, lane = iota((blocks, blocks), 0), iota((blocks, blocks), 1)
    turn = onehot(source == 2 * (lane & (groups - 1)) + lane // groups)
    lists = [x.get()[...] for x in (ut, ub, dt, db, mask)]
    stacked = jnp.concatenate([x.astype(F32) for x in lists], 0)
    stacked = jnp.concatenate([stacked, jnp.zeros((16 - stacked.shape[0], blocks), F32)], 0)
    stacked = dot(stacked.astype(BF16), turn)

    def entry_row(at):
        pair = stacked[at : at + 2]
        parts = [
            pair[k : k + 1, odd * groups : (odd + 1) * groups]
            for odd in range(2)
            for k in range(2)
        ]
        return jnp.concatenate(parts, 1)

    tile_row = iota((tiles, entries), 0).astype(F32)
    earlier = onehot(iota((entries, entries), 0) < iota((entries, entries), 1))
    labels = None
    for first, out, base in ((0, up_out, 0), (4, down_out, SLOTS)):
        target, block = entry_row(first), entry_row(first + 2)
        named = jnp.where(target == tile_row, 1.0, 0.0)
        rank = jnp.sum(named * dot(named.astype(BF16), earlier), 0, keepdims=True)
        rank = rank.astype(jnp.int32)
        target = target.astype(jnp.int32)
        rows = tiles * SLOTS // 2
        at = (rank // 2) * tiles + target
        for half in range(2):
            wanted = jnp.where((rank & 1) == half, at, -1)
            out[half] = onehot(iota((rows, entries), 0) == wanted)
        carried = (named * (block + 1.0)).astype(BF16)
        chosen = onehot(iota((LANES, entries), 0) == rank + base)
        term = dot(carried, chosen, NT)
        labels = term if labels is None else labels + term
    label_out[...] = labels
    diagonal = iota((groups, groups), 0) == iota((groups, groups), 1)
    spread = None
    for odd in range(2):
        row = stacked[8:9, odd * groups : (odd + 1) * groups]
        picked = jnp.where(diagonal, row, 0.0).astype(BF16)
        side = onehot((iota((groups, LANES), 1) // BLOCK) == odd)
        term = dot(picked, side)
        spread = term if spread is None else spread + term
    mask_out[...] = spread
    row, column = iota((256, 512), 0), iota((256, 512), 1)
    same = ((row >> 6) & 1) * 2 + (row & 1) == (column >> 7)
    cell = ((row >> 1) & 31) * 2 + (row >> 7)
    order_out[...] = onehot(same & (cell == (column & 63)))


def upwind(x, positive, negative, below, above):
    return x - positive * (x - below) - negative * (above - x)


def surface_kernel(sea, air, sea_c, air_c, o0, o1, o2, o3, first_out, last_out, sbuf, abuf, sems):
    rows = sea_c.shape[0] // 2
    size = 2 * rows
    outs = (o0, o1, o2, o3)
    order = (1, 2, 3, 0)

    def copy(n, d):
        state, buf = ((sea, sbuf), (air, abuf))[n]
        return pltpu.make_async_copy(state.at[pl.ds(d * size, size)], buf.at[d], sems.at[n, d])

    for d in order:
        for n in range(2):
            copy(n, d).start()
    lane = iota((rows, LANES), 1)
    first = lane == 0
    last = lane == LANES - 1
    signs = []
    for n, speed in enumerate((sea_c, air_c)):
        c = speed.get()[pl.ds(0, rows, stride=2), :]
        signs.append((jnp.maximum(c, 0.0), jnp.minimum(c, 0.0)))
    for d in order:
        out = outs[d]
        for n, (buf, speed) in enumerate(((sbuf, sea_c), (abuf, air_c))):
            copy(n, d).wait()
            positive, negative = signs[n]
            x = buf[d, pl.ds(0, rows, stride=2), :]
            for step in range(2):
                below = pltpu.roll(x, 1, 1)
                below = jnp.where(first, pltpu.roll(below, 1, 0), below)
                above = pltpu.roll(x, LANES - 1, 1)
                above = jnp.where(last, pltpu.roll(above, rows - 1, 0), above)
                x = upwind(x, positive, negative, below, above)
            out[n * rows : (n + 1) * rows, :] = x
            at = 2 * rows + n
            out[at : at + 1, :] = buf[d, 0:1, :]
            out[at + 2 : at + 3, :] = speed.get()[0:1, :]
            out[at + 4 : at + 5, :] = buf[d, size - 2 : size - 1, :]
            out[at + 6 : at + 7, :] = speed.get()[size - 2 : size - 1, :]
            at = n * 10 + 2 * d
            first_out[at : at + 2, :] = buf[d, 0:2, :]
            last_out[at : at + 2, :] = buf[d, size - 2 : size, :]
    for n, speed in enumerate((sea_c, air_c)):
        at = n * 10 + 8
        first_out[at : at + 2, :] = speed.get()[0:2, :]
        last_out[at : at + 2, :] = speed.get()[size - 2 : size, :]


def advect_kernel(
    fields, sea, air, sea_c, air_c, left, right, lev, o0, o1, o2, o3, xbuf, cbuf
):
    rows = sea_c.shape[0] // 2
    total = rows + 16
    lane = iota((total, LANES), 1)
    first = lane == 0
    last = lane == LANES - 1

    def extended(buf, middle, at):
        buf[0:8, :] = jnp.broadcast_to(left.get()[pl.ds(at, 1), :], (8, LANES))
        buf[8 : rows + 8, :] = middle
        buf[rows + 8 :, :] = jnp.broadcast_to(right.get()[pl.ds(at, 1), :], (8, LANES))
        return buf[...]

    for n, (state, courant) in enumerate(((sea, sea_c), (air, air_c))):
        for level in range(2):
            c = courant.get()[pl.ds(level, rows, stride=2), :]
            c = extended(cbuf, c, n * 10 + 8 + level)
            positive, negative = jnp.maximum(c, 0.0), jnp.minimum(c, 0.0)
            for d, out in enumerate((o0, o1, o2, o3)):
                field = lax.rem(lev[0] + d, fields)
                at = field * 2 * rows + level
                x = state.get()[pl.ds(at, rows, stride=2), :]
                x = extended(xbuf, x, n * 10 + 2 * field + level)
                for step in range(2):
                    below = pltpu.roll(x, 1, 1)
                    below = jnp.where(first, pltpu.roll(below, 1, 0), below)
                    above = pltpu.roll(x, LANES - 1, 1)
                    above = jnp.where(last, pltpu.roll(above, total - 1, 0), above)
                    x = upwind(x, positive, negative, below, above)
                at = (2 * n + level) * rows
                out[at : at + rows, :] = x[8 : rows + 8, :]


def mended(ends, left, right):
    low = low_half((2, LANES))
    out = []
    for at, outer, kept in ((0, left, low), (4, right, jnp.logical_not(low))):
        x = jnp.where(kept, ends[at : at + 2, :], outer[4 - at : 6 - at, :])
        c = jnp.where(kept, ends[at + 2 : at + 4, :], outer[6 - at : 8 - at, :])
        positive, negative = jnp.maximum(c, 0.0), jnp.minimum(c, 0.0)
        for step in range(2):
            x = upwind(x, positive, negative, pltpu.roll(x, 1, 1), pltpu.roll(x, LANES - 1, 1))
        out.append(x)
    return out


def mend(row, mended_row, at_end):
    lane = iota(row.shape, 1)
    return jnp.where(lane >= LANES - 2 if at_end else lane < 2, mended_row, row)


def weight_copies(weight, wbuf, sems):
    pieces = sems.shape[0]
    size = weight.shape[0] // pieces
    return [
        pltpu.make_async_copy(
            weight.at[pl.ds(n * size, size)], wbuf.at[pl.ds(n * size, size)], sems.at[n]
        )
        for n in range(pieces)
    ]


def product_rows(values, ones, put):
    half = low_half(values.shape)
    zero = jnp.zeros(values.shape, F32)
    high = values.astype(BF16).astype(F32)
    sets = [(0, 2, high), (2, 2, values - high)]
    if ones is not None:
        sets.append((8, 0, ones))
    for base, gap, x in sets:
        turned = swap(x)
        for odd in range(2):
            for parity in range(2):
                row = base + odd * (2 + gap) + parity
                chosen = turned if odd != parity else x
                put(row, jnp.where(half == (parity == 0), chosen, zero))
    if ones is not None:
        for row in range(12, 16):
            put(row, zero)


def product_sums(got, with_ones):
    half = low_half(got(0).shape)
    out = [jnp.where(half, got(p) + got(2 + p), got(4 + p) + got(6 + p)) for p in range(2)]
    if with_ones:
        out.extend(jnp.where(half, got(8 + p), got(10 + p)) for p in range(2))
    return out


def products(values, ones, copies, wbuf, lhs, res):
    groups = values.shape[0]
    count = 8 if ones is None else 16

    def put(row, x):
        lhs[pl.ds(row, groups, stride=count), :] = x

    product_rows(values, ones, put)

    def body(g, carry):
        at = pl.ds(pl.multiple_of(g * count, count), count)
        w = wbuf[pl.ds(pl.multiple_of(g * LANES, LANES), LANES), :]
        res[at, :] = dot(lhs[at, :].astype(BF16), w, NT)
        return carry

    each = groups // len(copies)
    for n, copy in enumerate(copies):
        copy.wait()
        lax.fori_loop(n * each, (n + 1) * each, body, 0, unroll=8)
    return product_sums(lambda row: res[pl.ds(row, groups, stride=count), :], ones is not None)


def entry_values(sums, order):
    def ordered(pair):
        high, low = split(jnp.concatenate(pair, 1))
        return dot(high, order), dot(low, order)

    y = ordered(sums[:2])
    if len(sums) > 2:
        half = low_half(y[0].shape[:1] + (LANES,))
        half = jnp.concatenate([half] * 4, 1)
        y = [jnp.where(half, a, b) for a, b in zip(y, ordered(sums[2:]))]
    terms = []
    for part in y:
        part = part.astype(BF16)
        terms.append(jnp.concatenate([part[:, q * LANES : (q + 1) * LANES] for q in range(4)], 0))
    return jnp.concatenate(terms, 1)


def dispatched(place, entries):
    out = []
    for half in range(2):
        slots = dot(place[half], entries)
        out.append(slots[:, :LANES] + slots[:, LANES:])
    return out


def up_kernel(surface, mask, weight, sums_out, wbuf, lhs, res, wsems):
    groups = mask.shape[0]
    copies = weight_copies(weight, wbuf, wsems)
    for copy in copies:
        copy.start()
    mask_value = mask.get()[...]
    values = surface.get()[0:groups, :] * mask_value
    sums = products(values, mask_value, copies, wbuf, lhs, res)
    sums_out[...] = jnp.concatenate(sums, 1)


def slot_kernel(
    sums, surface, left, right, mask, weight, place, order, labels, out, wbuf, lhs, sems
):
    groups = mask.shape[0]
    tiles = labels.shape[0]
    copies = [
        pltpu.make_async_copy(weight.at[pl.ds(at, LANES)], wbuf.at[n], sems.at[n])
        for n, at in enumerate((0, (groups - 1) * LANES))
    ]
    for copy in copies:
        copy.start()
    surface, mask, sums = surface.get(), mask.get(), sums.get()
    mended_rows = mended(
        surface[2 * groups : 2 * groups + 8, :], left.get()[...], right.get()[...]
    )
    row_at = iota((groups, LANES), 0)
    parts = [sums[:, n * LANES : (n + 1) * LANES] for n in range(4)]
    for n, g in enumerate((0, groups - 1)):
        row = surface[g : g + 1, :]
        row = mend(row, mended_rows[n][0:1], n == 1) * mask[g : g + 1, :]

        def put(at, x):
            lhs[at : at + 1, :] = x

        product_rows(row, None, put)
        copies[n].wait()
        res = dot(lhs[...].astype(BF16), wbuf[n], NT)
        for p, new in enumerate(product_sums(lambda at: res[at : at + 1], False)):
            parts[p] = jnp.where(row_at == g, new, parts[p])
    even, odd = dispatched(place.get(), entry_values(parts, order.get()[...]))
    half = low_half((tiles, LANES))
    pitch = out.shape[0] // tiles
    for i in range(SLOTS // 2):
        a, b = even[i * tiles : (i + 1) * tiles], odd[i * tiles : (i + 1) * tiles]
        out[pl.ds(i, tiles, stride=pitch), :] = jnp.where(half, a, swap(b))
        out[pl.ds(SLOTS // 2 + i, tiles, stride=pitch), :] = jnp.where(half, swap(a), b)
    out[pl.ds(SLOTS, tiles, stride=pitch), :] = labels.get()[...]


def named_blocks(labels, base, blocks):
    turned = jnp.transpose(jnp.concatenate([labels, labels], 0))
    half = low_half((1, LANES))
    out = []
    for slot_half in range(2):
        row = []
        for i in range(0, SLOTS // 2, 2):
            at = base + 2 * i + slot_half
            row.append(jnp.where(half, turned[at : at + 1], turned[at + 2 : at + 3]))
        row = jnp.concatenate(row, 1).astype(jnp.int32)
        for odd in range(2):
            out.append(onehot(2 * iota((blocks, row.shape[1]), 0) + odd + 1 == row))
    return out


def collected(parts, names):
    halves = []
    for part in parts:
        halves.extend(split(part))
    values = jnp.concatenate(halves, 1)
    sums = [dot(name, values) for name in names]
    half = low_half((sums[0].shape[0], LANES))
    out = []
    for n in range(len(parts)):
        at = 2 * n * LANES
        g = [s[:, at : at + LANES] + s[:, at + LANES : at + 2 * LANES] for s in sums]
        out.append(jnp.where(half, g[0] + swap(g[2]), swap(g[1]) + g[3]))
    return out


def slot_rows(arrived, start, count, tiles):
    pitch = arrived.shape[0] // tiles
    return jnp.concatenate(
        [arrived[pl.ds(start + i, tiles, stride=pitch), :] for i in range(count)], 0
    )


def middle_kernel(
    arrived, surface, left, right, mixing, weight, place, order,
    flux_out, out, label_out, wbuf, lhs, res, wsems,
):
    groups = flux_out.shape[0]
    tiles = label_out.shape[0]
    copies = weight_copies(weight, wbuf, wsems)
    for copy in copies:
        copy.start()
    labels = arrived[pl.ds(SLOTS, tiles, stride=SLOTS + 1), :]
    label_out[...] = labels
    names = named_blocks(labels, 0, groups)
    field = slot_rows(arrived, 0, SLOTS // 2, tiles)
    cover = slot_rows(arrived, SLOTS // 2, SLOTS // 2, tiles)
    received, coverage = collected((field, cover), names)
    surface = surface.get()
    mended_rows = mended(
        surface[2 * groups : 2 * groups + 8, :], left.get()[...], right.get()[...]
    )
    for n, at in enumerate((groups, 2 * groups - 1)):
        surface[at : at + 1, :] = mend(surface[at : at + 1, :], mended_rows[n][1:2], n == 1)
    factor = mixing.get()[pl.ds(0, groups, stride=8), :]
    flux = factor * (coverage * surface[groups : 2 * groups, :] - received)
    flux_out[...] = flux
    sums = products(flux, None, copies, wbuf, lhs, res)
    even, odd = dispatched(place.get(), entry_values(sums, order.get()[...]))
    half = low_half((tiles, LANES))
    pitch = out.shape[0] // tiles
    for i in range(SLOTS // 2):
        a, b = even[i * tiles : (i + 1) * tiles], odd[i * tiles : (i + 1) * tiles]
        out[pl.ds(i, tiles, stride=pitch), :] = jnp.where(half, a, b)


def solve_kernel(with_flux, p0, p1, p2, p3, mixing, extra, lev, *refs):
    if with_flux:
        out, buf, sems = refs
    else:
        out, unit_out, buf, sems = refs
    groups = extra.shape[0]
    chunk = 16
    levels = 8
    base = 2 * groups if with_flux else 0
    copies = []
    for d, part in enumerate((p0, p1, p2, p3)):
        source = lax.rem(lev[0] + 4 - d, 4)
        copies.append(
            pltpu.make_async_copy(
                part.at[pl.ds(base, 2 * groups)], buf.at[source], sems.at[d]
            )
        )
    for copy in copies:
        copy.start()
    kbuf, ebuf = mixing.get(), extra.get()
    for copy in copies:
        copy.wait()

    def body(step, carry):
        at = pl.multiple_of(step * chunk, chunk)
        rows = pl.ds(at, chunk)
        k = [
            kbuf[pl.ds(at * levels + level, chunk, stride=levels), :] for level in range(levels)
        ]
        cs, ds, es = [], [], []
        for level in range(levels):
            r = buf[level // 2, pl.ds((level % 2) * groups + at, chunk), :]
            if level == 0:
                inverse = 1.0 / (1.0 + k[1])
                if with_flux:
                    r = r - ebuf[rows, :]
                else:
                    es.append(k[0] * ebuf[rows, :] * inverse)
                ds.append(r * inverse)
            else:
                total = 1.0 + k[level] - k[level] * cs[-1]
                if level + 1 < levels:
                    total = total + k[level + 1]
                inverse = 1.0 / total
                ds.append((r + k[level] * ds[-1]) * inverse)
                if not with_flux:
                    es.append(k[level] * es[-1] * inverse)
            if level + 1 < levels:
                cs.append(k[level + 1] * inverse)
        for terms, ref in ((ds, out),) if with_flux else ((ds, out), (es, unit_out)):
            x = terms[-1]
            ref[pl.ds(at * levels + levels - 1, chunk, stride=levels), :] = x
            for level in range(levels - 2, -1, -1):
                x = terms[level] + cs[level] * x
                ref[pl.ds(at * levels + level, chunk, stride=levels), :] = x
        return carry

    lax.fori_loop(0, groups // chunk, body, 0)


def last_kernel(arrived, labels, base, unit, out, gain):
    tiles = labels.shape[0]
    groups = gain.shape[0]
    names = named_blocks(labels.get()[...], SLOTS, groups)
    (total,) = collected((slot_rows(arrived, 0, SLOTS // 2, tiles),), names)
    gain[...] = total
    bbuf, ubuf = base.get(), unit.get()

    def body(step, carry):
        at = pl.ds(pl.multiple_of(step * 8, 8), 8)
        out[at, :] = bbuf[at, :] + ubuf[at, :] * gain[pl.ds(step, 1), :]
        return carry

    lax.fori_loop(0, groups, body, 0, unroll=8)


VMEM = pl.BlockSpec(memory_space=pltpu.VMEM)
SMEM = pl.BlockSpec(memory_space=pltpu.SMEM)
HBM = pl.BlockSpec(memory_space=pltpu.HBM)
DMA = pltpu.SemaphoreType.DMA


def call(kernel, shapes, args, spaces, scratch=(), name=None, us=1.0, after=()):
    fetched = [i for i, space in enumerate(spaces) if space == "f"]
    outs = len(shapes) if isinstance(shapes, tuple) else 1

    def body(*refs):
        refs = list(refs)
        del refs[len(args) : len(args) + len(after)]
        end = len(refs) - 2 * len(fetched)
        for n, i in enumerate(fetched):
            refs[i] = Fetched(refs[i], refs[end + n], refs[end + len(fetched) + n])
        kernel(*refs[:end])

    extra = [pltpu.VMEM(args[i].shape, args[i].dtype) for i in fetched]
    extra += [DMA(()) for i in fetched]
    return pl.pallas_call(
        body,
        out_shape=shapes,
        in_specs=[{"v": VMEM, "s": SMEM, "h": HBM, "f": HBM}[space] for space in spaces]
        + [HBM] * len(after),
        out_specs=jax.tree.map(lambda _: VMEM, shapes),
        scratch_shapes=list(scratch) + extra,
        compiler_params=pltpu.CompilerParams(vmem_limit_bytes=64 * 1024 * 1024),
        cost_estimate=pl.CostEstimate(
            flops=0, bytes_accessed=int(us * 3.6e6), transcendentals=0
        ),
        name=name,
    )(*args, *after)


def shape(*dims, dtype=F32):
    return jax.ShapeDtypeStruct(dims, dtype)


def tile_rows(x, lead):
    levels, cells = x.shape[-2:]
    x = x.reshape(lead, levels, cells // LANES, LANES)
    return x.transpose(0, 2, 1, 3).reshape(lead * levels * cells // LANES, LANES)


def weight_rows(w):
    blocks, fan, size = w.shape
    w = w.reshape(blocks, fan, size // LANES, LANES).transpose(0, 2, 1, 3)
    return w.reshape(blocks * fan * size // LANES, LANES)


def on_device(
    air_state,
    sea_state,
    air_courant,
    sea_courant,
    air_mixing,
    sea_mixing,
    upward_weight,
    upward_target,
    upward_block,
    downward_weight,
    downward_target,
    downward_block,
    sea_mask,
):
    fields, pair, cells = air_state.shape
    tiles = lax.axis_size("tiles")
    levs = lax.axis_size("lev")
    rows = cells // LANES
    groups = sea_mask.shape[0] // 2
    lev = lax.axis_index("lev").astype(jnp.int32)
    lev_ref = lev.reshape(1)
    forward = [(i, (i + 1) % tiles) for i in range(tiles)]
    backward = [(b, a) for a, b in forward]
    states = (
        tile_rows(sea_state, fields),
        tile_rows(air_state, fields),
        tile_rows(sea_courant, 1),
        tile_rows(air_courant, 1),
    )
    size = pair * rows

    *parts, rest_first, rest_last = call(
        surface_kernel,
        tuple(shape(size + 8, LANES) for _ in range(4)) + (shape(20, LANES),) * 2,
        states,
        "hhff",
        scratch=[
            pltpu.VMEM((4, size, LANES), F32),
            pltpu.VMEM((4, size, LANES), F32),
            DMA((2, 4)),
        ],
        name="surface",
        us=3.0,
    )
    moved = [lax.ppermute(parts[d], "lev", [(0, d)]) for d in range(1, levs)]
    surface = jnp.where(lev == 0, parts[0], moved[0] + moved[1] + moved[2])
    ends = surface[size:]
    left = lax.ppermute(ends, "tiles", forward)
    right = lax.ppermute(ends, "tiles", backward)
    rest_left = lax.ppermute(rest_last, "tiles", forward)
    rest_right = lax.ppermute(rest_first, "tiles", backward)

    places = tiles * SLOTS // 2
    entries = 4 * groups
    place_up, place_down, labels, mask, order = call(
        functools.partial(prepare_kernel, tiles),
        (
            shape(2, places, entries, dtype=BF16),
            shape(2, places, entries, dtype=BF16),
            shape(tiles, LANES),
            shape(groups, LANES),
            shape(256, 512, dtype=BF16),
        ),
        (
            upward_target.T,
            upward_block.T,
            downward_target.T,
            downward_block.T,
            sea_mask.reshape(1, -1),
        ),
        "fffff",
        name="prepare",
        us=3.0,
        after=(parts[0],),
    )
    air_k = tile_rows(air_mixing, 1)
    sea_k = tile_rows(sea_mixing, 1)
    up_rows = weight_rows(upward_weight)
    down_rows = weight_rows(downward_weight)

    def workspace(count):
        return [
            pltpu.VMEM(up_rows.shape, BF16),
            pltpu.VMEM((groups * count, LANES), F32),
            pltpu.VMEM((groups * count, LANES), F32),
        ]

    sums = call(
        up_kernel,
        shape(groups, 4 * LANES),
        (surface, mask, up_rows),
        "ffh",
        scratch=[*workspace(16), DMA((8,))],
        name="upward",
        us=5.0,
        after=(rest_left, rest_right),
    )
    pitch = SLOTS + 1
    outgoing = call(
        slot_kernel,
        shape(tiles * pitch, LANES),
        (sums, surface, left, right, mask, up_rows, place_up, order, labels),
        "fffffhfff",
        scratch=[
            pltpu.VMEM((2, LANES, LANES), BF16),
            pltpu.VMEM((8, LANES), F32),
            DMA((2,)),
        ],
        name="to_slots",
        us=2.0,
    )

    def over_tiles(x):
        y = x.reshape(tiles, 1, x.size // tiles)
        y = lax.all_to_all(y, "tiles", split_axis=0, concat_axis=0, tiled=True)
        return y.reshape(x.shape)

    rest = call(
        functools.partial(advect_kernel, fields),
        tuple(shape(2 * size, LANES) for _ in range(4)),
        (*states, rest_left, rest_right, lev_ref),
        "ffffffs",
        scratch=[pltpu.VMEM((rows + 16, LANES), F32)] * 2,
        name="advect",
        us=3.0,
        after=(outgoing,),
    )
    rest = [rest[0]] + [
        lax.ppermute(rest[d], "lev", [(i, (i + d) % levs) for i in range(levs)])
        for d in range(1, levs)
    ]
    arrived = over_tiles(outgoing)
    flux, returning, labels_down = call(
        middle_kernel,
        (shape(groups, LANES), shape(tiles * SLOTS // 2, LANES), shape(tiles, LANES)),
        (arrived, surface, left, right, air_k, down_rows, place_down, order),
        "vffffhff",
        scratch=[*workspace(8), DMA((8,))],
        name="middle",
        us=7.0,
        after=tuple(rest[1:]),
    )
    gained = over_tiles(returning)

    column = shape(8 * rows, LANES)

    def solve(with_flux, k, extra, name):
        return call(
            functools.partial(solve_kernel, with_flux),
            column if with_flux else (column, column),
            (*rest, k, extra, lev_ref),
            "hhhhffs",
            scratch=[pltpu.VMEM((4, size, LANES), F32), DMA((4,))],
            name=name,
            us=2.0,
        )

    base, unit = solve(False, sea_k, mask, "solve_sea")
    air_out = solve(True, air_k, flux, "solve_air")
    sea_out = call(
        last_kernel,
        column,
        (gained, labels_down, base, unit),
        "vfff",
        scratch=[pltpu.VMEM((rows, LANES), F32)],
        name="last",
        us=2.0,
    )

    def levels_first(x):
        return x.reshape(rows, 8, LANES).transpose(1, 0, 2).reshape(1, 8, cells)

    return levels_first(air_out), levels_first(sea_out)


def solution(mesh):
    return jax.shard_map(
        on_device,
        mesh=mesh,
        in_specs=(
            P(None, "lev", "tiles"),
            P(None, "lev", "tiles"),
            P("lev", "tiles"),
            P("lev", "tiles"),
            P(None, "tiles"),
            P(None, "tiles"),
            P("tiles", None, None),
            P("tiles", None),
            P("tiles", None),
            P("tiles", None, None),
            P("tiles", None),
            P("tiles", None),
            P("tiles"),
        ),
        out_specs=(P("lev", None, "tiles"), P("lev", None, "tiles")),
        check_vma=False,
    )
```

profile of v0, /device:TPU:1, one launch (start us, length us, event | category | flops | bytes accessed | tf_op | source)
XLA Modules:
  0.0 108.6 jit_solution(783497716107098141)
XLA Ops:
  0.6 3.7 %surface.1 = (f32[264,128]{1,0:T(8,128)}, f32[264,128]{1,0:T(8,128)}, f32[264,128]{1,0:T(8,128)}, f32[264,128]{1,0:T(8,128)}, f32[20,128]{1,0:T(8,128)}, /*index=5*/f32[20,128]{1,0:T(8,128)}) custom-call(f32[1024,128]{1,0:T(8,128)} %bitcast.66, f32[1024,128]{1,0:T(8,128)} %bitcast.68, f32[256,128]{1,0:T(8,128)} %bitcast.72, f32[256,128]{1,0:T(8,128)} %bitcast.74), custom_call_target="tpu_custom_call" | custom-call | bytes 10800000 | tf_op jit(solution)/shard_map/surface/pallas_call | solution.py:518
  4.3 0.7 collective-permute-start.4
  5.0 1.3 %collective-permute-start.2 = (f32[264,128]{1,0:T(8,128)}, f32[264,128]{1,0:T(8,128)S(1)}, u32[]{:S(2)}, u32[]{:S(2)}) collective-permute-start(f32[264,128]{1,0:T(8,128)} %get-tuple-element.25), channel_id=1, source_target_pairs={{0,1},{4,5},{8,9},{12,13},{16,17},{20,21},{24,25},{28,29},{32,33},... | collective-permute-start | bytes 405512 | tf_op jit(solution)/shard_map/ppermute | solution.py:594
  6.3 0.7 collective-permute-start.3
  7.0 2.5 %collective-permute-start = (f32[20,128]{1,0:T(8,128)}, f32[20,128]{1,0:T(8,128)}, u32[]{:S(2)}, u32[]{:S(2)}) collective-permute-start(f32[20,128]{1,0:T(8,128)} %get-tuple-element.22), channel_id=1, source_target_pairs={{0,4},{4,8},{8,12},{12,16},{16,20},{20,24},{24,28},{28,32},{32,36}... | collective-permute-start | bytes 30728 | tf_op jit(solution)/shard_map/ppermute | solution.py:599
  9.5 8.9 %collective-permute-start.1 = (f32[20,128]{1,0:T(8,128)}, f32[20,128]{1,0:T(8,128)}, u32[]{:S(2)}, u32[]{:S(2)}) collective-permute-start(f32[20,128]{1,0:T(8,128)} %get-tuple-element.23), channel_id=1, source_target_pairs={{4,0},{8,4},{12,8},{16,12},{20,16},{24,20},{28,24},{32,28},{36,32}... | collective-permute-start | bytes 30728 | tf_op jit(solution)/shard_map/ppermute | solution.py:600
  18.5 0.0 collective-permute-done.4
  18.5 0.0 collective-permute-done.2
  18.5 0.0 collective-permute-done.3
  18.5 0.1 add_select_fusion.refs_0_.refs_1_
  18.5 0.0 copy-start
  18.6 0.6 copy-done
  19.2 0.6 slice.4
  19.8 0.0 collective-permute-start.5
  19.8 7.2 %collective-permute-start.6 = (f32[8,128]{1,0:T(8,128)}, f32[8,128]{1,0:T(8,128)}, u32[]{:S(2)}, u32[]{:S(2)}) collective-permute-start(f32[8,128]{1,0:T(8,128)} %slice.4), channel_id=1, source_target_pairs={{4,0},{8,4},{12,8},{16,12},{20,16},{24,20},{28,24},{32,28},{36,32}... | collective-permute-start | bytes 12296 | tf_op jit(solution)/shard_map/ppermute | solution.py:598
  27.0 3.3 %prepare.1 = (bf16[2,512,512]{2,1,0:T(8,128)(2,1)}, bf16[2,512,512]{2,1,0:T(8,128)(2,1)}, f32[64,128]{1,0:T(8,128)}, f32[128,128]{1,0:T(8,128)}, bf16[256,512]{1,0:T(8,128)(2,1)}) custom-call(s32[2,256]{1,0:T(2,128)} %bitcast.78, s32[2,256]{1,0:T(2,128)} %bitcast.79, s32[2,256]{1,0:T(2,128)} %bitcast.80, s32[2,256]{1,0:T(2,128)} %bitcast.81, ...), custom_call_target="tpu_custom_call" | custom-call | bytes 10800000 | tf_op jit(solution)/shard_map/prepare/pallas_call | solution.py:518
  30.2 0.0 collective-permute-done.refs_3_.refs_4_
  30.3 0.0 collective-permute-done.1.refs_4_.refs_5_
  30.3 7.5 %upward.1.refs_0_ = f32[128,512]{1,0:T(8,128)} custom-call(f32[264,128]{1,0:T(8,128)} %copy-done, f32[128,128]{1,0:T(8,128)} %get-tuple-element.28.refs_1_.refs_4_.refs_5_, bf16[16384,128]{1,0:T(8,128)(2,1)} %bitcast.60, f32[20,128]{1,0:T(8,128)} %collective-permute-done.refs_3_.refs_4_, f32[20,128]{1,0:T(8,128)} %collective-permute-done.1.refs_4_.refs_5_), custom_call_target="tpu_custom_call" | custom-call | bytes 18000000 | tf_op jit(solution)/shard_map/upward/pallas_call | solution.py:518
  37.7 0.0 collective-permute-done.5.refs_2_
  37.7 0.0 collective-permute-done.6.refs_3_
  37.8 3.3 %to_slots.1.refs_7_ = f32[1088,128]{1,0:T(8,128)} custom-call(f32[128,512]{1,0:T(8,128)} %upward.1.refs_0_, f32[264,128]{1,0:T(8,128)} %copy-done, f32[8,128]{1,0:T(8,128)} %collective-permute-done.5.refs_2_, f32[8,128]{1,0:T(8,128)} %collective-permute-done.6.refs_3_, f32[128,128]{1,0:T(8,128)} %get-tuple-element.28.refs_1_.refs_4_.refs_5_, ...), custom_call_target="tpu_custom_call" | custom-call | bytes 7200000 | tf_op jit(solution)/shard_map/to_slots/pallas_call | solution.py:518
  41.0 5.5 %all-to-all-start = ((f32[64,1,2176]{2,1,0:T(1,128)}), f32[64,1,2176]{2,1,0:T(1,128)}, u32[]{:S(2)}, u32[]{:S(2)}) async-start(f32[64,1,2176]{2,1,0:T(1,128)} %bitcast.62), calls=%async_computation | async-start | bytes 1114112 | tf_op jit(solution)/shard_map/all_to_all | solution.py:664
  46.5 4.3 %advect.1 = (f32[512,128]{1,0:T(8,128)}, f32[512,128]{1,0:T(8,128)}, f32[512,128]{1,0:T(8,128)}, f32[512,128]{1,0:T(8,128)}) custom-call(f32[1024,128]{1,0:T(8,128)} %bitcast.67, f32[1024,128]{1,0:T(8,128)} %bitcast.69, f32[256,128]{1,0:T(8,128)} %bitcast.73, f32[256,128]{1,0:T(8,128)} %bitcast.75, f32[20,128]{1,0:T(8,128)} %collective-permute-done.refs_3_.refs_4_, ...), custom_call_target="tpu_custom_call" | custom-call | bytes 10800000 | tf_op jit(solution)/shard_map/advect/pallas_call | solution.py:518
  50.8 2.2 %collective-permute-start.7 = (f32[512,128]{1,0:T(8,128)}, f32[512,128]{1,0:T(8,128)}, u32[]{:S(2)}, u32[]{:S(2)}) collective-permute-start(f32[512,128]{1,0:T(8,128)} %get-tuple-element.33), channel_id=1, source_target_pairs={{0,1},{1,2},{2,3},{3,0},{4,5},{5,6},{6,7},{7,4},{8,9},{9,10},{10,1... | collective-permute-start | bytes 786440 | tf_op jit(solution)/shard_map/ppermute | solution.py:678
  53.0 4.2 %collective-permute-start.8 = (f32[512,128]{1,0:T(8,128)}, f32[512,128]{1,0:T(8,128)}, u32[]{:S(2)}, u32[]{:S(2)}) collective-permute-start(f32[512,128]{1,0:T(8,128)} %get-tuple-element.34), channel_id=1, source_target_pairs={{0,2},{1,3},{2,0},{3,1},{4,6},{5,7},{6,4},{7,5},{8,10},{9,11},{10,... | collective-permute-start | bytes 786440 | tf_op jit(solution)/shard_map/ppermute | solution.py:678
  57.2 0.0 collective-permute-start.9
  57.2 2.5 %collective-permute-done.7.refs_8_.refs_1_ = f32[512,128]{1,0:T(8,128)} collective-permute-done((f32[512,128]{1,0:T(8,128)}, f32[512,128]{1,0:T(8,128)}, u32[]{:S(2)}, u32[]{:S(2)}) %collective-permute-start.7) | collective-permute-done | bytes 262176 | tf_op jit(solution)/shard_map/ppermute | solution.py:678
  59.7 10.9 %collective-permute-done.8.refs_9_.refs_2_ = f32[512,128]{1,0:T(8,128)} collective-permute-done((f32[512,128]{1,0:T(8,128)}, f32[512,128]{1,0:T(8,128)}, u32[]{:S(2)}, u32[]{:S(2)}) %collective-permute-start.8) | collective-permute-done | bytes 262176 | tf_op jit(solution)/shard_map/ppermute | solution.py:678
  70.5 0.3 collective-permute-done.9.refs_10_.refs_3_
  70.8 0.0 all-to-all-done
  70.8 9.0 %middle.1 = (f32[128,128]{1,0:T(8,128)}, f32[512,128]{1,0:T(8,128)}, f32[64,128]{1,0:T(8,128)}) custom-call(f32[1088,128]{1,0:T(8,128)} %bitcast.33.refs_0_, f32[264,128]{1,0:T(8,128)} %copy-done, f32[8,128]{1,0:T(8,128)} %collective-permute-done.5.refs_2_, f32[8,128]{1,0:T(8,128)} %collective-permute-done.6.refs_3_, f32[1024,128]{1,0:T(8,128)} %bitcast.64, ...), custom_call_target="tpu_custom_call" | custom-call | bytes 25200000 | tf_op jit(solution)/shard_map/middle/pallas_call | solution.py:518
  79.8 12.1 %all-to-all-start.1 = ((f32[64,1,1024]{2,1,0:T(1,128)}), f32[64,1,1024]{2,1,0:T(1,128)}, u32[]{:S(2)}, u32[]{:S(2)}) async-start(f32[64,1,1024]{2,1,0:T(1,128)} %bitcast.77), calls=%async_computation.1 | async-start | bytes 524288 | tf_op jit(solution)/shard_map/all_to_all | solution.py:664
  91.9 3.1 %solve_sea.1 = (f32[1024,128]{1,0:T(8,128)}, f32[1024,128]{1,0:T(8,128)}) custom-call(f32[512,128]{1,0:T(8,128)} %get-tuple-element.32.refs_0_, f32[512,128]{1,0:T(8,128)} %collective-permute-done.7.refs_8_.refs_1_, f32[512,128]{1,0:T(8,128)} %collective-permute-done.8.refs_9_.refs_2_, f32[512,128]{1,0:T(8,128)} %collective-permute-done.9.refs_10_.refs_3_, ...), custom_call_target="tpu_custom_call" | custom-call | bytes 7200000 | tf_op jit(solution)/shard_map/solve_sea/pallas_call | solution.py:518
  95.0 2.9 %solve_air.1 = f32[1024,128]{1,0:T(8,128)} custom-call(f32[512,128]{1,0:T(8,128)} %get-tuple-element.32.refs_0_, f32[512,128]{1,0:T(8,128)} %collective-permute-done.7.refs_8_.refs_1_, f32[512,128]{1,0:T(8,128)} %collective-permute-done.8.refs_9_.refs_2_, f32[512,128]{1,0:T(8,128)} %collective-permute-done.9.refs_10_.refs_3_, f32[1024,128]{1,0:T(8,128)} %bitcast.65, ...), custom_call_target="tpu_custom_call" | custom-call | bytes 7200000 | tf_op jit(solution)/shard_map/solve_air/pallas_call | solution.py:518
  98.0 7.4 %all-to-all-done.1 = f32[64,1,1024]{2,1,0:T(1,128)} async-done(((f32[64,1,1024]{2,1,0:T(1,128)}), f32[64,1,1024]{2,1,0:T(1,128)}, u32[]{:S(2)}, u32[]{:S(2)}) %all-to-all-start.1) | async-done | bytes 262176 | tf_op jit(solution)/shard_map/all_to_all | solution.py:664
  105.3 3.1 %last.1 = f32[1024,128]{1,0:T(8,128)} custom-call(f32[512,128]{1,0:T(8,128)} %bitcast.43.refs_0_, f32[64,128]{1,0:T(8,128)} %get-tuple-element.39.refs_1_, f32[1024,128]{1,0:T(8,128)} %get-tuple-element.40.refs_2_, f32[1024,128]{1,0:T(8,128)} %get-tuple-element.41.refs_3_), custom_call_target="tpu_custom_call" | custom-call | bytes 7200000 | tf_op jit(solution)/shard_map/last/pallas_call | solution.py:518
Async XLA Ops:
  4.3 14.1 %collective-permute-start.4 = (f32[264,128]{1,0:T(8,128)}, f32[264,128]{1,0:T(8,128)S(1)}, u32[]{:S(2)}, u32[]{:S(2)}) collective-permute-start(f32[264,128]{1,0:T(8,128)} %get-tuple-element.27), channel_id=1, source_target_pairs={{0,3},{4,7},{8,11},{12,15},{16,19},{20,23},{24,27},{28,31},{32,35}... | collective-permute-start | bytes 405512 | tf_op jit(solution)/shard_map/ppermute | solution.py:594
  5.0 13.5 %collective-permute-start.2 = (f32[264,128]{1,0:T(8,128)}, f32[264,128]{1,0:T(8,128)S(1)}, u32[]{:S(2)}, u32[]{:S(2)}) collective-permute-start(f32[264,128]{1,0:T(8,128)} %get-tuple-element.25), channel_id=1, source_target_pairs={{0,1},{4,5},{8,9},{12,13},{16,17},{20,21},{24,25},{28,29},{32,33},... | collective-permute-start | bytes 405512 | tf_op jit(solution)/shard_map/ppermute | solution.py:594
  6.3 12.2 %collective-permute-start.3 = (f32[264,128]{1,0:T(8,128)}, f32[264,128]{1,0:T(8,128)S(1)}, u32[]{:S(2)}, u32[]{:S(2)}) collective-permute-start(f32[264,128]{1,0:T(8,128)} %get-tuple-element.26), channel_id=1, source_target_pairs={{0,2},{4,6},{8,10},{12,14},{16,18},{20,22},{24,26},{28,30},{32,34}... | collective-permute-start | bytes 405512 | tf_op jit(solution)/shard_map/ppermute | solution.py:594
  7.0 23.3 %collective-permute-start = (f32[20,128]{1,0:T(8,128)}, f32[20,128]{1,0:T(8,128)}, u32[]{:S(2)}, u32[]{:S(2)}) collective-permute-start(f32[20,128]{1,0:T(8,128)} %get-tuple-element.22), channel_id=1, source_target_pairs={{0,4},{4,8},{8,12},{12,16},{16,20},{20,24},{24,28},{28,32},{32,36}... | collective-permute-start | bytes 30728 | tf_op jit(solution)/shard_map/ppermute | solution.py:599
  9.5 20.7 %collective-permute-start.1 = (f32[20,128]{1,0:T(8,128)}, f32[20,128]{1,0:T(8,128)}, u32[]{:S(2)}, u32[]{:S(2)}) collective-permute-start(f32[20,128]{1,0:T(8,128)} %get-tuple-element.23), channel_id=1, source_target_pairs={{4,0},{8,4},{12,8},{16,12},{20,16},{24,20},{28,24},{32,28},{36,32}... | collective-permute-start | bytes 30728 | tf_op jit(solution)/shard_map/ppermute | solution.py:600
  18.5 0.6 copy-start
  19.8 18.0 %collective-permute-start.5 = (f32[8,128]{1,0:T(8,128)}, f32[8,128]{1,0:T(8,128)}, u32[]{:S(2)}, u32[]{:S(2)}) collective-permute-start(f32[8,128]{1,0:T(8,128)} %slice.4), channel_id=1, source_target_pairs={{0,4},{4,8},{8,12},{12,16},{16,20},{20,24},{24,28},{28,32},{32,36}... | collective-permute-start | bytes 12296 | tf_op jit(solution)/shard_map/ppermute | solution.py:597
  19.8 18.0 %collective-permute-start.6 = (f32[8,128]{1,0:T(8,128)}, f32[8,128]{1,0:T(8,128)}, u32[]{:S(2)}, u32[]{:S(2)}) collective-permute-start(f32[8,128]{1,0:T(8,128)} %slice.4), channel_id=1, source_target_pairs={{4,0},{8,4},{12,8},{16,12},{20,16},{24,20},{28,24},{32,28},{36,32}... | collective-permute-start | bytes 12296 | tf_op jit(solution)/shard_map/ppermute | solution.py:598
  41.0 29.8 %all-to-all-start = ((f32[64,1,2176]{2,1,0:T(1,128)}), f32[64,1,2176]{2,1,0:T(1,128)}, u32[]{:S(2)}, u32[]{:S(2)}) async-start(f32[64,1,2176]{2,1,0:T(1,128)} %bitcast.62), calls=%async_computation | async-start | bytes 1114112 | tf_op jit(solution)/shard_map/all_to_all | solution.py:664
  50.8 8.9 %collective-permute-start.7 = (f32[512,128]{1,0:T(8,128)}, f32[512,128]{1,0:T(8,128)}, u32[]{:S(2)}, u32[]{:S(2)}) collective-permute-start(f32[512,128]{1,0:T(8,128)} %get-tuple-element.33), channel_id=1, source_target_pairs={{0,1},{1,2},{2,3},{3,0},{4,5},{5,6},{6,7},{7,4},{8,9},{9,10},{10,1... | collective-permute-start | bytes 786440 | tf_op jit(solution)/shard_map/ppermute | solution.py:678
  53.0 17.5 %collective-permute-start.8 = (f32[512,128]{1,0:T(8,128)}, f32[512,128]{1,0:T(8,128)}, u32[]{:S(2)}, u32[]{:S(2)}) collective-permute-start(f32[512,128]{1,0:T(8,128)} %get-tuple-element.34), channel_id=1, source_target_pairs={{0,2},{1,3},{2,0},{3,1},{4,6},{5,7},{6,4},{7,5},{8,10},{9,11},{10,... | collective-permute-start | bytes 786440 | tf_op jit(solution)/shard_map/ppermute | solution.py:678
  57.2 13.6 %collective-permute-start.9 = (f32[512,128]{1,0:T(8,128)}, f32[512,128]{1,0:T(8,128)}, u32[]{:S(2)}, u32[]{:S(2)}) collective-permute-start(f32[512,128]{1,0:T(8,128)} %get-tuple-element.35), channel_id=1, source_target_pairs={{0,3},{1,0},{2,1},{3,2},{4,7},{5,4},{6,5},{7,6},{8,11},{9,8},{10,9... | collective-permute-start | bytes 786440 | tf_op jit(solution)/shard_map/ppermute | solution.py:678
  79.8 25.5 %all-to-all-start.1 = ((f32[64,1,1024]{2,1,0:T(1,128)}), f32[64,1,1024]{2,1,0:T(1,128)}, u32[]{:S(2)}, u32[]{:S(2)}) async-start(f32[64,1,1024]{2,1,0:T(1,128)} %bitcast.77), calls=%async_computation.1 | async-start | bytes 524288 | tf_op jit(solution)/shard_map/all_to_all | solution.py:664
where the time goes:
time: 109 us
  starting transfers between devices  45.3 us (42%)
  Pallas kernels  40.1 us (37%)
  waiting for transfers between devices  21 us (19%)
  local copies, waits for them, and re-layouts  1.23 us (1%)
    pallas_call x9, Pallas kernels, call(): pl.pallas_call(body, out_shape=shapes, in_specs=[{'v': VMEM, 's': SMEM, '...  40.1 us
    all_to_all x2, starting transfers between devices, over_tiles(): y = lax.all_to_all(y, 'tiles', split_axis=0, concat_axis=0, tiled=True)  17.6 us
    ppermute x3, waiting for transfers between devices, on_device(): lax.ppermute(rest[d], 'lev', [(i, (i + d) % levs) for i in range(levs)])  13.6 us
    ppermute x1, starting transfers between devices, on_device(): rest_right = lax.ppermute(rest_first, 'tiles', backward)  8.94 us
    all_to_all x2, waiting for transfers between devices, over_tiles(): y = lax.all_to_all(y, 'tiles', split_axis=0, concat_axis=0, tiled=True)  7.39 us
    ppermute x1, starting transfers between devices, on_device(): right = lax.ppermute(ends, 'tiles', backward)  7.19 us
    ppermute x3, starting transfers between devices, on_device(): lax.ppermute(rest[d], 'lev', [(i, (i + d) % levs) for i in range(levs)])  6.36 us
    ppermute x3, starting transfers between devices, on_device(): moved = [lax.ppermute(parts[d], 'lev', [(0, d)]) for d in range(1, levs)]  2.63 us
  transfers between devices with their start and end apart: 12, of which 4 were waited for; matrix products, arithmetic and copies ran while one was open for 1% of the time, Pallas kernels for 19%

commit v1 on v0

--- a/solution.py
+++ b/solution.py
@@ -10,6 +10,8 @@
 BLOCK = 64
 LANES = 128
 SLOTS = 16
+PIECES = 4
+AHEAD = 2
 F32 = jnp.float32
 BF16 = jnp.bfloat16
 NT = (((1,), (1,)), ((), ()))
@@ -56,7 +58,7 @@
     return jnp.where(condition, 1.0, 0.0).astype(BF16)
 
 
-def prepare_kernel(tiles, ut, ub, dt, db, mask, up_out, down_out, label_out, mask_out, order_out):
+def prepare_kernel(tiles, ut, ub, dt, db, mask, up_out, down_out, label_out, mask_out):
     blocks = ut.shape[1]
     groups = blocks // 2
     entries = 2 * blocks
@@ -85,11 +87,9 @@
         rank = jnp.sum(named * dot(named.astype(BF16), earlier), 0, keepdims=True)
         rank = rank.astype(jnp.int32)
         target = target.astype(jnp.int32)
-        rows = tiles * SLOTS // 2
         at = (rank // 2) * tiles + target
         for half in range(2):
-            wanted = jnp.where((rank & 1) == half, at, -1)
-            out[half] = onehot(iota((rows, entries), 0) == wanted)
+            out[half : half + 1, :] = jnp.where((rank & 1) == half, at, -1)
         carried = (named * (block + 1.0)).astype(BF16)
         chosen = onehot(iota((LANES, entries), 0) == rank + base)
         term = dot(carried, chosen, NT)
@@ -104,114 +104,103 @@
         term = dot(picked, side)
         spread = term if spread is None else spread + term
     mask_out[...] = spread
-    row, column = iota((256, 512), 0), iota((256, 512), 1)
-    same = ((row >> 6) & 1) * 2 + (row & 1) == (column >> 7)
-    cell = ((row >> 1) & 31) * 2 + (row >> 7)
-    order_out[...] = onehot(same & (cell == (column & 63)))
-
-
-def upwind(x, positive, negative, below, above):
-    return x - positive * (x - below) - negative * (above - x)
-
-
-def surface_kernel(sea, air, sea_c, air_c, o0, o1, o2, o3, first_out, last_out, sbuf, abuf, sems):
+
+
+def edge_kernel(sea, air, sea_c, air_c, place, pair_out, next_out, first, last, sems):
+    fields = 4
+    copies = []
+    for n, (state, courant) in enumerate(((sea, sea_c), (air, air_c))):
+        size = courant.shape[0]
+        for at in range(fields + 1):
+            source, base = (state, at * size) if at < fields else (courant, 0)
+            for side, (buf, start) in enumerate(((first, 0), (last, size - 8))):
+                copies.append(
+                    pltpu.make_async_copy(
+                        source.at[pl.ds(base + start, 8)], buf.at[n, at], sems.at[n, at, side]
+                    )
+                )
+    for copy in copies:
+        copy.start()
+    for copy in copies:
+        copy.wait()
+    for n in range(2):
+        for at in range(fields + 1):
+            row = n * 2 * (fields + 1) + 2 * at
+            low, high = first[n, at, 0:2, :], last[n, at, 6:8, :]
+            pair_out[row : row + 2, :] = jnp.where(place[0] // 4 == 0, high, low)
+            next_out[row : row + 2, :] = jnp.where(place[0] // 4 == 0, low, high)
+
+
+def neighbours(pair, other, place):
+    pair, other = pair.get()[...], other.get()[...]
+    even = place[0] // 4 == 0
+    return jnp.where(even, other, pair), jnp.where(even, pair, other)
+
+
+def stepped(x, low, high, positive, negative, buf):
+    rows = x.shape[0]
+    total = buf.shape[0]
+    lane = iota((total, LANES), 1)
+    first = lane == 0
+    last = lane == LANES - 1
+    buf[0:8, :] = jnp.broadcast_to(low, (8, LANES))
+    buf[8 : rows + 8, :] = x
+    buf[rows + 8 :, :] = jnp.broadcast_to(high, (8, LANES))
+    x = buf[...]
+    for step in range(2):
+        below = pltpu.roll(x, 1, 1)
+        below = jnp.where(first, pltpu.roll(below, 1, 0), below)
+        above = pltpu.roll(x, LANES - 1, 1)
+        above = jnp.where(last, pltpu.roll(above, total - 1, 0), above)
+        x = x - positive * (x - below) - negative * (above - x)
+    return x[8 : rows + 8, :]
+
+
+def speeds(c, low, high, buf):
+    rows = c.shape[0]
+    buf[0:8, :] = jnp.broadcast_to(low, (8, LANES))
+    buf[8 : rows + 8, :] = c
+    buf[rows + 8 :, :] = jnp.broadcast_to(high, (8, LANES))
+    c = buf[...]
+    return jnp.maximum(c, 0.0), jnp.minimum(c, 0.0)
+
+
+def surface_kernel(sea, sea_c, pair, other, place, o0, o1, o2, o3, sbuf, xbuf, cbuf, sems):
     rows = sea_c.shape[0] // 2
     size = 2 * rows
     outs = (o0, o1, o2, o3)
     order = (1, 2, 3, 0)
 
-    def copy(n, d):
-        state, buf = ((sea, sbuf), (air, abuf))[n]
-        return pltpu.make_async_copy(state.at[pl.ds(d * size, size)], buf.at[d], sems.at[n, d])
+    def copy(d):
+        return pltpu.make_async_copy(sea.at[pl.ds(d * size, size)], sbuf.at[d], sems.at[d])
 
     for d in order:
-        for n in range(2):
-            copy(n, d).start()
-    lane = iota((rows, LANES), 1)
-    first = lane == 0
-    last = lane == LANES - 1
-    signs = []
-    for n, speed in enumerate((sea_c, air_c)):
-        c = speed.get()[pl.ds(0, rows, stride=2), :]
-        signs.append((jnp.maximum(c, 0.0), jnp.minimum(c, 0.0)))
+        copy(d).start()
+    left, right = neighbours(pair, other, place)
+    c = sea_c.get()[pl.ds(0, rows, stride=2), :]
+    positive, negative = speeds(c, left[8:9, :], right[8:9, :], cbuf)
     for d in order:
-        out = outs[d]
-        for n, (buf, speed) in enumerate(((sbuf, sea_c), (abuf, air_c))):
-            copy(n, d).wait()
-            positive, negative = signs[n]
-            x = buf[d, pl.ds(0, rows, stride=2), :]
-            for step in range(2):
-                below = pltpu.roll(x, 1, 1)
-                below = jnp.where(first, pltpu.roll(below, 1, 0), below)
-                above = pltpu.roll(x, LANES - 1, 1)
-                above = jnp.where(last, pltpu.roll(above, rows - 1, 0), above)
-                x = upwind(x, positive, negative, below, above)
-            out[n * rows : (n + 1) * rows, :] = x
-            at = 2 * rows + n
-            out[at : at + 1, :] = buf[d, 0:1, :]
-            out[at + 2 : at + 3, :] = speed.get()[0:1, :]
-            out[at + 4 : at + 5, :] = buf[d, size - 2 : size - 1, :]
-            out[at + 6 : at + 7, :] = speed.get()[size - 2 : size - 1, :]
-            at = n * 10 + 2 * d
-            first_out[at : at + 2, :] = buf[d, 0:2, :]
-            last_out[at : at + 2, :] = buf[d, size - 2 : size, :]
-    for n, speed in enumerate((sea_c, air_c)):
-        at = n * 10 + 8
-        first_out[at : at + 2, :] = speed.get()[0:2, :]
-        last_out[at : at + 2, :] = speed.get()[size - 2 : size, :]
+        copy(d).wait()
+        x = sbuf[d, pl.ds(0, rows, stride=2), :]
+        low, high = left[2 * d : 2 * d + 1, :], right[2 * d : 2 * d + 1, :]
+        outs[d][...] = stepped(x, low, high, positive, negative, xbuf)
 
 
 def advect_kernel(
-    fields, sea, air, sea_c, air_c, left, right, lev, o0, o1, o2, o3, xbuf, cbuf
+    fields, base, state, courant, pair, other, lev, o0, o1, o2, o3, lows, highs, xbuf, cbuf
 ):
-    rows = sea_c.shape[0] // 2
-    total = rows + 16
-    lane = iota((total, LANES), 1)
-    first = lane == 0
-    last = lane == LANES - 1
-
-    def extended(buf, middle, at):
-        buf[0:8, :] = jnp.broadcast_to(left.get()[pl.ds(at, 1), :], (8, LANES))
-        buf[8 : rows + 8, :] = middle
-        buf[rows + 8 :, :] = jnp.broadcast_to(right.get()[pl.ds(at, 1), :], (8, LANES))
-        return buf[...]
-
-    for n, (state, courant) in enumerate(((sea, sea_c), (air, air_c))):
-        for level in range(2):
-            c = courant.get()[pl.ds(level, rows, stride=2), :]
-            c = extended(cbuf, c, n * 10 + 8 + level)
-            positive, negative = jnp.maximum(c, 0.0), jnp.minimum(c, 0.0)
-            for d, out in enumerate((o0, o1, o2, o3)):
-                field = lax.rem(lev[0] + d, fields)
-                at = field * 2 * rows + level
-                x = state.get()[pl.ds(at, rows, stride=2), :]
-                x = extended(xbuf, x, n * 10 + 2 * field + level)
-                for step in range(2):
-                    below = pltpu.roll(x, 1, 1)
-                    below = jnp.where(first, pltpu.roll(below, 1, 0), below)
-                    above = pltpu.roll(x, LANES - 1, 1)
-                    above = jnp.where(last, pltpu.roll(above, total - 1, 0), above)
-                    x = upwind(x, positive, negative, below, above)
-                at = (2 * n + level) * rows
-                out[at : at + rows, :] = x[8 : rows + 8, :]
-
-
-def mended(ends, left, right):
-    low = low_half((2, LANES))
-    out = []
-    for at, outer, kept in ((0, left, low), (4, right, jnp.logical_not(low))):
-        x = jnp.where(kept, ends[at : at + 2, :], outer[4 - at : 6 - at, :])
-        c = jnp.where(kept, ends[at + 2 : at + 4, :], outer[6 - at : 8 - at, :])
-        positive, negative = jnp.maximum(c, 0.0), jnp.minimum(c, 0.0)
-        for step in range(2):
-            x = upwind(x, positive, negative, pltpu.roll(x, 1, 1), pltpu.roll(x, LANES - 1, 1))
-        out.append(x)
-    return out
-
-
-def mend(row, mended_row, at_end):
-    lane = iota(row.shape, 1)
-    return jnp.where(lane >= LANES - 2 if at_end else lane < 2, mended_row, row)
+    rows = courant.shape[0] // 2
+    lows[...], highs[...] = neighbours(pair, other, lev)
+    for level in range(2):
+        c = courant.get()[pl.ds(level, rows, stride=2), :]
+        at = base + 8 + level
+        positive, negative = speeds(c, lows[at : at + 1, :], highs[at : at + 1, :], cbuf)
+        for d, out in enumerate((o0, o1, o2, o3)):
+            field = lax.rem(lev[0] + d, fields)
+            x = state.get()[pl.ds(field * 2 * rows + level, rows, stride=2), :]
+            at = pl.ds(base + 2 * field + level, 1)
+            x = stepped(x, lows[at, :], highs[at, :], positive, negative, xbuf)
+            out[level * rows : (level + 1) * rows, :] = x
 
 
 def weight_copies(weight, wbuf, sems):
@@ -261,20 +250,30 @@
 
     product_rows(values, ones, put)
 
-    def body(g, carry):
-        at = pl.ds(pl.multiple_of(g * count, count), count)
-        w = wbuf[pl.ds(pl.multiple_of(g * LANES, LANES), LANES), :]
-        res[at, :] = dot(lhs[at, :].astype(BF16), w, NT)
+    def body(step, carry):
+        w = wbuf[pl.ds(pl.multiple_of(step * 2 * LANES, 2 * LANES), 2 * LANES), :]
+        both = pl.ds(pl.multiple_of(step * 2 * count, 2 * count), 2 * count)
+        out = dot(lhs[both, :].astype(BF16), w, NT)
+        for n in range(2):
+            at = pl.ds(pl.multiple_of((2 * step + n) * count, count), count)
+            res[at, :] = out[n * count : (n + 1) * count, n * LANES : (n + 1) * LANES]
         return carry
 
-    each = groups // len(copies)
+    each = groups // 2 // len(copies)
     for n, copy in enumerate(copies):
         copy.wait()
-        lax.fori_loop(n * each, (n + 1) * each, body, 0, unroll=8)
+        if n + AHEAD < len(copies):
+            copies[n + AHEAD].start()
+        lax.fori_loop(n * each, (n + 1) * each, body, 0, unroll=each)
     return product_sums(lambda row: res[pl.ds(row, groups, stride=count), :], ones is not None)
 
 
-def entry_values(sums, order):
+def entry_values(sums):
+    row, column = iota((256, 512), 0), iota((256, 512), 1)
+    same = ((row >> 6) & 1) * 2 + (row & 1) == (column >> 7)
+    cell = ((row >> 1) & 31) * 2 + (row >> 7)
+    order = onehot(same & (cell == (column & 63)))
+
     def ordered(pair):
         high, low = split(jnp.concatenate(pair, 1))
         return dot(high, order), dot(low, order)
@@ -292,54 +291,40 @@
 
 
 def dispatched(place, entries):
+    count = entries.shape[0]
     out = []
     for half in range(2):
-        slots = dot(place[half], entries)
+        chosen = onehot(iota((count, count), 0) == place[half : half + 1, :])
+        slots = dot(chosen, entries)
         out.append(slots[:, :LANES] + slots[:, LANES:])
     return out
 
 
-def up_kernel(surface, mask, weight, sums_out, wbuf, lhs, res, wsems):
-    groups = mask.shape[0]
+def surface_copy(parts, at, lev, buf, sem):
+    copies = [
+        pltpu.make_async_copy(part.at[pl.ds(at, buf.shape[0])], buf, sem) for part in parts
+    ]
+    for d, copy in enumerate(copies):
+
+        @pl.when(lev[0] % 4 == d)
+        def start(copy=copy):
+            copy.start()
+
+    return copies[0]
+
+
+def up_kernel(
+    p0, p1, p2, p3, mask, place, labels, weight, lev, out, values, wbuf, lhs, res, sem, wsems
+):
+    tiles = labels.shape[0]
+    field = surface_copy((p0, p1, p2, p3), 0, lev, values, sem)
     copies = weight_copies(weight, wbuf, wsems)
-    for copy in copies:
+    for copy in copies[:AHEAD]:
         copy.start()
+    field.wait()
     mask_value = mask.get()[...]
-    values = surface.get()[0:groups, :] * mask_value
-    sums = products(values, mask_value, copies, wbuf, lhs, res)
-    sums_out[...] = jnp.concatenate(sums, 1)
-
-
-def slot_kernel(
-    sums, surface, left, right, mask, weight, place, order, labels, out, wbuf, lhs, sems
-):
-    groups = mask.shape[0]
-    tiles = labels.shape[0]
-    copies = [
-        pltpu.make_async_copy(weight.at[pl.ds(at, LANES)], wbuf.at[n], sems.at[n])
-        for n, at in enumerate((0, (groups - 1) * LANES))
-    ]
-    for copy in copies:
-        copy.start()
-    surface, mask, sums = surface.get(), mask.get(), sums.get()
-    mended_rows = mended(
-        surface[2 * groups : 2 * groups + 8, :], left.get()[...], right.get()[...]
-    )
-    row_at = iota((groups, LANES), 0)
-    parts = [sums[:, n * LANES : (n + 1) * LANES] for n in range(4)]
-    for n, g in enumerate((0, groups - 1)):
-        row = surface[g : g + 1, :]
-        row = mend(row, mended_rows[n][0:1], n == 1) * mask[g : g + 1, :]
-
-        def put(at, x):
-            lhs[at : at + 1, :] = x
-
-        product_rows(row, None, put)
-        copies[n].wait()
-        res = dot(lhs[...].astype(BF16), wbuf[n], NT)
-        for p, new in enumerate(product_sums(lambda at: res[at : at + 1], False)):
-            parts[p] = jnp.where(row_at == g, new, parts[p])
-    even, odd = dispatched(place.get(), entry_values(parts, order.get()[...]))
+    sums = products(values[...] * mask_value, mask_value, copies, wbuf, lhs, res)
+    even, odd = dispatched(place.get(), entry_values(sums))
     half = low_half((tiles, LANES))
     pitch = out.shape[0] // tiles
     for i in range(SLOTS // 2):
@@ -387,31 +372,28 @@
 
 
 def middle_kernel(
-    arrived, surface, left, right, mixing, weight, place, order,
-    flux_out, out, label_out, wbuf, lhs, res, wsems,
+    arrived, p0, p1, p2, p3, mixing, place, weight, lev,
+    flux_out, out, label_out, values, wbuf, lhs, res, sem, wsems,
 ):
     groups = flux_out.shape[0]
     tiles = label_out.shape[0]
+    surface = surface_copy((p0, p1, p2, p3), 0, lev, values, sem)
     copies = weight_copies(weight, wbuf, wsems)
-    for copy in copies:
+    for copy in copies[:AHEAD]:
         copy.start()
+    arrived = arrived.get()
     labels = arrived[pl.ds(SLOTS, tiles, stride=SLOTS + 1), :]
     label_out[...] = labels
     names = named_blocks(labels, 0, groups)
     field = slot_rows(arrived, 0, SLOTS // 2, tiles)
     cover = slot_rows(arrived, SLOTS // 2, SLOTS // 2, tiles)
     received, coverage = collected((field, cover), names)
-    surface = surface.get()
-    mended_rows = mended(
-        surface[2 * groups : 2 * groups + 8, :], left.get()[...], right.get()[...]
-    )
-    for n, at in enumerate((groups, 2 * groups - 1)):
-        surface[at : at + 1, :] = mend(surface[at : at + 1, :], mended_rows[n][1:2], n == 1)
+    surface.wait()
     factor = mixing.get()[pl.ds(0, groups, stride=8), :]
-    flux = factor * (coverage * surface[groups : 2 * groups, :] - received)
+    flux = factor * (coverage * values[...] - received)
     flux_out[...] = flux
     sums = products(flux, None, copies, wbuf, lhs, res)
-    even, odd = dispatched(place.get(), entry_values(sums, order.get()[...]))
+    even, odd = dispatched(place.get(), entry_values(sums))
     half = low_half((tiles, LANES))
     pitch = out.shape[0] // tiles
     for i in range(SLOTS // 2):
@@ -427,13 +409,12 @@
     groups = extra.shape[0]
     chunk = 16
     levels = 8
-    base = 2 * groups if with_flux else 0
     copies = []
     for d, part in enumerate((p0, p1, p2, p3)):
         source = lax.rem(lev[0] + 4 - d, 4)
         copies.append(
             pltpu.make_async_copy(
-                part.at[pl.ds(base, 2 * groups)], buf.at[source], sems.at[d]
+                part.at[pl.ds(0, 2 * groups)], buf.at[source], sems.at[d]
             )
         )
     for copy in copies:
@@ -481,6 +462,7 @@
 
 def last_kernel(arrived, labels, base, unit, out, gain):
     tiles = labels.shape[0]
+    arrived = arrived.get()
     groups = gain.shape[0]
     names = named_blocks(labels.get()[...], SLOTS, groups)
     (total,) = collected((slot_rows(arrived, 0, SLOTS // 2, tiles),), names)
@@ -567,9 +549,8 @@
     rows = cells // LANES
     groups = sea_mask.shape[0] // 2
     lev = lax.axis_index("lev").astype(jnp.int32)
-    lev_ref = lev.reshape(1)
-    forward = [(i, (i + 1) % tiles) for i in range(tiles)]
-    backward = [(b, a) for a, b in forward]
+    tile = lax.axis_index("tiles").astype(jnp.int32)
+    lev_ref = (lev + levs * (tile % 2)).reshape(1)
     states = (
         tile_rows(sea_state, fields),
         tile_rows(air_state, fields),
@@ -578,37 +559,52 @@
     )
     size = pair * rows
 
-    *parts, rest_first, rest_last = call(
+    to_pair, to_other = call(
+        edge_kernel,
+        (shape(20, LANES),) * 2,
+        (*states, lev_ref),
+        "hhhhs",
+        scratch=[
+            pltpu.VMEM((2, fields + 1, 8, LANES), F32),
+            pltpu.VMEM((2, fields + 1, 8, LANES), F32),
+            DMA((2, fields + 1, 2)),
+        ],
+        name="edges",
+        us=1.5,
+    )
+    pairs = [(i, i + 1 - 2 * (i % 2)) for i in range(tiles)]
+    others = [(i, (i - 1 + 2 * (i % 2)) % tiles) for i in range(tiles)]
+    ends = (
+        lax.ppermute(to_pair, "tiles", pairs),
+        lax.ppermute(to_other, "tiles", others),
+    )
+    extended = pltpu.VMEM((rows + 16, LANES), F32)
+
+    def around(parts):
+        return [parts[0]] + [
+            lax.ppermute(parts[d], "lev", [(i, (i + d) % levs) for i in range(levs)])
+            for d in range(1, levs)
+        ]
+
+    surface = call(
         surface_kernel,
-        tuple(shape(size + 8, LANES) for _ in range(4)) + (shape(20, LANES),) * 2,
-        states,
-        "hhff",
-        scratch=[
-            pltpu.VMEM((4, size, LANES), F32),
-            pltpu.VMEM((4, size, LANES), F32),
-            DMA((2, 4)),
-        ],
+        (shape(rows, LANES),) * 4,
+        (states[0], states[2], *ends, lev_ref),
+        "hfffs",
+        scratch=[pltpu.VMEM((4, size, LANES), F32), extended, extended, DMA((4,))],
         name="surface",
-        us=3.0,
-    )
-    moved = [lax.ppermute(parts[d], "lev", [(0, d)]) for d in range(1, levs)]
-    surface = jnp.where(lev == 0, parts[0], moved[0] + moved[1] + moved[2])
-    ends = surface[size:]
-    left = lax.ppermute(ends, "tiles", forward)
-    right = lax.ppermute(ends, "tiles", backward)
-    rest_left = lax.ppermute(rest_last, "tiles", forward)
-    rest_right = lax.ppermute(rest_first, "tiles", backward)
-
-    places = tiles * SLOTS // 2
+        us=2.5,
+    )
+    surface_parts = around(surface)
+
     entries = 4 * groups
-    place_up, place_down, labels, mask, order = call(
+    place_up, place_down, labels, mask = call(
         functools.partial(prepare_kernel, tiles),
         (
-            shape(2, places, entries, dtype=BF16),
-            shape(2, places, entries, dtype=BF16),
+            shape(2, entries, dtype=jnp.int32),
+            shape(2, entries, dtype=jnp.int32),
             shape(tiles, LANES),
             shape(groups, LANES),
-            shape(256, 512, dtype=BF16),
         ),
         (
             upward_target.T,
@@ -619,8 +615,8 @@
         ),
         "fffff",
         name="prepare",
-        us=3.0,
-        after=(parts[0],),
+        us=2.5,
+        after=(surface[0],),
     )
     air_k = tile_rows(air_mixing, 1)
     sea_k = tile_rows(sea_mixing, 1)
@@ -634,83 +630,72 @@
             pltpu.VMEM((groups * count, LANES), F32),
         ]
 
-    sums = call(
-        up_kernel,
-        shape(groups, 4 * LANES),
-        (surface, mask, up_rows),
-        "ffh",
-        scratch=[*workspace(16), DMA((8,))],
-        name="upward",
-        us=5.0,
-        after=(rest_left, rest_right),
-    )
     pitch = SLOTS + 1
     outgoing = call(
-        slot_kernel,
+        up_kernel,
         shape(tiles * pitch, LANES),
-        (sums, surface, left, right, mask, up_rows, place_up, order, labels),
-        "fffffhfff",
-        scratch=[
-            pltpu.VMEM((2, LANES, LANES), BF16),
-            pltpu.VMEM((8, LANES), F32),
-            DMA((2,)),
-        ],
-        name="to_slots",
-        us=2.0,
+        (*surface_parts, mask, place_up, labels, up_rows, lev_ref),
+        "hhhhfffhs",
+        scratch=[pltpu.VMEM((rows, LANES), F32), *workspace(16), DMA(()), DMA((PIECES,))],
+        name="upward",
+        us=8.0,
     )
 
     def over_tiles(x):
-        y = x.reshape(tiles, 1, x.size // tiles)
+        pitch = x.shape[0] // tiles
+        y = x.reshape((tiles, pitch, LANES) if pitch % 8 == 0 else (tiles, 1, pitch * LANES))
         y = lax.all_to_all(y, "tiles", split_axis=0, concat_axis=0, tiled=True)
         return y.reshape(x.shape)
 
-    rest = call(
-        functools.partial(advect_kernel, fields),
-        tuple(shape(2 * size, LANES) for _ in range(4)),
-        (*states, rest_left, rest_right, lev_ref),
-        "ffffffs",
-        scratch=[pltpu.VMEM((rows + 16, LANES), F32)] * 2,
-        name="advect",
-        us=3.0,
-        after=(outgoing,),
-    )
-    rest = [rest[0]] + [
-        lax.ppermute(rest[d], "lev", [(i, (i + d) % levs) for i in range(levs)])
-        for d in range(1, levs)
-    ]
+    def advected(state, courant, base, name):
+        return call(
+            functools.partial(advect_kernel, fields, base),
+            tuple(shape(size, LANES) for _ in range(4)),
+            (state, courant, *ends, lev_ref),
+            "ffffs",
+            scratch=[pltpu.VMEM((20, LANES), F32)] * 2 + [extended, extended],
+            name=name,
+            us=2.5,
+            after=(outgoing,),
+        )
+
+    air = around(advected(states[1], states[3], 10, "advect_air"))
+    sea_own = advected(states[0], states[2], 0, "advect_sea")
     arrived = over_tiles(outgoing)
     flux, returning, labels_down = call(
         middle_kernel,
         (shape(groups, LANES), shape(tiles * SLOTS // 2, LANES), shape(tiles, LANES)),
-        (arrived, surface, left, right, air_k, down_rows, place_down, order),
-        "vffffhff",
-        scratch=[*workspace(8), DMA((8,))],
+        (arrived, *air, air_k, place_down, down_rows, lev_ref),
+        "fhhhhffhs",
+        scratch=[pltpu.VMEM((rows, LANES), F32), *workspace(8), DMA(()), DMA((PIECES,))],
         name="middle",
-        us=7.0,
-        after=tuple(rest[1:]),
+        us=8.0,
+        after=(sea_own[0],),
     )
     gained = over_tiles(returning)
+    sea = around(sea_own)
 
     column = shape(8 * rows, LANES)
 
-    def solve(with_flux, k, extra, name):
+    def solve(with_flux, parts, k, extra, name, after=()):
         return call(
             functools.partial(solve_kernel, with_flux),
             column if with_flux else (column, column),
-            (*rest, k, extra, lev_ref),
+            (*parts, k, extra, lev_ref),
             "hhhhffs",
             scratch=[pltpu.VMEM((4, size, LANES), F32), DMA((4,))],
             name=name,
-            us=2.0,
+            us=3.0,
+            after=after,
         )
 
-    base, unit = solve(False, sea_k, mask, "solve_sea")
-    air_out = solve(True, air_k, flux, "solve_air")
+    air_out = solve(True, air, air_k, flux, "solve_air")
+    base, unit = solve(False, sea, sea_k, mask, "solve_sea", (air_out,))
     sea_out = call(
         last_kernel,
         column,
         (gained, labels_down, base, unit),
-        "vfff",
+        "ffff",
         scratch=[pltpu.VMEM((rows, LANES), F32)],
         name="last",
         us=2.0,

time: 109 us -> 92 us (0.84)
  starting transfers between devices: 45.3 us -> 36.4 us
  Pallas kernels: 40.1 us -> 31.9 us
  local copies, waits for them, and re-layouts: 1.23 us -> 0 us
  waiting for transfers between devices: 21 us -> 22.2 us
    ppermute x10 -> x11, starting transfers between devices: 27.7 us -> 18 us  [the longest x1 9.58 us: on_device(): lax.ppermute(to_other, 'tiles', others)]
    pallas_call x9 -> x10, Pallas kernels: 40.1 us -> 31.9 us  [call(): pl.pallas_call(body, out_shape=shapes, in_specs=[{'v': VMEM, 's': SMEM, '...]
    ppermute x10 -> x11, waiting for transfers between devices: 13.7 us -> 18.3 us  [the longest x9 16.9 us: around(): lax.ppermute(parts[d], 'lev', [(i, (i + d) % levs) for i in range(levs)])]
    all_to_all x2, waiting for transfers between devices: 7.39 us -> 3.88 us  [over_tiles(): y = lax.all_to_all(y, 'tiles', split_axis=0, concat_axis=0, tiled=True)]
  transfers between devices with their start and end apart: 12 -> 13, of which waited for: 4 -> 10; matrix products, arithmetic and copies ran while one was open for 1% -> 0% of each run, Pallas kernels for 19% -> 15%
where the time goes in v1:
time: 92 us; the launch traced here: 91.4 us
  starting transfers between devices  36.4 us (40%)
  Pallas kernels  31.9 us (35%)
  waiting for transfers between devices  22.2 us (24%)
  between operations  0.92 us (1%)
    pallas_call x10, Pallas kernels, call(): pl.pallas_call(body, out_shape=shapes, in_specs=[{'v': VMEM, 's': SMEM, '...  31.9 us
    all_to_all x2, starting transfers between devices, over_tiles(): y = lax.all_to_all(y, 'tiles', split_axis=0, concat_axis=0, tiled=True)  18.4 us
    ppermute x9, waiting for transfers between devices, around(): lax.ppermute(parts[d], 'lev', [(i, (i + d) % levs) for i in range(levs)])  16.9 us
    ppermute x1, starting transfers between devices, on_device(): lax.ppermute(to_other, 'tiles', others)  9.58 us
    ppermute x9, starting transfers between devices, around(): lax.ppermute(parts[d], 'lev', [(i, (i + d) % levs) for i in range(levs)])  5.91 us
    all_to_all x2, waiting for transfers between devices, over_tiles(): y = lax.all_to_all(y, 'tiles', split_axis=0, concat_axis=0, tiled=True)  3.88 us
    ppermute x1, starting transfers between devices, on_device(): lax.ppermute(to_pair, 'tiles', pairs)  2.55 us
  transfers between devices with their start and end apart: 13, of which 10 were waited for; matrix products, arithmetic and copies ran while one was open for 0% of the time, Pallas kernels for 15%

profile of v1, /device:TPU:1, one launch (start us, length us, event | category | flops | bytes accessed | tf_op | source)
XLA Modules:
  0.0 91.4 jit_solution(837424889462332071)
XLA Ops:
  0.6 1.7 %edges.1 = (f32[20,128]{1,0:T(8,128)}, f32[20,128]{1,0:T(8,128)}) custom-call(f32[1024,128]{1,0:T(8,128)} %bitcast.61, f32[1024,128]{1,0:T(8,128)} %bitcast.66, f32[256,128]{1,0:T(8,128)} %bitcast.71, f32[256,128]{1,0:T(8,128)} %bitcast.75, s32[1]{0:T(128)} %bitcast.16.refs_4_.refs_8_.refs_6_), custom_call_target="tpu_custom_call" | custom-call | bytes 5400000 | tf_op jit(solution)/shard_map/edges/pallas_call | solution.py:500
  2.3 2.6 %collective-permute-start = (f32[20,128]{1,0:T(8,128)}, f32[20,128]{1,0:T(8,128)}, u32[]{:S(2)}, u32[]{:S(2)}) collective-permute-start(f32[20,128]{1,0:T(8,128)} %get-tuple-element.25), channel_id=1, source_target_pairs={{0,4},{4,0},{8,12},{12,8},{16,20},{20,16},{24,28},{28,24},{32,36},... | collective-permute-start | bytes 30728 | tf_op jit(solution)/shard_map/ppermute | solution.py:578
  4.9 9.6 %collective-permute-start.1 = (f32[20,128]{1,0:T(8,128)}, f32[20,128]{1,0:T(8,128)}, u32[]{:S(2)}, u32[]{:S(2)}) collective-permute-start(f32[20,128]{1,0:T(8,128)} %get-tuple-element.26), channel_id=1, source_target_pairs={{0,252},{4,8},{8,4},{12,16},{16,12},{20,24},{24,20},{28,32},{32,28... | collective-permute-start | bytes 30728 | tf_op jit(solution)/shard_map/ppermute | solution.py:579
  14.4 0.0 collective-permute-done.refs_2_
  14.4 1.4 %collective-permute-done.1.refs_3_ = f32[20,128]{1,0:T(8,128)} collective-permute-done((f32[20,128]{1,0:T(8,128)}, f32[20,128]{1,0:T(8,128)}, u32[]{:S(2)}, u32[]{:S(2)}) %collective-permute-start.1) | collective-permute-done | bytes 10272 | tf_op jit(solution)/shard_map/ppermute | solution.py:579
  15.8 2.6 %surface.1 = (f32[128,128]{1,0:T(8,128)}, f32[128,128]{1,0:T(8,128)}, f32[128,128]{1,0:T(8,128)}, f32[128,128]{1,0:T(8,128)}) custom-call(f32[1024,128]{1,0:T(8,128)} %bitcast.62, f32[256,128]{1,0:T(8,128)} %bitcast.72, f32[20,128]{1,0:T(8,128)} %collective-permute-done.refs_2_, f32[20,128]{1,0:T(8,128)} %collective-permute-done.1.refs_3_, ...), custom_call_target="tpu_custom_call" | custom-call | bytes 9000000 | tf_op jit(solution)/shard_map/surface/pallas_call | solution.py:500
  18.5 2.1 %collective-permute-start.2 = (f32[128,128]{1,0:T(8,128)}, f32[128,128]{1,0:T(8,128)}, u32[]{:S(2)}, u32[]{:S(2)}) collective-permute-start(f32[128,128]{1,0:T(8,128)} %get-tuple-element.28), channel_id=1, source_target_pairs={{0,1},{1,2},{2,3},{3,0},{4,5},{5,6},{6,7},{7,4},{8,9},{9,10},{10,1... | collective-permute-start | bytes 196616 | tf_op jit(solution)/shard_map/ppermute | solution.py:585
  20.6 1.2 %collective-permute-start.3 = (f32[128,128]{1,0:T(8,128)}, f32[128,128]{1,0:T(8,128)}, u32[]{:S(2)}, u32[]{:S(2)}) collective-permute-start(f32[128,128]{1,0:T(8,128)} %get-tuple-element.29), channel_id=1, source_target_pairs={{0,2},{1,3},{2,0},{3,1},{4,6},{5,7},{6,4},{7,5},{8,10},{9,11},{10,... | collective-permute-start | bytes 196616 | tf_op jit(solution)/shard_map/ppermute | solution.py:585
  21.7 0.0 collective-permute-start.4
  21.7 2.1 %prepare.1 = (s32[2,512]{1,0:T(2,128)}, s32[2,512]{1,0:T(2,128)}, f32[64,128]{1,0:T(8,128)}, f32[128,128]{1,0:T(8,128)}) custom-call(s32[2,256]{1,0:T(2,128)} %bitcast.79, s32[2,256]{1,0:T(2,128)} %bitcast.80, s32[2,256]{1,0:T(2,128)} %bitcast.81, s32[2,256]{1,0:T(2,128)} %bitcast.82, s32[1,256]{1,0:T(1,128)} %bitcast.83, ...), custom_call_target="tpu_custom_call" | custom-call | bytes 9000000 | tf_op jit(solution)/shard_map/prepare/pallas_call | solution.py:500
  23.8 0.0 collective-permute-done.2.refs_1_
  23.8 1.5 %collective-permute-done.3.refs_2_ = f32[128,128]{1,0:T(8,128)} collective-permute-done((f32[128,128]{1,0:T(8,128)}, f32[128,128]{1,0:T(8,128)}, u32[]{:S(2)}, u32[]{:S(2)}) %collective-permute-start.3) | collective-permute-done | bytes 65568 | tf_op jit(solution)/shard_map/ppermute | solution.py:585
  25.3 0.5 collective-permute-done.4.refs_3_
  25.8 5.8 %upward.1.refs_5_ = f32[1088,128]{1,0:T(8,128)} custom-call(f32[128,128]{1,0:T(8,128)} %get-tuple-element.27.refs_5_.refs_0_, f32[128,128]{1,0:T(8,128)} %collective-permute-done.2.refs_1_, f32[128,128]{1,0:T(8,128)} %collective-permute-done.3.refs_2_, f32[128,128]{1,0:T(8,128)} %collective-permute-done.4.refs_3_, ...), custom_call_target="tpu_custom_call" | custom-call | bytes 28800000 | tf_op jit(solution)/shard_map/upward/pallas_call | solution.py:500
  31.6 10.0 %all-to-all-start = ((f32[64,1,2176]{2,1,0:T(1,128)}), f32[64,1,2176]{2,1,0:T(1,128)}, u32[]{:S(2)}, u32[]{:S(2)}) async-start(f32[64,1,2176]{2,1,0:T(1,128)} %bitcast.60), calls=%async_computation | async-start | bytes 1114112 | tf_op jit(solution)/shard_map/all_to_all | solution.py:647
  41.6 2.9 %advect_air.1 = (f32[256,128]{1,0:T(8,128)}, f32[256,128]{1,0:T(8,128)}, f32[256,128]{1,0:T(8,128)}, f32[256,128]{1,0:T(8,128)}) custom-call(f32[1024,128]{1,0:T(8,128)} %bitcast.67, f32[256,128]{1,0:T(8,128)} %bitcast.76, f32[20,128]{1,0:T(8,128)} %collective-permute-done.refs_2_, f32[20,128]{1,0:T(8,128)} %collective-permute-done.1.refs_3_, ...), custom_call_target="tpu_custom_call" | custom-call | bytes 9000000 | tf_op jit(solution)/shard_map/advect_air/pallas_call | solution.py:500
  44.5 0.5 collective-permute-start.5
  45.0 1.0 %collective-permute-start.6 = (f32[256,128]{1,0:T(8,128)}, f32[256,128]{1,0:T(8,128)}, u32[]{:S(2)}, u32[]{:S(2)}) collective-permute-start(f32[256,128]{1,0:T(8,128)} %get-tuple-element.36), channel_id=1, source_target_pairs={{0,2},{1,3},{2,0},{3,1},{4,6},{5,7},{6,4},{7,5},{8,10},{9,11},{10,... | collective-permute-start | bytes 393224 | tf_op jit(solution)/shard_map/ppermute | solution.py:585
  46.0 0.0 collective-permute-start.7
  46.0 2.9 %advect_sea.1 = (f32[256,128]{1,0:T(8,128)}, f32[256,128]{1,0:T(8,128)}, f32[256,128]{1,0:T(8,128)}, f32[256,128]{1,0:T(8,128)}) custom-call(f32[1024,128]{1,0:T(8,128)} %bitcast.63, f32[256,128]{1,0:T(8,128)} %bitcast.73, f32[20,128]{1,0:T(8,128)} %collective-permute-done.refs_2_, f32[20,128]{1,0:T(8,128)} %collective-permute-done.1.refs_3_, ...), custom_call_target="tpu_custom_call" | custom-call | bytes 9000000 | tf_op jit(solution)/shard_map/advect_sea/pallas_call | solution.py:500
  48.9 0.5 collective-permute-done.5.refs_2_.refs_1_
  49.4 7.3 %collective-permute-done.6.refs_3_.refs_2_ = f32[256,128]{1,0:T(8,128)} collective-permute-done((f32[256,128]{1,0:T(8,128)}, f32[256,128]{1,0:T(8,128)}, u32[]{:S(2)}, u32[]{:S(2)}) %collective-permute-start.6) | collective-permute-done | bytes 131104 | tf_op jit(solution)/shard_map/ppermute | solution.py:585
  56.7 0.5 collective-permute-done.7.refs_4_.refs_3_
  57.2 3.3 %all-to-all-done = f32[64,1,2176]{2,1,0:T(1,128)} async-done(((f32[64,1,2176]{2,1,0:T(1,128)}), f32[64,1,2176]{2,1,0:T(1,128)}, u32[]{:S(2)}, u32[]{:S(2)}) %all-to-all-start) | async-done | bytes 557088 | tf_op jit(solution)/shard_map/all_to_all | solution.py:647
  60.5 5.7 %middle.1 = (f32[128,128]{1,0:T(8,128)}, f32[512,128]{1,0:T(8,128)}, f32[64,128]{1,0:T(8,128)}) custom-call(f32[1088,128]{1,0:T(8,128)} %bitcast.33.refs_0_, f32[256,128]{1,0:T(8,128)} %get-tuple-element.34.refs_1_.refs_0_, f32[256,128]{1,0:T(8,128)} %collective-permute-done.5.refs_2_.refs_1_, f32[256,128]{1,0:T(8,128)} %collective-permute-done.6.refs_3_.refs_2_, ...), custom_call_target="tpu_custom_call" | custom-call | bytes 28800000 | tf_op jit(solution)/shard_map/middle/pallas_call | solution.py:500
  66.2 8.3 %all-to-all-start.1 = ((f32[64,8,128]{2,1,0:T(8,128)}), f32[64,8,128]{2,1,0:T(8,128)}, u32[]{:S(2)}, u32[]{:S(2)}) async-start(f32[64,8,128]{2,1,0:T(8,128)} %bitcast.78), calls=%async_computation.1 | async-start | bytes 524288 | tf_op jit(solution)/shard_map/all_to_all | solution.py:647
  74.6 0.1 collective-permute-start.8
  74.7 1.1 %collective-permute-start.9 = (f32[256,128]{1,0:T(8,128)}, f32[256,128]{1,0:T(8,128)}, u32[]{:S(2)}, u32[]{:S(2)}) collective-permute-start(f32[256,128]{1,0:T(8,128)} %get-tuple-element.44), channel_id=1, source_target_pairs={{0,2},{1,3},{2,0},{3,1},{4,6},{5,7},{6,4},{7,5},{8,10},{9,11},{10,... | collective-permute-start | bytes 393224 | tf_op jit(solution)/shard_map/ppermute | solution.py:585
  75.7 0.0 collective-permute-start.10
  75.7 2.9 %solve_air.1.refs_7_ = f32[1024,128]{1,0:T(8,128)} custom-call(f32[256,128]{1,0:T(8,128)} %get-tuple-element.34.refs_1_.refs_0_, f32[256,128]{1,0:T(8,128)} %collective-permute-done.5.refs_2_.refs_1_, f32[256,128]{1,0:T(8,128)} %collective-permute-done.6.refs_3_.refs_2_, f32[256,128]{1,0:T(8,128)} %collective-permute-done.7.refs_4_.refs_3_, ...), custom_call_target="tpu_custom_call" | custom-call | bytes 10800000 | tf_op jit(solution)/shard_map/solve_air/pallas_call | solution.py:500
  78.6 0.0 collective-permute-done.8.refs_1_
  78.6 5.6 %collective-permute-done.9.refs_2_ = f32[256,128]{1,0:T(8,128)} collective-permute-done((f32[256,128]{1,0:T(8,128)}, f32[256,128]{1,0:T(8,128)}, u32[]{:S(2)}, u32[]{:S(2)}) %collective-permute-start.9) | collective-permute-done | bytes 131104 | tf_op jit(solution)/shard_map/ppermute | solution.py:585
  84.3 1.0 %collective-permute-done.10.refs_3_ = f32[256,128]{1,0:T(8,128)} collective-permute-done((f32[256,128]{1,0:T(8,128)}, f32[256,128]{1,0:T(8,128)}, u32[]{:S(2)}, u32[]{:S(2)}) %collective-permute-start.10) | collective-permute-done | bytes 131104 | tf_op jit(solution)/shard_map/ppermute | solution.py:585
  85.2 3.1 %solve_sea.1 = (f32[1024,128]{1,0:T(8,128)}, f32[1024,128]{1,0:T(8,128)}) custom-call(f32[256,128]{1,0:T(8,128)} %get-tuple-element.39.refs_9_.refs_0_, f32[256,128]{1,0:T(8,128)} %collective-permute-done.8.refs_1_, f32[256,128]{1,0:T(8,128)} %collective-permute-done.9.refs_2_, f32[256,128]{1,0:T(8,128)} %collective-permute-done.10.refs_3_, ...), custom_call_target="tpu_custom_call" | custom-call | bytes 10800000 | tf_op jit(solution)/shard_map/solve_sea/pallas_call | solution.py:500
  88.3 0.6 all-to-all-done.1
  88.9 2.3 %last.1 = f32[1024,128]{1,0:T(8,128)} custom-call(f32[512,128]{1,0:T(8,128)} %bitcast.43.refs_0_, f32[64,128]{1,0:T(8,128)} %get-tuple-element.42.refs_1_, f32[1024,128]{1,0:T(8,128)} %get-tuple-element.46.refs_2_, f32[1024,128]{1,0:T(8,128)} %get-tuple-element.47.refs_3_), custom_call_target="tpu_custom_call" | custom-call | bytes 7200000 | tf_op jit(solution)/shard_map/last/pallas_call | solution.py:500
Async XLA Ops:
  2.3 12.1 %collective-permute-start = (f32[20,128]{1,0:T(8,128)}, f32[20,128]{1,0:T(8,128)}, u32[]{:S(2)}, u32[]{:S(2)}) collective-permute-start(f32[20,128]{1,0:T(8,128)} %get-tuple-element.25), channel_id=1, source_target_pairs={{0,4},{4,0},{8,12},{12,8},{16,20},{20,16},{24,28},{28,24},{32,36},... | collective-permute-start | bytes 30728 | tf_op jit(solution)/shard_map/ppermute | solution.py:578
  4.9 11.0 %collective-permute-start.1 = (f32[20,128]{1,0:T(8,128)}, f32[20,128]{1,0:T(8,128)}, u32[]{:S(2)}, u32[]{:S(2)}) collective-permute-start(f32[20,128]{1,0:T(8,128)} %get-tuple-element.26), channel_id=1, source_target_pairs={{0,252},{4,8},{8,4},{12,16},{16,12},{20,24},{24,20},{28,32},{32,28... | collective-permute-start | bytes 30728 | tf_op jit(solution)/shard_map/ppermute | solution.py:579
  18.5 5.3 %collective-permute-start.2 = (f32[128,128]{1,0:T(8,128)}, f32[128,128]{1,0:T(8,128)}, u32[]{:S(2)}, u32[]{:S(2)}) collective-permute-start(f32[128,128]{1,0:T(8,128)} %get-tuple-element.28), channel_id=1, source_target_pairs={{0,1},{1,2},{2,3},{3,0},{4,5},{5,6},{6,7},{7,4},{8,9},{9,10},{10,1... | collective-permute-start | bytes 196616 | tf_op jit(solution)/shard_map/ppermute | solution.py:585
  20.6 4.7 %collective-permute-start.3 = (f32[128,128]{1,0:T(8,128)}, f32[128,128]{1,0:T(8,128)}, u32[]{:S(2)}, u32[]{:S(2)}) collective-permute-start(f32[128,128]{1,0:T(8,128)} %get-tuple-element.29), channel_id=1, source_target_pairs={{0,2},{1,3},{2,0},{3,1},{4,6},{5,7},{6,4},{7,5},{8,10},{9,11},{10,... | collective-permute-start | bytes 196616 | tf_op jit(solution)/shard_map/ppermute | solution.py:585
  21.7 4.1 %collective-permute-start.4 = (f32[128,128]{1,0:T(8,128)}, f32[128,128]{1,0:T(8,128)}, u32[]{:S(2)}, u32[]{:S(2)}) collective-permute-start(f32[128,128]{1,0:T(8,128)} %get-tuple-element.30), channel_id=1, source_target_pairs={{0,3},{1,0},{2,1},{3,2},{4,7},{5,4},{6,5},{7,6},{8,11},{9,8},{10,9... | collective-permute-start | bytes 196616 | tf_op jit(solution)/shard_map/ppermute | solution.py:585
  31.6 29.0 %all-to-all-start = ((f32[64,1,2176]{2,1,0:T(1,128)}), f32[64,1,2176]{2,1,0:T(1,128)}, u32[]{:S(2)}, u32[]{:S(2)}) async-start(f32[64,1,2176]{2,1,0:T(1,128)} %bitcast.60), calls=%async_computation | async-start | bytes 1114112 | tf_op jit(solution)/shard_map/all_to_all | solution.py:647
  44.5 4.9 %collective-permute-start.5 = (f32[256,128]{1,0:T(8,128)}, f32[256,128]{1,0:T(8,128)}, u32[]{:S(2)}, u32[]{:S(2)}) collective-permute-start(f32[256,128]{1,0:T(8,128)} %get-tuple-element.35), channel_id=1, source_target_pairs={{0,1},{1,2},{2,3},{3,0},{4,5},{5,6},{6,7},{7,4},{8,9},{9,10},{10,1... | collective-permute-start | bytes 393224 | tf_op jit(solution)/shard_map/ppermute | solution.py:585
  45.0 11.7 %collective-permute-start.6 = (f32[256,128]{1,0:T(8,128)}, f32[256,128]{1,0:T(8,128)}, u32[]{:S(2)}, u32[]{:S(2)}) collective-permute-start(f32[256,128]{1,0:T(8,128)} %get-tuple-element.36), channel_id=1, source_target_pairs={{0,2},{1,3},{2,0},{3,1},{4,6},{5,7},{6,4},{7,5},{8,10},{9,11},{10,... | collective-permute-start | bytes 393224 | tf_op jit(solution)/shard_map/ppermute | solution.py:585
  46.0 11.3 %collective-permute-start.7 = (f32[256,128]{1,0:T(8,128)}, f32[256,128]{1,0:T(8,128)}, u32[]{:S(2)}, u32[]{:S(2)}) collective-permute-start(f32[256,128]{1,0:T(8,128)} %get-tuple-element.37), channel_id=1, source_target_pairs={{0,3},{1,0},{2,1},{3,2},{4,7},{5,4},{6,5},{7,6},{8,11},{9,8},{10,9... | collective-permute-start | bytes 393224 | tf_op jit(solution)/shard_map/ppermute | solution.py:585
  66.2 22.7 %all-to-all-start.1 = ((f32[64,8,128]{2,1,0:T(8,128)}), f32[64,8,128]{2,1,0:T(8,128)}, u32[]{:S(2)}, u32[]{:S(2)}) async-start(f32[64,8,128]{2,1,0:T(8,128)} %bitcast.78), calls=%async_computation.1 | async-start | bytes 524288 | tf_op jit(solution)/shard_map/all_to_all | solution.py:647
  74.6 4.1 %collective-permute-start.8 = (f32[256,128]{1,0:T(8,128)}, f32[256,128]{1,0:T(8,128)}, u32[]{:S(2)}, u32[]{:S(2)}) collective-permute-start(f32[256,128]{1,0:T(8,128)} %get-tuple-element.43), channel_id=1, source_target_pairs={{0,1},{1,2},{2,3},{3,0},{4,5},{5,6},{6,7},{7,4},{8,9},{9,10},{10,1... | collective-permute-start | bytes 393224 | tf_op jit(solution)/shard_map/ppermute | solution.py:585
  74.7 9.6 %collective-permute-start.9 = (f32[256,128]{1,0:T(8,128)}, f32[256,128]{1,0:T(8,128)}, u32[]{:S(2)}, u32[]{:S(2)}) collective-permute-start(f32[256,128]{1,0:T(8,128)} %get-tuple-element.44), channel_id=1, source_target_pairs={{0,2},{1,3},{2,0},{3,1},{4,6},{5,7},{6,4},{7,5},{8,10},{9,11},{10,... | collective-permute-start | bytes 393224 | tf_op jit(solution)/shard_map/ppermute | solution.py:585
  75.7 9.5 %collective-permute-start.10 = (f32[256,128]{1,0:T(8,128)}, f32[256,128]{1,0:T(8,128)}, u32[]{:S(2)}, u32[]{:S(2)}) collective-permute-start(f32[256,128]{1,0:T(8,128)} %get-tuple-element.45), channel_id=1, source_target_pairs={{0,3},{1,0},{2,1},{3,2},{4,7},{5,4},{6,5},{7,6},{8,11},{9,8},{10,9... | collective-permute-start | bytes 393224 | tf_op jit(solution)/shard_map/ppermute | solution.py:585

commit v2 on v1

--- a/solution.py
+++ b/solution.py
@@ -58,7 +58,9 @@
     return jnp.where(condition, 1.0, 0.0).astype(BF16)
 
 
-def prepare_kernel(tiles, ut, ub, dt, db, mask, up_out, down_out, label_out, mask_out):
+def prepare_kernel(
+    tiles, ut, ub, dt, db, mask, up_out, down_out, label_out, mask_out, ready_out
+):
     blocks = ut.shape[1]
     groups = blocks // 2
     entries = 2 * blocks
@@ -104,6 +106,7 @@
         term = dot(picked, side)
         spread = term if spread is None else spread + term
     mask_out[...] = spread
+    ready_out[...] = spread[0:8]
 
 
 def edge_kernel(sea, air, sea_c, air_c, place, pair_out, next_out, first, last, sems):
@@ -165,31 +168,86 @@
     return jnp.maximum(c, 0.0), jnp.minimum(c, 0.0)
 
 
-def surface_kernel(sea, sea_c, pair, other, place, o0, o1, o2, o3, sbuf, xbuf, cbuf, sems):
-    rows = sea_c.shape[0] // 2
+def upwind(x, positive, negative, below, above):
+    return x - positive * (x - below) - negative * (above - x)
+
+
+def sea_kernel(fields, state, courant, place, o0, o1, o2, o3, sbuf, sems):
+    rows = courant.shape[0] // 2
     size = 2 * rows
     outs = (o0, o1, o2, o3)
     order = (1, 2, 3, 0)
 
     def copy(d):
-        return pltpu.make_async_copy(sea.at[pl.ds(d * size, size)], sbuf.at[d], sems.at[d])
+        field = lax.rem(place[0] + d, fields)
+        at = pl.multiple_of(field * size, size)
+        return pltpu.make_async_copy(state.at[pl.ds(at, size)], sbuf.at[d], sems.at[d])
 
     for d in order:
         copy(d).start()
-    left, right = neighbours(pair, other, place)
-    c = sea_c.get()[pl.ds(0, rows, stride=2), :]
-    positive, negative = speeds(c, left[8:9, :], right[8:9, :], cbuf)
+    lane = iota((rows, LANES), 1)
+    first = lane == 0
+    last = lane == LANES - 1
+    courant = courant.get()
+    signs = []
+    for level in range(2):
+        c = courant[pl.ds(level, rows, stride=2), :]
+        signs.append((jnp.maximum(c, 0.0), jnp.minimum(c, 0.0)))
     for d in order:
         copy(d).wait()
-        x = sbuf[d, pl.ds(0, rows, stride=2), :]
-        low, high = left[2 * d : 2 * d + 1, :], right[2 * d : 2 * d + 1, :]
-        outs[d][...] = stepped(x, low, high, positive, negative, xbuf)
+        out = outs[d]
+        for level in range(2):
+            positive, negative = signs[level]
+            x = sbuf[d, pl.ds(level, rows, stride=2), :]
+            for step in range(2):
+                below = pltpu.roll(x, 1, 1)
+                below = jnp.where(first, pltpu.roll(below, 1, 0), below)
+                above = pltpu.roll(x, LANES - 1, 1)
+                above = jnp.where(last, pltpu.roll(above, rows - 1, 0), above)
+                x = upwind(x, positive, negative, below, above)
+            out[level * rows : (level + 1) * rows, :] = x
+        out[size : size + 2, :] = sbuf[d, 0:2, :]
+        out[size + 2 : size + 4, :] = sbuf[d, size - 2 : size, :]
+        out[size + 4 : size + 6, :] = courant[0:2, :]
+        out[size + 6 : size + 8, :] = courant[size - 2 : size, :]
+
+
+def mended(first, last, left, right):
+    low = low_half(first[0].shape)
+    out = []
+    for inner, outer, kept in ((first, left, low), (last, right, jnp.logical_not(low))):
+        x = jnp.where(kept, inner[0], outer[0])
+        c = jnp.where(kept, inner[1], outer[1])
+        positive, negative = jnp.maximum(c, 0.0), jnp.minimum(c, 0.0)
+        for step in range(2):
+            x = upwind(x, positive, negative, pltpu.roll(x, 1, 1), pltpu.roll(x, LANES - 1, 1))
+        out.append(x)
+    return out
+
+
+def mend(row, mended_row, at_end):
+    lane = iota(row.shape, 1)
+    return jnp.where(lane >= LANES - 2 if at_end else lane < 2, mended_row, row)
+
+
+def outer_rows(halo, field, level, place):
+    rows = (halo.shape[0] - 8) // 2
+    pair, other = [
+        (halo[pl.ds(n * rows + 2 * field + level, 1), :], halo[n * rows + 8 + level : n * rows + 9 + level, :])
+        for n in range(2)
+    ]
+    even = place[0] // 4 == 0
+    left = [jnp.where(even, b, a) for a, b in zip(pair, other)]
+    right = [jnp.where(even, a, b) for a, b in zip(pair, other)]
+    return left, right
 
 
 def advect_kernel(
-    fields, base, state, courant, pair, other, lev, o0, o1, o2, o3, lows, highs, xbuf, cbuf
+    fields, base, state, courant, mixing, pair, other, lev,
+    o0, o1, o2, o3, factor_out, lows, highs, xbuf, cbuf,
 ):
     rows = courant.shape[0] // 2
+    factor_out[...] = mixing.get()[pl.ds(0, rows, stride=8), :]
     lows[...], highs[...] = neighbours(pair, other, lev)
     for level in range(2):
         c = courant.get()[pl.ds(level, rows, stride=2), :]
@@ -262,18 +320,20 @@
     each = groups // 2 // len(copies)
     for n, copy in enumerate(copies):
         copy.wait()
-        if n + AHEAD < len(copies):
-            copies[n + AHEAD].start()
+        if n + AHEAD + 1 < len(copies):
+            copies[n + AHEAD + 1].start()
         lax.fori_loop(n * each, (n + 1) * each, body, 0, unroll=each)
     return product_sums(lambda row: res[pl.ds(row, groups, stride=count), :], ones is not None)
 
 
-def entry_values(sums):
+def entry_order():
     row, column = iota((256, 512), 0), iota((256, 512), 1)
     same = ((row >> 6) & 1) * 2 + (row & 1) == (column >> 7)
     cell = ((row >> 1) & 31) * 2 + (row >> 7)
-    order = onehot(same & (cell == (column & 63)))
-
+    return onehot(same & (cell == (column & 63)))
+
+
+def entry_values(sums, order):
     def ordered(pair):
         high, low = split(jnp.concatenate(pair, 1))
         return dot(high, order), dot(low, order)
@@ -290,12 +350,15 @@
     return jnp.concatenate(terms, 1)
 
 
-def dispatched(place, entries):
-    count = entries.shape[0]
+def slot_order(place):
+    count = place.shape[1]
+    return [onehot(iota((count, count), 0) == place[half : half + 1, :]) for half in range(2)]
+
+
+def dispatched(orders, entries):
     out = []
-    for half in range(2):
-        chosen = onehot(iota((count, count), 0) == place[half : half + 1, :])
-        slots = dot(chosen, entries)
+    for order in orders:
+        slots = dot(order, entries)
         out.append(slots[:, :LANES] + slots[:, LANES:])
     return out
 
@@ -314,17 +377,30 @@
 
 
 def up_kernel(
-    p0, p1, p2, p3, mask, place, labels, weight, lev, out, values, wbuf, lhs, res, sem, wsems
+    p0, p1, p2, p3, h0, h1, h2, h3, mask, place, labels, weight, lev,
+    out, values, halo, wbuf, lhs, res, sems, wsems,
 ):
     tiles = labels.shape[0]
-    field = surface_copy((p0, p1, p2, p3), 0, lev, values, sem)
+    rows = mask.shape[0]
+    own = surface_copy((h0, h1, h2, h3), 0, lev, halo, sems.at[1])
+    field = surface_copy((p0, p1, p2, p3), 0, lev, values, sems.at[0])
     copies = weight_copies(weight, wbuf, wsems)
     for copy in copies[:AHEAD]:
         copy.start()
+    order = entry_order()
+    slots = slot_order(place.get())
     field.wait()
+    own.wait()
+    copies[AHEAD].start()
+    ends = values[2 * rows :, :]
+    mended_rows = mended(
+        (ends[0:1], ends[4:5]), (ends[2:3], ends[6:7]), *outer_rows(halo, lev[0] % 4, 0, lev)
+    )
+    for n, at in enumerate((0, rows - 1)):
+        values[at : at + 1, :] = mend(values[at : at + 1, :], mended_rows[n], n == 1)
     mask_value = mask.get()[...]
-    sums = products(values[...] * mask_value, mask_value, copies, wbuf, lhs, res)
-    even, odd = dispatched(place.get(), entry_values(sums))
+    sums = products(values[0:rows, :] * mask_value, mask_value, copies, wbuf, lhs, res)
+    even, odd = dispatched(slots, entry_values(sums, order))
     half = low_half((tiles, LANES))
     pitch = out.shape[0] // tiles
     for i in range(SLOTS // 2):
@@ -372,7 +448,7 @@
 
 
 def middle_kernel(
-    arrived, p0, p1, p2, p3, mixing, place, weight, lev,
+    arrived, p0, p1, p2, p3, factor, place, weight, lev,
     flux_out, out, label_out, values, wbuf, lhs, res, sem, wsems,
 ):
     groups = flux_out.shape[0]
@@ -381,7 +457,10 @@
     copies = weight_copies(weight, wbuf, wsems)
     for copy in copies[:AHEAD]:
         copy.start()
+    order = entry_order()
+    slots = slot_order(place.get())
     arrived = arrived.get()
+    copies[AHEAD].start()
     labels = arrived[pl.ds(SLOTS, tiles, stride=SLOTS + 1), :]
     label_out[...] = labels
     names = named_blocks(labels, 0, groups)
@@ -389,11 +468,10 @@
     cover = slot_rows(arrived, SLOTS // 2, SLOTS // 2, tiles)
     received, coverage = collected((field, cover), names)
     surface.wait()
-    factor = mixing.get()[pl.ds(0, groups, stride=8), :]
-    flux = factor * (coverage * values[...] - received)
+    flux = factor.get()[...] * (coverage * values[...] - received)
     flux_out[...] = flux
     sums = products(flux, None, copies, wbuf, lhs, res)
-    even, odd = dispatched(place.get(), entry_values(sums))
+    even, odd = dispatched(slots, entry_values(sums, order))
     half = low_half((tiles, LANES))
     pitch = out.shape[0] // tiles
     for i in range(SLOTS // 2):
@@ -401,27 +479,42 @@
         out[pl.ds(i, tiles, stride=pitch), :] = jnp.where(half, a, b)
 
 
-def solve_kernel(with_flux, p0, p1, p2, p3, mixing, extra, lev, *refs):
+def solve_kernel(with_flux, p0, p1, p2, p3, *refs):
     if with_flux:
-        out, buf, sems = refs
+        mixing, extra, lev, out, buf, sems = refs
+        sources = [((p0, p1, p2, p3), buf, 0)]
     else:
-        out, unit_out, buf, sems = refs
+        h0, h1, h2, h3, mixing, extra, lev, out, unit_out, buf, halo, sems = refs
+        sources = [((p0, p1, p2, p3), buf, 0), ((h0, h1, h2, h3), halo, 4)]
     groups = extra.shape[0]
     chunk = 16
     levels = 8
     copies = []
-    for d, part in enumerate((p0, p1, p2, p3)):
-        source = lax.rem(lev[0] + 4 - d, 4)
-        copies.append(
-            pltpu.make_async_copy(
-                part.at[pl.ds(0, 2 * groups)], buf.at[source], sems.at[d]
-            )
-        )
+    for parts, to, base in sources:
+        for d, part in enumerate(parts):
+            source = lax.rem(lev[0] + 4 - d, 4)
+            copies.append(pltpu.make_async_copy(part, to.at[source], sems.at[base + d]))
     for copy in copies:
         copy.start()
     kbuf, ebuf = mixing.get(), extra.get()
     for copy in copies:
         copy.wait()
+    if not with_flux:
+        parts = [[[], []] for n in range(4)]
+        for level in range(levels):
+            at = 2 * groups + level % 2
+            ends = [buf[level // 2, at + 2 * n : at + 2 * n + 1, :] for n in range(4)]
+            left, right = outer_rows(halo.at[level // 2], lev[0] % 4, level % 2, lev)
+            for n, rows in enumerate(((ends[0], ends[2]), (ends[1], ends[3]), left, right)):
+                parts[n][0].append(rows[0])
+                parts[n][1].append(rows[1])
+        mended_rows = mended(*[[jnp.concatenate(rows, 0) for rows in part] for part in parts])
+        for level in range(levels):
+            at = (level % 2) * groups
+            for n, row in enumerate((at, at + groups - 1)):
+                old = buf[level // 2, row : row + 1, :]
+                new = mended_rows[n][level : level + 1]
+                buf[level // 2, row : row + 1, :] = mend(old, new, n == 1)
 
     def body(step, carry):
         at = pl.multiple_of(step * chunk, chunk)
@@ -460,21 +553,28 @@
     lax.fori_loop(0, groups // chunk, body, 0)
 
 
-def last_kernel(arrived, labels, base, unit, out, gain):
+def last_kernel(arrived, labels, base, unit, out, gain, obuf, sems):
     tiles = labels.shape[0]
-    arrived = arrived.get()
     groups = gain.shape[0]
     names = named_blocks(labels.get()[...], SLOTS, groups)
-    (total,) = collected((slot_rows(arrived, 0, SLOTS // 2, tiles),), names)
+    (total,) = collected((slot_rows(arrived.get(), 0, SLOTS // 2, tiles),), names)
     gain[...] = total
     bbuf, ubuf = base.get(), unit.get()
 
     def body(step, carry):
         at = pl.ds(pl.multiple_of(step * 8, 8), 8)
-        out[at, :] = bbuf[at, :] + ubuf[at, :] * gain[pl.ds(step, 1), :]
+        obuf[at, :] = bbuf[at, :] + ubuf[at, :] * gain[pl.ds(step, 1), :]
         return carry
 
-    lax.fori_loop(0, groups, body, 0, unroll=8)
+    pieces = sems.shape[0]
+    copies = []
+    for n in range(pieces):
+        lax.fori_loop(n * groups // pieces, (n + 1) * groups // pieces, body, 0, unroll=8)
+        rows = pl.ds(n * 8 * groups // pieces, 8 * groups // pieces)
+        copies.append(pltpu.make_async_copy(obuf.at[rows], out.at[rows], sems.at[n]))
+        copies[n].start()
+    for copy in copies:
+        copy.wait()
 
 
 VMEM = pl.BlockSpec(memory_space=pltpu.VMEM)
@@ -483,7 +583,7 @@
 DMA = pltpu.SemaphoreType.DMA
 
 
-def call(kernel, shapes, args, spaces, scratch=(), name=None, us=1.0, after=()):
+def call(kernel, shapes, args, spaces, scratch=(), name=None, us=1.0, after=(), to=None):
     fetched = [i for i, space in enumerate(spaces) if space == "f"]
     outs = len(shapes) if isinstance(shapes, tuple) else 1
 
@@ -502,7 +602,7 @@
         out_shape=shapes,
         in_specs=[{"v": VMEM, "s": SMEM, "h": HBM, "f": HBM}[space] for space in spaces]
         + [HBM] * len(after),
-        out_specs=jax.tree.map(lambda _: VMEM, shapes),
+        out_specs=jax.tree.map(lambda _: VMEM, shapes) if to is None else to,
         scratch_shapes=list(scratch) + extra,
         compiler_params=pltpu.CompilerParams(vmem_limit_bytes=64 * 1024 * 1024),
         cost_estimate=pl.CostEstimate(
@@ -586,25 +686,26 @@
             for d in range(1, levs)
         ]
 
-    surface = call(
-        surface_kernel,
-        (shape(rows, LANES),) * 4,
-        (states[0], states[2], *ends, lev_ref),
-        "hfffs",
-        scratch=[pltpu.VMEM((4, size, LANES), F32), extended, extended, DMA((4,))],
-        name="surface",
-        us=2.5,
-    )
-    surface_parts = around(surface)
-
+    sea_own = call(
+        functools.partial(sea_kernel, fields),
+        (shape(size + 8, LANES),) * 4,
+        (states[0], states[2], lev_ref),
+        "hfs",
+        scratch=[pltpu.VMEM((4, size, LANES), F32), DMA((4,))],
+        name="sea",
+        us=3.0,
+        after=(to_pair,),
+    )
+    sea = around(sea_own)
     entries = 4 * groups
-    place_up, place_down, labels, mask = call(
+    place_up, place_down, labels, mask, ready = call(
         functools.partial(prepare_kernel, tiles),
         (
             shape(2, entries, dtype=jnp.int32),
             shape(2, entries, dtype=jnp.int32),
             shape(tiles, LANES),
             shape(groups, LANES),
+            shape(8, LANES),
         ),
         (
             upward_target.T,
@@ -616,8 +717,9 @@
         "fffff",
         name="prepare",
         us=2.5,
-        after=(surface[0],),
-    )
+        after=(sea_own[0],),
+    )
+    halo = around([jnp.concatenate([*ends, ready], 0)] * 4)
     air_k = tile_rows(air_mixing, 1)
     sea_k = tile_rows(sea_mixing, 1)
     up_rows = weight_rows(upward_weight)
@@ -634,9 +736,15 @@
     outgoing = call(
         up_kernel,
         shape(tiles * pitch, LANES),
-        (*surface_parts, mask, place_up, labels, up_rows, lev_ref),
-        "hhhhfffhs",
-        scratch=[pltpu.VMEM((rows, LANES), F32), *workspace(16), DMA(()), DMA((PIECES,))],
+        (*sea, *halo, mask, place_up, labels, up_rows, lev_ref),
+        "hhhhhhhhfffhs",
+        scratch=[
+            pltpu.VMEM((size + 8, LANES), F32),
+            pltpu.VMEM(halo[0].shape, F32),
+            *workspace(16),
+            DMA((2,)),
+            DMA((PIECES,)),
+        ],
         name="upward",
         us=8.0,
     )
@@ -650,54 +758,57 @@
     def advected(state, courant, base, name):
         return call(
             functools.partial(advect_kernel, fields, base),
-            tuple(shape(size, LANES) for _ in range(4)),
-            (state, courant, *ends, lev_ref),
-            "ffffs",
+            (shape(size, LANES),) * 4 + (shape(rows, LANES),),
+            (state, courant, air_k, *ends, lev_ref),
+            "fffffs",
             scratch=[pltpu.VMEM((20, LANES), F32)] * 2 + [extended, extended],
             name=name,
             us=2.5,
             after=(outgoing,),
         )
 
-    air = around(advected(states[1], states[3], 10, "advect_air"))
-    sea_own = advected(states[0], states[2], 0, "advect_sea")
+    *air, factor = advected(states[1], states[3], 10, "advect_air")
+    air = around(air)
     arrived = over_tiles(outgoing)
     flux, returning, labels_down = call(
         middle_kernel,
         (shape(groups, LANES), shape(tiles * SLOTS // 2, LANES), shape(tiles, LANES)),
-        (arrived, *air, air_k, place_down, down_rows, lev_ref),
+        (arrived, *air, factor, place_down, down_rows, lev_ref),
         "fhhhhffhs",
         scratch=[pltpu.VMEM((rows, LANES), F32), *workspace(8), DMA(()), DMA((PIECES,))],
         name="middle",
         us=8.0,
-        after=(sea_own[0],),
     )
     gained = over_tiles(returning)
-    sea = around(sea_own)
 
     column = shape(8 * rows, LANES)
 
-    def solve(with_flux, parts, k, extra, name, after=()):
+    def solve(with_flux, parts, k, extra, name):
+        part, halo_part = (4, *parts[0].shape), (4, *halo[0].shape)
         return call(
             functools.partial(solve_kernel, with_flux),
             column if with_flux else (column, column),
             (*parts, k, extra, lev_ref),
-            "hhhhffs",
-            scratch=[pltpu.VMEM((4, size, LANES), F32), DMA((4,))],
+            "h" * len(parts) + "ffs",
+            scratch=[
+                pltpu.VMEM(part, F32),
+                *([] if with_flux else [pltpu.VMEM(halo_part, F32)]),
+                DMA((len(parts),)),
+            ],
             name=name,
             us=3.0,
-            after=after,
         )
 
+    base, unit = solve(False, [*sea, *halo], sea_k, mask, "solve_sea")
     air_out = solve(True, air, air_k, flux, "solve_air")
-    base, unit = solve(False, sea, sea_k, mask, "solve_sea", (air_out,))
     sea_out = call(
         last_kernel,
         column,
         (gained, labels_down, base, unit),
         "ffff",
-        scratch=[pltpu.VMEM((rows, LANES), F32)],
+        scratch=[pltpu.VMEM((rows, LANES), F32), pltpu.VMEM((8 * rows, LANES), F32), DMA((4,))],
         name="last",
+        to=HBM,
         us=2.0,
     )
 

time: 92 us -> 91.3 us (level)
  waiting for transfers between devices: 22.2 us -> 26 us
  starting transfers between devices: 36.4 us -> 33.2 us
  Pallas kernels: 31.9 us -> 29.2 us
    all_to_all x2, waiting for transfers between devices: 3.88 us -> 12.8 us  [over_tiles(): y = lax.all_to_all(y, 'tiles', split_axis=0, concat_axis=0, tiled=True)]
    all_to_all x2, starting transfers between devices: 18.4 us -> 12.8 us  [over_tiles(): y = lax.all_to_all(y, 'tiles', split_axis=0, concat_axis=0, tiled=True)]
    ppermute x9, waiting for transfers between devices: 16.9 us -> 13.2 us  [around(): lax.ppermute(parts[d], 'lev', [(i, (i + d) % levs) for i in range(levs)])]
    pallas_call x10 -> x9, Pallas kernels: 31.9 us -> 29.2 us  [call(): pl.pallas_call(body, out_shape=shapes, in_specs=[{'v': VMEM, 's': SMEM, '...]
    ppermute x9, starting transfers between devices: 5.91 us -> 8.31 us  [around(): lax.ppermute(parts[d], 'lev', [(i, (i + d) % levs) for i in range(levs)])]
    ppermute x1, waiting for transfers between devices: 1.39 us -> 0.01 us  [on_device(): lax.ppermute(to_other, 'tiles', others)]
  transfers between devices with their start and end apart: 13 -> 13, of which waited for: 10 -> 8; matrix products, arithmetic and copies ran while one was open for 0% -> 1% of each run, Pallas kernels for 15% -> 16%
where the time goes in v2:
time: 91.3 us; the launch traced here: 90.7 us
  starting transfers between devices  33.2 us (36%)
  Pallas kernels  29.2 us (32%)
  waiting for transfers between devices  26 us (28%)
  between operations  0.94 us (1%)
    pallas_call x9, Pallas kernels, call(): pl.pallas_call(body, out_shape=shapes, in_specs=[{'v': VMEM, 's': SMEM, '...  29.2 us
    ppermute x9, waiting for transfers between devices, around(): lax.ppermute(parts[d], 'lev', [(i, (i + d) % levs) for i in range(levs)])  13.2 us
    all_to_all x2, waiting for transfers between devices, over_tiles(): y = lax.all_to_all(y, 'tiles', split_axis=0, concat_axis=0, tiled=True)  12.8 us
    all_to_all x2, starting transfers between devices, over_tiles(): y = lax.all_to_all(y, 'tiles', split_axis=0, concat_axis=0, tiled=True)  12.8 us
    ppermute x1, starting transfers between devices, on_device(): lax.ppermute(to_other, 'tiles', others)  9.58 us
    ppermute x9, starting transfers between devices, around(): lax.ppermute(parts[d], 'lev', [(i, (i + d) % levs) for i in range(levs)])  8.31 us
    ppermute x1, starting transfers between devices, on_device(): lax.ppermute(to_pair, 'tiles', pairs)  2.55 us
  transfers between devices with their start and end apart: 13, of which 8 were waited for; matrix products, arithmetic and copies ran while one was open for 1% of the time, Pallas kernels for 16%

profile of v2, /device:TPU:1, one launch (start us, length us, event | category | flops | bytes accessed | tf_op | source)
XLA Modules:
  0.0 90.7 jit_solution(4245286775863221680)
XLA Ops:
  0.6 1.7 %edges.1 = (f32[20,128]{1,0:T(8,128)}, f32[20,128]{1,0:T(8,128)}) custom-call(f32[1024,128]{1,0:T(8,128)} %bitcast.63, f32[1024,128]{1,0:T(8,128)} %bitcast.65, f32[256,128]{1,0:T(8,128)} %bitcast.72, f32[256,128]{1,0:T(8,128)} %bitcast.74, s32[1]{0:T(128)} %bitcast.19.refs_4_.refs_2_.refs_12_.refs_5_.refs_8_.refs_6_.refs_10_), custom_call_target="tpu_custom_call" | custom-call | bytes 5400000 | tf_op jit(solution)/shard_map/edges/pallas_call | solution.py:600
  2.3 2.6 %collective-permute-start = (f32[20,128]{1,0:T(8,128)}, f32[20,128]{1,0:T(8,128)}, u32[]{:S(2)}, u32[]{:S(2)}) collective-permute-start(f32[20,128]{1,0:T(8,128)} %get-tuple-element.23.refs_3_), channel_id=1, source_target_pairs={{0,4},{4,0},{8,12},{12,8},{16,20},{20,16},{24,28},{28,24},{32,36},... | collective-permute-start | bytes 30728 | tf_op jit(solution)/shard_map/ppermute | solution.py:678
  4.9 9.6 %collective-permute-start.1 = (f32[20,128]{1,0:T(8,128)}, f32[20,128]{1,0:T(8,128)}, u32[]{:S(2)}, u32[]{:S(2)}) collective-permute-start(f32[20,128]{1,0:T(8,128)} %get-tuple-element.24), channel_id=1, source_target_pairs={{0,252},{4,8},{8,4},{12,16},{16,12},{20,24},{24,20},{28,32},{32,28... | collective-permute-start | bytes 30728 | tf_op jit(solution)/shard_map/ppermute | solution.py:679
  14.4 3.0 %sea.1 = (f32[264,128]{1,0:T(8,128)}, f32[264,128]{1,0:T(8,128)}, f32[264,128]{1,0:T(8,128)}, f32[264,128]{1,0:T(8,128)}) custom-call(f32[1024,128]{1,0:T(8,128)} %bitcast.64, f32[256,128]{1,0:T(8,128)} %bitcast.73, s32[1]{0:T(128)} %bitcast.19.refs_4_.refs_2_.refs_12_.refs_5_.refs_8_.refs_6_.refs_10_, f32[20,128]{1,0:T(8,128)} %get-tuple-element.23.refs_3_), custom_call_target="tpu_custom_call" | custom-call | bytes 10800000 | tf_op jit(solution)/shard_map/sea/pallas_call | solution.py:600
  17.4 1.5 %collective-permute-start.2 = (f32[264,128]{1,0:T(8,128)}, f32[264,128]{1,0:T(8,128)}, u32[]{:S(2)}, u32[]{:S(2)}) collective-permute-start(f32[264,128]{1,0:T(8,128)} %get-tuple-element.26), channel_id=1, source_target_pairs={{0,1},{1,2},{2,3},{3,0},{4,5},{5,6},{6,7},{7,4},{8,9},{9,10},{10,1... | collective-permute-start | bytes 405512 | tf_op jit(solution)/shard_map/ppermute | solution.py:685
  19.0 1.2 %collective-permute-start.3 = (f32[264,128]{1,0:T(8,128)}, f32[264,128]{1,0:T(8,128)}, u32[]{:S(2)}, u32[]{:S(2)}) collective-permute-start(f32[264,128]{1,0:T(8,128)} %get-tuple-element.27), channel_id=1, source_target_pairs={{0,2},{1,3},{2,0},{3,1},{4,6},{5,7},{6,4},{7,5},{8,10},{9,11},{10,... | collective-permute-start | bytes 405512 | tf_op jit(solution)/shard_map/ppermute | solution.py:685
  20.1 0.0 collective-permute-start.4
  20.1 2.1 %prepare.1 = (s32[2,512]{1,0:T(2,128)}, s32[2,512]{1,0:T(2,128)}, f32[64,128]{1,0:T(8,128)}, f32[128,128]{1,0:T(8,128)}, f32[8,128]{1,0:T(8,128)}) custom-call(s32[2,256]{1,0:T(2,128)} %bitcast.77, s32[2,256]{1,0:T(2,128)} %bitcast.78, s32[2,256]{1,0:T(2,128)} %bitcast.79, s32[2,256]{1,0:T(2,128)} %bitcast.80, s32[1,256]{1,0:T(1,128)} %bitcast.81, ...), custom_call_target="tpu_custom_call" | custom-call | bytes 9000000 | tf_op jit(solution)/shard_map/prepare/pallas_call | solution.py:600
  22.2 0.0 collective-permute-done.refs_3_
  22.2 0.0 collective-permute-done.1.refs_4_
  22.2 0.7 pad_maximum_fusion.refs_4_
  23.0 0.0 copy-start
  23.0 1.8 %collective-permute-start.5 = (f32[48,128]{1,0:T(8,128)S(1)}, f32[48,128]{1,0:T(8,128)S(1)}, u32[]{:S(2)}, u32[]{:S(2)}) collective-permute-start(f32[48,128]{1,0:T(8,128)S(1)} %pad_maximum_fusion.refs_4_), channel_id=1, source_target_pairs={{0,1},{1,2},{2,3},{3,0},{4,5},{5,6},{6,7},{7,4},{8,9},{9,10},{10,1... | collective-permute-start | bytes 73736 | tf_op jit(solution)/shard_map/ppermute | solution.py:685
  24.8 0.3 collective-permute-start.6
  25.1 0.7 collective-permute-done.5.refs_5_
  25.8 0.0 copy-done
  25.8 0.0 copy-start.1
  25.8 1.9 %collective-permute-start.7 = (f32[48,128]{1,0:T(8,128)S(1)}, f32[48,128]{1,0:T(8,128)S(1)}, u32[]{:S(2)}, u32[]{:S(2)}) collective-permute-start(f32[48,128]{1,0:T(8,128)S(1)} %pad_maximum_fusion.refs_4_), channel_id=1, source_target_pairs={{0,3},{1,0},{2,1},{3,2},{4,7},{5,4},{6,5},{7,6},{8,11},{9,8},{10,9... | collective-permute-start | bytes 73736 | tf_op jit(solution)/shard_map/ppermute | solution.py:685
  27.7 0.4 collective-permute-done.6.refs_6_
  28.1 0.0 copy-start.2
  28.1 1.6 %collective-permute-done.7.refs_7_ = f32[48,128]{1,0:T(8,128)S(1)} collective-permute-done((f32[48,128]{1,0:T(8,128)S(1)}, f32[48,128]{1,0:T(8,128)S(1)}, u32[]{:S(2)}, u32[]{:S(2)}) %collective-permute-start.7) | collective-permute-done | bytes 24608 | tf_op jit(solution)/shard_map/ppermute | solution.py:685
  29.7 0.0 copy-done.1
  29.7 0.0 copy-start.3
  29.7 0.0 collective-permute-done.2.refs_1_
  29.7 0.0 copy-done.2
  29.7 0.0 collective-permute-done.3.refs_2_
  29.8 0.6 copy-done.3
  30.3 0.0 collective-permute-done.4.refs_3_
  30.3 5.5 %upward.1.refs_6_ = f32[1088,128]{1,0:T(8,128)} custom-call(f32[264,128]{1,0:T(8,128)} %get-tuple-element.25.refs_5_.refs_0_, f32[264,128]{1,0:T(8,128)} %collective-permute-done.2.refs_1_, f32[264,128]{1,0:T(8,128)} %collective-permute-done.3.refs_2_, f32[264,128]{1,0:T(8,128)} %collective-permute-done.4.refs_3_, f32[48,128]{1,0:T(8,128)} %copy-done, ...), custom_call_target="tpu_custom_call" | custom-call | bytes 28800000 | tf_op jit(solution)/shard_map/upward/pallas_call | solution.py:600
  35.9 5.5 %all-to-all-start = ((f32[64,1,2176]{2,1,0:T(1,128)}), f32[64,1,2176]{2,1,0:T(1,128)}, u32[]{:S(2)}, u32[]{:S(2)}) async-start(f32[64,1,2176]{2,1,0:T(1,128)} %bitcast.60), calls=%async_computation | async-start | bytes 1114112 | tf_op jit(solution)/shard_map/all_to_all | solution.py:755
  41.4 3.2 %advect_air.1 = (f32[256,128]{1,0:T(8,128)}, f32[256,128]{1,0:T(8,128)}, f32[256,128]{1,0:T(8,128)}, f32[256,128]{1,0:T(8,128)}, f32[128,128]{1,0:T(8,128)}) custom-call(f32[1024,128]{1,0:T(8,128)} %bitcast.66, f32[256,128]{1,0:T(8,128)} %bitcast.75, f32[1024,128]{1,0:T(8,128)} %bitcast.67, f32[20,128]{1,0:T(8,128)} %collective-permute-done.refs_3_, ...), custom_call_target="tpu_custom_call" | custom-call | bytes 9000000 | tf_op jit(solution)/shard_map/advect_air/pallas_call | solution.py:600
  44.5 0.1 collective-permute-start.8
  44.6 1.0 %collective-permute-start.9 = (f32[256,128]{1,0:T(8,128)}, f32[256,128]{1,0:T(8,128)}, u32[]{:S(2)}, u32[]{:S(2)}) collective-permute-start(f32[256,128]{1,0:T(8,128)} %get-tuple-element.35), channel_id=1, source_target_pairs={{0,2},{1,3},{2,0},{3,1},{4,6},{5,7},{6,4},{7,5},{8,10},{9,11},{10,... | collective-permute-start | bytes 393224 | tf_op jit(solution)/shard_map/ppermute | solution.py:685
  45.7 0.5 collective-permute-start.10
  46.2 1.6 %collective-permute-done.8.refs_2_.refs_1_ = f32[256,128]{1,0:T(8,128)} collective-permute-done((f32[256,128]{1,0:T(8,128)}, f32[256,128]{1,0:T(8,128)}, u32[]{:S(2)}, u32[]{:S(2)}) %collective-permute-start.8) | collective-permute-done | bytes 131104 | tf_op jit(solution)/shard_map/ppermute | solution.py:685
  47.8 7.4 %collective-permute-done.9.refs_3_.refs_2_ = f32[256,128]{1,0:T(8,128)} collective-permute-done((f32[256,128]{1,0:T(8,128)}, f32[256,128]{1,0:T(8,128)}, u32[]{:S(2)}, u32[]{:S(2)}) %collective-permute-start.9) | collective-permute-done | bytes 131104 | tf_op jit(solution)/shard_map/ppermute | solution.py:685
  55.2 1.4 %collective-permute-done.10.refs_4_.refs_3_ = f32[256,128]{1,0:T(8,128)} collective-permute-done((f32[256,128]{1,0:T(8,128)}, f32[256,128]{1,0:T(8,128)}, u32[]{:S(2)}, u32[]{:S(2)}) %collective-permute-start.10) | collective-permute-done | bytes 131104 | tf_op jit(solution)/shard_map/ppermute | solution.py:685
  56.7 4.7 %all-to-all-done = f32[64,1,2176]{2,1,0:T(1,128)} async-done(((f32[64,1,2176]{2,1,0:T(1,128)}), f32[64,1,2176]{2,1,0:T(1,128)}, u32[]{:S(2)}, u32[]{:S(2)}) %all-to-all-start) | async-done | bytes 557088 | tf_op jit(solution)/shard_map/all_to_all | solution.py:755
  61.4 5.2 %middle.1 = (f32[128,128]{1,0:T(8,128)}, f32[512,128]{1,0:T(8,128)}, f32[64,128]{1,0:T(8,128)}) custom-call(f32[1088,128]{1,0:T(8,128)} %bitcast.33.refs_0_, f32[256,128]{1,0:T(8,128)} %get-tuple-element.33.refs_1_.refs_0_, f32[256,128]{1,0:T(8,128)} %collective-permute-done.8.refs_2_.refs_1_, f32[256,128]{1,0:T(8,128)} %collective-permute-done.9.refs_3_.refs_2_, ...), custom_call_target="tpu_custom_call" | custom-call | bytes 28800000 | tf_op jit(solution)/shard_map/middle/pallas_call | solution.py:600
  66.6 7.3 %all-to-all-start.1 = ((f32[64,8,128]{2,1,0:T(8,128)}), f32[64,8,128]{2,1,0:T(8,128)}, u32[]{:S(2)}, u32[]{:S(2)}) async-start(f32[64,8,128]{2,1,0:T(8,128)} %bitcast.76), calls=%async_computation.1 | async-start | bytes 524288 | tf_op jit(solution)/shard_map/all_to_all | solution.py:755
  73.9 3.4 %solve_sea.1 = (f32[1024,128]{1,0:T(8,128)}, f32[1024,128]{1,0:T(8,128)}) custom-call(f32[264,128]{1,0:T(8,128)} %get-tuple-element.25.refs_5_.refs_0_, f32[264,128]{1,0:T(8,128)} %collective-permute-done.2.refs_1_, f32[264,128]{1,0:T(8,128)} %collective-permute-done.3.refs_2_, f32[264,128]{1,0:T(8,128)} %collective-permute-done.4.refs_3_, ...), custom_call_target="tpu_custom_call" | custom-call | bytes 10800000 | tf_op jit(solution)/shard_map/solve_sea/pallas_call | solution.py:600
  77.3 2.9 %solve_air.1 = f32[1024,128]{1,0:T(8,128)} custom-call(f32[256,128]{1,0:T(8,128)} %get-tuple-element.33.refs_1_.refs_0_, f32[256,128]{1,0:T(8,128)} %collective-permute-done.8.refs_2_.refs_1_, f32[256,128]{1,0:T(8,128)} %collective-permute-done.9.refs_3_.refs_2_, f32[256,128]{1,0:T(8,128)} %collective-permute-done.10.refs_4_.refs_3_, f32[1024,128]{1,0:T(8,128)} %bitcast.68, ...), custom_call_target="tpu_custom_call" | custom-call | bytes 10800000 | tf_op jit(solution)/shard_map/solve_air/pallas_call | solution.py:600
  80.2 8.1 %all-to-all-done.1 = f32[64,8,128]{2,1,0:T(8,128)} async-done(((f32[64,8,128]{2,1,0:T(8,128)}), f32[64,8,128]{2,1,0:T(8,128)}, u32[]{:S(2)}, u32[]{:S(2)}) %all-to-all-start.1) | async-done | bytes 262176 | tf_op jit(solution)/shard_map/all_to_all | solution.py:755
  88.3 2.3 %last.1 = f32[1024,128]{1,0:T(8,128)} custom-call(f32[512,128]{1,0:T(8,128)} %bitcast.41.refs_0_, f32[64,128]{1,0:T(8,128)} %get-tuple-element.41.refs_1_, f32[1024,128]{1,0:T(8,128)} %get-tuple-element.42.refs_2_, f32[1024,128]{1,0:T(8,128)} %get-tuple-element.43.refs_3_), custom_call_target="tpu_custom_call" | custom-call | bytes 7200000 | tf_op jit(solution)/shard_map/last/pallas_call | solution.py:600
Async XLA Ops:
  2.3 19.9 %collective-permute-start = (f32[20,128]{1,0:T(8,128)}, f32[20,128]{1,0:T(8,128)}, u32[]{:S(2)}, u32[]{:S(2)}) collective-permute-start(f32[20,128]{1,0:T(8,128)} %get-tuple-element.23.refs_3_), channel_id=1, source_target_pairs={{0,4},{4,0},{8,12},{12,8},{16,20},{20,16},{24,28},{28,24},{32,36},... | collective-permute-start | bytes 30728 | tf_op jit(solution)/shard_map/ppermute | solution.py:678
  4.9 17.4 %collective-permute-start.1 = (f32[20,128]{1,0:T(8,128)}, f32[20,128]{1,0:T(8,128)}, u32[]{:S(2)}, u32[]{:S(2)}) collective-permute-start(f32[20,128]{1,0:T(8,128)} %get-tuple-element.24), channel_id=1, source_target_pairs={{0,252},{4,8},{8,4},{12,16},{16,12},{20,24},{24,20},{28,32},{32,28... | collective-permute-start | bytes 30728 | tf_op jit(solution)/shard_map/ppermute | solution.py:679
  17.4 12.3 %collective-permute-start.2 = (f32[264,128]{1,0:T(8,128)}, f32[264,128]{1,0:T(8,128)}, u32[]{:S(2)}, u32[]{:S(2)}) collective-permute-start(f32[264,128]{1,0:T(8,128)} %get-tuple-element.26), channel_id=1, source_target_pairs={{0,1},{1,2},{2,3},{3,0},{4,5},{5,6},{6,7},{7,4},{8,9},{9,10},{10,1... | collective-permute-start | bytes 405512 | tf_op jit(solution)/shard_map/ppermute | solution.py:685
  19.0 10.8 %collective-permute-start.3 = (f32[264,128]{1,0:T(8,128)}, f32[264,128]{1,0:T(8,128)}, u32[]{:S(2)}, u32[]{:S(2)}) collective-permute-start(f32[264,128]{1,0:T(8,128)} %get-tuple-element.27), channel_id=1, source_target_pairs={{0,2},{1,3},{2,0},{3,1},{4,6},{5,7},{6,4},{7,5},{8,10},{9,11},{10,... | collective-permute-start | bytes 405512 | tf_op jit(solution)/shard_map/ppermute | solution.py:685
  20.1 10.2 %collective-permute-start.4 = (f32[264,128]{1,0:T(8,128)}, f32[264,128]{1,0:T(8,128)}, u32[]{:S(2)}, u32[]{:S(2)}) collective-permute-start(f32[264,128]{1,0:T(8,128)} %get-tuple-element.28), channel_id=1, source_target_pairs={{0,3},{1,0},{2,1},{3,2},{4,7},{5,4},{6,5},{7,6},{8,11},{9,8},{10,9... | collective-permute-start | bytes 405512 | tf_op jit(solution)/shard_map/ppermute | solution.py:685
  23.0 2.8 %copy-start = (f32[48,128]{1,0:T(8,128)}, f32[48,128]{1,0:T(8,128)S(1)}, u32[]{:S(2)}) copy-start(f32[48,128]{1,0:T(8,128)S(1)} %pad_maximum_fusion.refs_4_) | copy-start | bytes 73732
  23.0 2.8 %collective-permute-start.5 = (f32[48,128]{1,0:T(8,128)S(1)}, f32[48,128]{1,0:T(8,128)S(1)}, u32[]{:S(2)}, u32[]{:S(2)}) collective-permute-start(f32[48,128]{1,0:T(8,128)S(1)} %pad_maximum_fusion.refs_4_), channel_id=1, source_target_pairs={{0,1},{1,2},{2,3},{3,0},{4,5},{5,6},{6,7},{7,4},{8,9},{9,10},{10,1... | collective-permute-start | bytes 73736 | tf_op jit(solution)/shard_map/ppermute | solution.py:685
  24.8 3.3 %collective-permute-start.6 = (f32[48,128]{1,0:T(8,128)S(1)}, f32[48,128]{1,0:T(8,128)S(1)}, u32[]{:S(2)}, u32[]{:S(2)}) collective-permute-start(f32[48,128]{1,0:T(8,128)S(1)} %pad_maximum_fusion.refs_4_), channel_id=1, source_target_pairs={{0,2},{1,3},{2,0},{3,1},{4,6},{5,7},{6,4},{7,5},{8,10},{9,11},{10,... | collective-permute-start | bytes 73736 | tf_op jit(solution)/shard_map/ppermute | solution.py:685
  25.8 4.0 %copy-start.1 = (f32[48,128]{1,0:T(8,128)}, f32[48,128]{1,0:T(8,128)S(1)}, u32[]{:S(2)}) copy-start(f32[48,128]{1,0:T(8,128)S(1)} %collective-permute-done.5.refs_5_) | copy-start | bytes 73732
  25.8 4.0 %collective-permute-start.7 = (f32[48,128]{1,0:T(8,128)S(1)}, f32[48,128]{1,0:T(8,128)S(1)}, u32[]{:S(2)}, u32[]{:S(2)}) collective-permute-start(f32[48,128]{1,0:T(8,128)S(1)} %pad_maximum_fusion.refs_4_), channel_id=1, source_target_pairs={{0,3},{1,0},{2,1},{3,2},{4,7},{5,4},{6,5},{7,6},{8,11},{9,8},{10,9... | collective-permute-start | bytes 73736 | tf_op jit(solution)/shard_map/ppermute | solution.py:685
  28.1 1.6 %copy-start.2 = (f32[48,128]{1,0:T(8,128)}, f32[48,128]{1,0:T(8,128)S(1)}, u32[]{:S(2)}) copy-start(f32[48,128]{1,0:T(8,128)S(1)} %collective-permute-done.6.refs_6_) | copy-start | bytes 73732
  29.7 0.6 copy-start.3
  35.9 25.5 %all-to-all-start = ((f32[64,1,2176]{2,1,0:T(1,128)}), f32[64,1,2176]{2,1,0:T(1,128)}, u32[]{:S(2)}, u32[]{:S(2)}) async-start(f32[64,1,2176]{2,1,0:T(1,128)} %bitcast.60), calls=%async_computation | async-start | bytes 1114112 | tf_op jit(solution)/shard_map/all_to_all | solution.py:755
  44.5 3.3 %collective-permute-start.8 = (f32[256,128]{1,0:T(8,128)}, f32[256,128]{1,0:T(8,128)}, u32[]{:S(2)}, u32[]{:S(2)}) collective-permute-start(f32[256,128]{1,0:T(8,128)} %get-tuple-element.34), channel_id=1, source_target_pairs={{0,1},{1,2},{2,3},{3,0},{4,5},{5,6},{6,7},{7,4},{8,9},{9,10},{10,1... | collective-permute-start | bytes 393224 | tf_op jit(solution)/shard_map/ppermute | solution.py:685
  44.6 10.6 %collective-permute-start.9 = (f32[256,128]{1,0:T(8,128)}, f32[256,128]{1,0:T(8,128)}, u32[]{:S(2)}, u32[]{:S(2)}) collective-permute-start(f32[256,128]{1,0:T(8,128)} %get-tuple-element.35), channel_id=1, source_target_pairs={{0,2},{1,3},{2,0},{3,1},{4,6},{5,7},{6,4},{7,5},{8,10},{9,11},{10,... | collective-permute-start | bytes 393224 | tf_op jit(solution)/shard_map/ppermute | solution.py:685
  45.7 11.0 %collective-permute-start.10 = (f32[256,128]{1,0:T(8,128)}, f32[256,128]{1,0:T(8,128)}, u32[]{:S(2)}, u32[]{:S(2)}) collective-permute-start(f32[256,128]{1,0:T(8,128)} %get-tuple-element.36), channel_id=1, source_target_pairs={{0,3},{1,0},{2,1},{3,2},{4,7},{5,4},{6,5},{7,6},{8,11},{9,8},{10,9... | collective-permute-start | bytes 393224 | tf_op jit(solution)/shard_map/ppermute | solution.py:685
  66.6 21.7 %all-to-all-start.1 = ((f32[64,8,128]{2,1,0:T(8,128)}), f32[64,8,128]{2,1,0:T(8,128)}, u32[]{:S(2)}, u32[]{:S(2)}) async-start(f32[64,8,128]{2,1,0:T(8,128)} %bitcast.76), calls=%async_computation.1 | async-start | bytes 524288 | tf_op jit(solution)/shard_map/all_to_all | solution.py:755

commit v3 on v2

--- a/solution.py
+++ b/solution.py
@@ -189,27 +189,24 @@
     first = lane == 0
     last = lane == LANES - 1
     courant = courant.get()
-    signs = []
-    for level in range(2):
-        c = courant[pl.ds(level, rows, stride=2), :]
-        signs.append((jnp.maximum(c, 0.0), jnp.minimum(c, 0.0)))
+    c = courant[pl.ds(0, rows, stride=2), :]
+    positive, negative = jnp.maximum(c, 0.0), jnp.minimum(c, 0.0)
     for d in order:
         copy(d).wait()
         out = outs[d]
-        for level in range(2):
-            positive, negative = signs[level]
-            x = sbuf[d, pl.ds(level, rows, stride=2), :]
-            for step in range(2):
-                below = pltpu.roll(x, 1, 1)
-                below = jnp.where(first, pltpu.roll(below, 1, 0), below)
-                above = pltpu.roll(x, LANES - 1, 1)
-                above = jnp.where(last, pltpu.roll(above, rows - 1, 0), above)
-                x = upwind(x, positive, negative, below, above)
-            out[level * rows : (level + 1) * rows, :] = x
-        out[size : size + 2, :] = sbuf[d, 0:2, :]
-        out[size + 2 : size + 4, :] = sbuf[d, size - 2 : size, :]
-        out[size + 4 : size + 6, :] = courant[0:2, :]
-        out[size + 6 : size + 8, :] = courant[size - 2 : size, :]
+        x = sbuf[d, pl.ds(0, rows, stride=2), :]
+        for step in range(2):
+            below = pltpu.roll(x, 1, 1)
+            below = jnp.where(first, pltpu.roll(below, 1, 0), below)
+            above = pltpu.roll(x, LANES - 1, 1)
+            above = jnp.where(last, pltpu.roll(above, rows - 1, 0), above)
+            x = upwind(x, positive, negative, below, above)
+        out[0:rows, :] = x
+        out[rows : rows + 1, :] = sbuf[d, 0:1, :]
+        out[rows + 1 : rows + 2, :] = sbuf[d, size - 2 : size - 1, :]
+        out[rows + 2 : rows + 3, :] = courant[0:1, :]
+        out[rows + 3 : rows + 4, :] = courant[size - 2 : size - 1, :]
+        out[rows + 4 : rows + 8, :] = jnp.zeros((4, LANES), F32)
 
 
 def mended(first, last, left, right):
@@ -243,22 +240,26 @@
 
 
 def advect_kernel(
-    fields, base, state, courant, mixing, pair, other, lev,
-    o0, o1, o2, o3, factor_out, lows, highs, xbuf, cbuf,
+    fields, sea, air, sea_c, air_c, mixing, pair, other, lev,
+    o0, o1, o2, o3, q0, q1, q2, q3, factor_out, lows, highs, xbuf, cbuf,
 ):
-    rows = courant.shape[0] // 2
+    rows = air_c.shape[0] // 2
     factor_out[...] = mixing.get()[pl.ds(0, rows, stride=8), :]
     lows[...], highs[...] = neighbours(pair, other, lev)
-    for level in range(2):
+    levels = ((air, air_c, 1, 0), (air, air_c, 1, 1), (sea, sea_c, 0, 1))
+    for n, (state, courant, part, level) in enumerate(levels):
+        base = part * 2 * (fields + 1)
         c = courant.get()[pl.ds(level, rows, stride=2), :]
-        at = base + 8 + level
+        at = base + 2 * fields + level
         positive, negative = speeds(c, lows[at : at + 1, :], highs[at : at + 1, :], cbuf)
-        for d, out in enumerate((o0, o1, o2, o3)):
+        outs = (o0, o1, o2, o3) if part else (q0, q1, q2, q3)
+        for d, out in enumerate(outs):
             field = lax.rem(lev[0] + d, fields)
             x = state.get()[pl.ds(field * 2 * rows + level, rows, stride=2), :]
             at = pl.ds(base + 2 * field + level, 1)
             x = stepped(x, lows[at, :], highs[at, :], positive, negative, xbuf)
-            out[level * rows : (level + 1) * rows, :] = x
+            at = n * rows if part else 0
+            out[at : at + rows, :] = x
 
 
 def weight_copies(weight, wbuf, sems):
@@ -392,9 +393,9 @@
     field.wait()
     own.wait()
     copies[AHEAD].start()
-    ends = values[2 * rows :, :]
+    ends = values[rows:, :]
     mended_rows = mended(
-        (ends[0:1], ends[4:5]), (ends[2:3], ends[6:7]), *outer_rows(halo, lev[0] % 4, 0, lev)
+        (ends[0:1], ends[2:3]), (ends[1:2], ends[3:4]), *outer_rows(halo, lev[0] % 4, 0, lev)
     )
     for n, at in enumerate((0, rows - 1)):
         values[at : at + 1, :] = mend(values[at : at + 1, :], mended_rows[n], n == 1)
@@ -480,20 +481,31 @@
 
 
 def solve_kernel(with_flux, p0, p1, p2, p3, *refs):
+    rest = (p0, p1, p2, p3)
     if with_flux:
         mixing, extra, lev, out, buf, sems = refs
-        sources = [((p0, p1, p2, p3), buf, 0)]
+        groups = extra.shape[0]
+        moves = [(rest, 0, 2 * groups, buf, 0)]
     else:
-        h0, h1, h2, h3, mixing, extra, lev, out, unit_out, buf, halo, sems = refs
-        sources = [((p0, p1, p2, p3), buf, 0), ((h0, h1, h2, h3), halo, 4)]
-    groups = extra.shape[0]
+        *more, mixing, extra, lev, out, unit_out, buf, halo, sems = refs
+        groups = extra.shape[0]
+        moves = [
+            (rest, 0, groups, buf, groups),
+            (more[:4], 0, groups, buf, 0),
+            (more[:4], groups, 8, buf, 2 * groups),
+            (more[4:], 0, halo.shape[1], halo, 0),
+        ]
     chunk = 16
     levels = 8
     copies = []
-    for parts, to, base in sources:
+    for n, (parts, at, count, to, base) in enumerate(moves):
         for d, part in enumerate(parts):
             source = lax.rem(lev[0] + 4 - d, 4)
-            copies.append(pltpu.make_async_copy(part, to.at[source], sems.at[base + d]))
+            copies.append(
+                pltpu.make_async_copy(
+                    part.at[pl.ds(at, count)], to.at[source, pl.ds(base, count)], sems.at[n, d]
+                )
+            )
     for copy in copies:
         copy.start()
     kbuf, ebuf = mixing.get(), extra.get()
@@ -501,20 +513,18 @@
         copy.wait()
     if not with_flux:
         parts = [[[], []] for n in range(4)]
-        for level in range(levels):
-            at = 2 * groups + level % 2
-            ends = [buf[level // 2, at + 2 * n : at + 2 * n + 1, :] for n in range(4)]
-            left, right = outer_rows(halo.at[level // 2], lev[0] % 4, level % 2, lev)
+        for source in range(levels // 2):
+            ends = [buf[source, 2 * groups + n : 2 * groups + n + 1, :] for n in range(4)]
+            left, right = outer_rows(halo.at[source], lev[0] % 4, 0, lev)
             for n, rows in enumerate(((ends[0], ends[2]), (ends[1], ends[3]), left, right)):
                 parts[n][0].append(rows[0])
                 parts[n][1].append(rows[1])
         mended_rows = mended(*[[jnp.concatenate(rows, 0) for rows in part] for part in parts])
-        for level in range(levels):
-            at = (level % 2) * groups
-            for n, row in enumerate((at, at + groups - 1)):
-                old = buf[level // 2, row : row + 1, :]
-                new = mended_rows[n][level : level + 1]
-                buf[level // 2, row : row + 1, :] = mend(old, new, n == 1)
+        for source in range(levels // 2):
+            for n, row in enumerate((0, groups - 1)):
+                old = buf[source, row : row + 1, :]
+                new = mended_rows[n][source : source + 1]
+                buf[source, row : row + 1, :] = mend(old, new, n == 1)
 
     def body(step, carry):
         at = pl.multiple_of(step * chunk, chunk)
@@ -688,7 +698,7 @@
 
     sea_own = call(
         functools.partial(sea_kernel, fields),
-        (shape(size + 8, LANES),) * 4,
+        (shape(rows + 8, LANES),) * 4,
         (states[0], states[2], lev_ref),
         "hfs",
         scratch=[pltpu.VMEM((4, size, LANES), F32), DMA((4,))],
@@ -739,7 +749,7 @@
         (*sea, *halo, mask, place_up, labels, up_rows, lev_ref),
         "hhhhhhhhfffhs",
         scratch=[
-            pltpu.VMEM((size + 8, LANES), F32),
+            pltpu.VMEM((rows + 8, LANES), F32),
             pltpu.VMEM(halo[0].shape, F32),
             *workspace(16),
             DMA((2,)),
@@ -755,20 +765,17 @@
         y = lax.all_to_all(y, "tiles", split_axis=0, concat_axis=0, tiled=True)
         return y.reshape(x.shape)
 
-    def advected(state, courant, base, name):
-        return call(
-            functools.partial(advect_kernel, fields, base),
-            (shape(size, LANES),) * 4 + (shape(rows, LANES),),
-            (state, courant, air_k, *ends, lev_ref),
-            "fffffs",
-            scratch=[pltpu.VMEM((20, LANES), F32)] * 2 + [extended, extended],
-            name=name,
-            us=2.5,
-            after=(outgoing,),
-        )
-
-    *air, factor = advected(states[1], states[3], 10, "advect_air")
-    air = around(air)
+    *rest, factor = call(
+        functools.partial(advect_kernel, fields),
+        (shape(size, LANES),) * 4 + (shape(rows, LANES),) * 5,
+        (*states, air_k, *ends, lev_ref),
+        "fffffffs",
+        scratch=[pltpu.VMEM((20, LANES), F32)] * 2 + [extended, extended],
+        name="advect",
+        us=4.0,
+        after=(outgoing,),
+    )
+    air = around(rest[:4])
     arrived = over_tiles(outgoing)
     flux, returning, labels_down = call(
         middle_kernel,
@@ -780,27 +787,29 @@
         us=8.0,
     )
     gained = over_tiles(returning)
+    sea_rest = around(rest[4:])
 
     column = shape(8 * rows, LANES)
 
-    def solve(with_flux, parts, k, extra, name):
-        part, halo_part = (4, *parts[0].shape), (4, *halo[0].shape)
+    def solve(with_flux, parts, k, extra, name, after=()):
+        buf = pltpu.VMEM((4, 2 * rows if with_flux else 2 * rows + 8, LANES), F32)
         return call(
             functools.partial(solve_kernel, with_flux),
             column if with_flux else (column, column),
             (*parts, k, extra, lev_ref),
             "h" * len(parts) + "ffs",
             scratch=[
-                pltpu.VMEM(part, F32),
-                *([] if with_flux else [pltpu.VMEM(halo_part, F32)]),
-                DMA((len(parts),)),
+                buf,
+                *([] if with_flux else [pltpu.VMEM((4, *halo[0].shape), F32)]),
+                DMA((1 if with_flux else 4, 4)),
             ],
             name=name,
             us=3.0,
+            after=after,
         )
 
-    base, unit = solve(False, [*sea, *halo], sea_k, mask, "solve_sea")
     air_out = solve(True, air, air_k, flux, "solve_air")
+    base, unit = solve(False, [*sea_rest, *sea, *halo], sea_k, mask, "solve_sea", (air_out,))
     sea_out = call(
         last_kernel,
         column,

time: 91.3 us -> 89.9 us (0.985)
  waiting for transfers between devices: 26 us -> 19.8 us
  starting transfers between devices: 33.2 us -> 37.5 us
    all_to_all x2, waiting for transfers between devices: 12.8 us -> 4.29 us  [over_tiles(): y = lax.all_to_all(y, 'tiles', split_axis=0, concat_axis=0, tiled=True)]
    all_to_all x2, starting transfers between devices: 12.8 us -> 17.6 us  [over_tiles(): y = lax.all_to_all(y, 'tiles', split_axis=0, concat_axis=0, tiled=True)]
    ppermute x1, starting transfers between devices: 2.55 us -> 0.01 us  [on_device(): lax.ppermute(to_pair, 'tiles', pairs)]
    ppermute x9 -> x12, waiting for transfers between devices: 13.2 us -> 15.5 us  [around(): lax.ppermute(parts[d], 'lev', [(i, (i + d) % levs) for i in range(levs)])]
    ppermute x1, starting transfers between devices: 9.58 us -> 11.4 us  [on_device(): lax.ppermute(to_other, 'tiles', others)]
    ppermute x9 -> x12, starting transfers between devices: 8.31 us -> 8.53 us  [around(): lax.ppermute(parts[d], 'lev', [(i, (i + d) % levs) for i in range(levs)])]
  transfers between devices with their start and end apart: 13 -> 16, of which waited for: 8 -> 9; matrix products, arithmetic and copies ran while one was open for 1% -> 1% of each run, Pallas kernels for 16% -> 17%
where the time goes in v3:
time: 89.9 us; the launch traced here: 89.4 us
  starting transfers between devices  37.5 us (42%)
  Pallas kernels  29.8 us (33%)
  waiting for transfers between devices  19.8 us (22%)
  between operations  0.95 us (1%)
    pallas_call x9, Pallas kernels, call(): pl.pallas_call(body, out_shape=shapes, in_specs=[{'v': VMEM, 's': SMEM, '...  29.8 us
    all_to_all x2, starting transfers between devices, over_tiles(): y = lax.all_to_all(y, 'tiles', split_axis=0, concat_axis=0, tiled=True)  17.6 us
    ppermute x12, waiting for transfers between devices, around(): lax.ppermute(parts[d], 'lev', [(i, (i + d) % levs) for i in range(levs)])  15.5 us
    ppermute x1, starting transfers between devices, on_device(): lax.ppermute(to_other, 'tiles', others)  11.4 us
    ppermute x12, starting transfers between devices, around(): lax.ppermute(parts[d], 'lev', [(i, (i + d) % levs) for i in range(levs)])  8.53 us
    all_to_all x2, waiting for transfers between devices, over_tiles(): y = lax.all_to_all(y, 'tiles', split_axis=0, concat_axis=0, tiled=True)  4.29 us
  transfers between devices with their start and end apart: 16, of which 9 were waited for; matrix products, arithmetic and copies ran while one was open for 1% of the time, Pallas kernels for 17%

profile of v3, /device:TPU:1, one launch (start us, length us, event | category | flops | bytes accessed | tf_op | source)
XLA Modules:
  0.0 89.4 jit_solution(16162616507550639191)
XLA Ops:
  0.6 1.7 %edges.1 = (f32[20,128]{1,0:T(8,128)}, f32[20,128]{1,0:T(8,128)}) custom-call(f32[1024,128]{1,0:T(8,128)} %bitcast.61, f32[1024,128]{1,0:T(8,128)} %bitcast.66, f32[256,128]{1,0:T(8,128)} %bitcast.71, f32[256,128]{1,0:T(8,128)} %bitcast.76, s32[1]{0:T(128)} %bitcast.23.refs_4_.refs_2_.refs_12_.refs_7_.refs_8_.refs_6_.refs_14_), custom_call_target="tpu_custom_call" | custom-call | bytes 5400000 | tf_op jit(solution)/shard_map/edges/pallas_call | solution.py:610
  2.3 11.4 %collective-permute-start.1 = (f32[20,128]{1,0:T(8,128)}, f32[20,128]{1,0:T(8,128)}, u32[]{:S(2)}, u32[]{:S(2)}) collective-permute-start(f32[20,128]{1,0:T(8,128)} %get-tuple-element.28), channel_id=1, source_target_pairs={{0,252},{4,8},{8,4},{12,16},{16,12},{20,24},{24,20},{28,32},{32,28... | collective-permute-start | bytes 30728 | tf_op jit(solution)/shard_map/ppermute | solution.py:689
  13.7 0.0 collective-permute-start
  13.7 2.6 %sea.1 = (f32[136,128]{1,0:T(8,128)}, f32[136,128]{1,0:T(8,128)}, f32[136,128]{1,0:T(8,128)}, f32[136,128]{1,0:T(8,128)}) custom-call(f32[1024,128]{1,0:T(8,128)} %bitcast.62, f32[256,128]{1,0:T(8,128)} %bitcast.72, s32[1]{0:T(128)} %bitcast.23.refs_4_.refs_2_.refs_12_.refs_7_.refs_8_.refs_6_.refs_14_, f32[20,128]{1,0:T(8,128)} %get-tuple-element.27.refs_3_), custom_call_target="tpu_custom_call" | custom-call | bytes 10800000 | tf_op jit(solution)/shard_map/sea/pallas_call | solution.py:610
  16.3 1.2 %collective-permute-start.2 = (f32[136,128]{1,0:T(8,128)}, f32[136,128]{1,0:T(8,128)}, u32[]{:S(2)}, u32[]{:S(2)}) collective-permute-start(f32[136,128]{1,0:T(8,128)} %get-tuple-element.30), channel_id=1, source_target_pairs={{0,1},{1,2},{2,3},{3,0},{4,5},{5,6},{6,7},{7,4},{8,9},{9,10},{10,1... | collective-permute-start | bytes 208904 | tf_op jit(solution)/shard_map/ppermute | solution.py:695
  17.5 1.2 %collective-permute-start.3 = (f32[136,128]{1,0:T(8,128)}, f32[136,128]{1,0:T(8,128)}, u32[]{:S(2)}, u32[]{:S(2)}) collective-permute-start(f32[136,128]{1,0:T(8,128)} %get-tuple-element.31), channel_id=1, source_target_pairs={{0,2},{1,3},{2,0},{3,1},{4,6},{5,7},{6,4},{7,5},{8,10},{9,11},{10,... | collective-permute-start | bytes 208904 | tf_op jit(solution)/shard_map/ppermute | solution.py:695
  18.7 0.0 collective-permute-start.4
  18.7 2.1 %prepare.1 = (s32[2,512]{1,0:T(2,128)}, s32[2,512]{1,0:T(2,128)}, f32[64,128]{1,0:T(8,128)}, f32[128,128]{1,0:T(8,128)}, f32[8,128]{1,0:T(8,128)}) custom-call(s32[2,256]{1,0:T(2,128)} %bitcast.79, s32[2,256]{1,0:T(2,128)} %bitcast.80, s32[2,256]{1,0:T(2,128)} %bitcast.81, s32[2,256]{1,0:T(2,128)} %bitcast.82, s32[1,256]{1,0:T(1,128)} %bitcast.83, ...), custom_call_target="tpu_custom_call" | custom-call | bytes 9000000 | tf_op jit(solution)/shard_map/prepare/pallas_call | solution.py:610
  20.8 0.0 collective-permute-done.1.refs_6_
  20.8 0.0 collective-permute-done.refs_5_
  20.8 0.7 pad_maximum_fusion.refs_4_.refs_8_
  21.6 0.0 copy-start
  21.6 0.8 collective-permute-start.7
  22.3 1.2 %collective-permute-start.6 = (f32[48,128]{1,0:T(8,128)S(1)}, f32[48,128]{1,0:T(8,128)S(1)}, u32[]{:S(2)}, u32[]{:S(2)}) collective-permute-start(f32[48,128]{1,0:T(8,128)S(1)} %pad_maximum_fusion.refs_4_.refs_8_), channel_id=1, source_target_pairs={{0,2},{1,3},{2,0},{3,1},{4,6},{5,7},{6,4},{7,5},{8,10},{9,11},{10,... | collective-permute-start | bytes 73736 | tf_op jit(solution)/shard_map/ppermute | solution.py:695
  23.5 1.5 %collective-permute-done.7.refs_7_.refs_11_ = f32[48,128]{1,0:T(8,128)S(1)} collective-permute-done((f32[48,128]{1,0:T(8,128)S(1)}, f32[48,128]{1,0:T(8,128)S(1)}, u32[]{:S(2)}, u32[]{:S(2)}) %collective-permute-start.7) | collective-permute-done | bytes 24608 | tf_op jit(solution)/shard_map/ppermute | solution.py:695
  25.0 0.0 copy-done
  25.0 0.0 copy-start.1
  25.0 0.0 collective-permute-start.5
  25.0 0.1 collective-permute-done.6.refs_6_.refs_10_
  25.2 1.1 %collective-permute-done.5.refs_5_.refs_9_ = f32[48,128]{1,0:T(8,128)S(1)} collective-permute-done((f32[48,128]{1,0:T(8,128)S(1)}, f32[48,128]{1,0:T(8,128)S(1)}, u32[]{:S(2)}, u32[]{:S(2)}) %collective-permute-start.5) | collective-permute-done | bytes 24608 | tf_op jit(solution)/shard_map/ppermute | solution.py:695
  26.2 0.0 copy-done.1
  26.2 0.0 collective-permute-done.2.refs_1_.refs_5_
  26.2 0.0 copy-done.2
  26.2 0.0 collective-permute-done.3.refs_2_.refs_6_
  26.3 0.6 copy-done.3
  26.8 0.0 collective-permute-done.4.refs_3_.refs_7_
  26.8 5.5 %upward.1.refs_8_ = f32[1088,128]{1,0:T(8,128)} custom-call(f32[136,128]{1,0:T(8,128)} %get-tuple-element.29.refs_5_.refs_0_.refs_4_, f32[136,128]{1,0:T(8,128)} %collective-permute-done.2.refs_1_.refs_5_, f32[136,128]{1,0:T(8,128)} %collective-permute-done.3.refs_2_.refs_6_, f32[136,128]{1,0:T(8,128)} %collective-permute-done.4.refs_3_.refs_7_, ...), custom_call_target="tpu_custom_call" | custom-call | bytes 28800000 | tf_op jit(solution)/shard_map/upward/pallas_call | solution.py:610
  32.4 5.7 %all-to-all-start = ((f32[64,1,2176]{2,1,0:T(1,128)}), f32[64,1,2176]{2,1,0:T(1,128)}, u32[]{:S(2)}, u32[]{:S(2)}) async-start(f32[64,1,2176]{2,1,0:T(1,128)} %bitcast.60), calls=%async_computation | async-start | bytes 1114112 | tf_op jit(solution)/shard_map/all_to_all | solution.py:765
  38.0 4.0 %advect.1 = (f32[256,128]{1,0:T(8,128)}, f32[256,128]{1,0:T(8,128)}, f32[256,128]{1,0:T(8,128)}, f32[256,128]{1,0:T(8,128)}, f32[128,128]{1,0:T(8,128)}, /*index...) custom-call(f32[1024,128]{1,0:T(8,128)} %bitcast.63, f32[1024,128]{1,0:T(8,128)} %bitcast.67, ...), custom_call_target="tpu_custom_call" | custom-call | bytes 14400000 | tf_op jit(solution)/shard_map/advect/pallas_call | solution.py:610
  42.0 2.0 %collective-permute-start.8 = (f32[256,128]{1,0:T(8,128)}, f32[256,128]{1,0:T(8,128)}, u32[]{:S(2)}, u32[]{:S(2)}) collective-permute-start(f32[256,128]{1,0:T(8,128)} %get-tuple-element.38), channel_id=1, source_target_pairs={{0,1},{1,2},{2,3},{3,0},{4,5},{5,6},{6,7},{7,4},{8,9},{9,10},{10,1... | collective-permute-start | bytes 393224 | tf_op jit(solution)/shard_map/ppermute | solution.py:695
  44.0 1.4 %collective-permute-start.9 = (f32[256,128]{1,0:T(8,128)}, f32[256,128]{1,0:T(8,128)}, u32[]{:S(2)}, u32[]{:S(2)}) collective-permute-start(f32[256,128]{1,0:T(8,128)} %get-tuple-element.39), channel_id=1, source_target_pairs={{0,2},{1,3},{2,0},{3,1},{4,6},{5,7},{6,4},{7,5},{8,10},{9,11},{10,... | collective-permute-start | bytes 393224 | tf_op jit(solution)/shard_map/ppermute | solution.py:695
  45.4 0.0 collective-permute-start.10
  45.4 3.7 %collective-permute-done.8.refs_2_.refs_1_ = f32[256,128]{1,0:T(8,128)} collective-permute-done((f32[256,128]{1,0:T(8,128)}, f32[256,128]{1,0:T(8,128)}, u32[]{:S(2)}, u32[]{:S(2)}) %collective-permute-start.8) | collective-permute-done | bytes 131104 | tf_op jit(solution)/shard_map/ppermute | solution.py:695
  49.1 5.3 %collective-permute-done.9.refs_3_.refs_2_ = f32[256,128]{1,0:T(8,128)} collective-permute-done((f32[256,128]{1,0:T(8,128)}, f32[256,128]{1,0:T(8,128)}, u32[]{:S(2)}, u32[]{:S(2)}) %collective-permute-start.9) | collective-permute-done | bytes 131104 | tf_op jit(solution)/shard_map/ppermute | solution.py:695
  54.5 0.7 collective-permute-done.10.refs_4_.refs_3_
  55.1 0.0 all-to-all-done
  55.1 5.3 %middle.1 = (f32[128,128]{1,0:T(8,128)}, f32[512,128]{1,0:T(8,128)}, f32[64,128]{1,0:T(8,128)}) custom-call(f32[1088,128]{1,0:T(8,128)} %bitcast.33.refs_0_, f32[256,128]{1,0:T(8,128)} %get-tuple-element.37.refs_1_.refs_0_, f32[256,128]{1,0:T(8,128)} %collective-permute-done.8.refs_2_.refs_1_, f32[256,128]{1,0:T(8,128)} %collective-permute-done.9.refs_3_.refs_2_, ...), custom_call_target="tpu_custom_call" | custom-call | bytes 28800000 | tf_op jit(solution)/shard_map/middle/pallas_call | solution.py:610
  60.4 11.9 %all-to-all-start.1 = ((f32[64,8,128]{2,1,0:T(8,128)}), f32[64,8,128]{2,1,0:T(8,128)}, u32[]{:S(2)}, u32[]{:S(2)}) async-start(f32[64,8,128]{2,1,0:T(8,128)} %bitcast.78), calls=%async_computation.1 | async-start | bytes 524288 | tf_op jit(solution)/shard_map/all_to_all | solution.py:765
  72.3 0.1 collective-permute-start.11
  72.4 0.7 collective-permute-start.12
  73.1 0.1 collective-permute-start.13
  73.1 2.9 %solve_air.1.refs_15_ = f32[1024,128]{1,0:T(8,128)} custom-call(f32[256,128]{1,0:T(8,128)} %get-tuple-element.37.refs_1_.refs_0_, f32[256,128]{1,0:T(8,128)} %collective-permute-done.8.refs_2_.refs_1_, f32[256,128]{1,0:T(8,128)} %collective-permute-done.9.refs_3_.refs_2_, f32[256,128]{1,0:T(8,128)} %collective-permute-done.10.refs_4_.refs_3_, ...), custom_call_target="tpu_custom_call" | custom-call | bytes 10800000 | tf_op jit(solution)/shard_map/solve_air/pallas_call | solution.py:610
  76.0 0.0 collective-permute-done.11.refs_1_
  76.0 0.8 collective-permute-done.12.refs_2_
  76.8 2.4 %collective-permute-done.13.refs_3_ = f32[128,128]{1,0:T(8,128)} collective-permute-done((f32[128,128]{1,0:T(8,128)}, f32[128,128]{1,0:T(8,128)}, u32[]{:S(2)}, u32[]{:S(2)}) %collective-permute-start.13) | collective-permute-done | bytes 65568 | tf_op jit(solution)/shard_map/ppermute | solution.py:695
  79.2 3.5 %solve_sea.1 = (f32[1024,128]{1,0:T(8,128)}, f32[1024,128]{1,0:T(8,128)}) custom-call(f32[128,128]{1,0:T(8,128)} %get-tuple-element.46.refs_0_, f32[128,128]{1,0:T(8,128)} %collective-permute-done.11.refs_1_, f32[128,128]{1,0:T(8,128)} %collective-permute-done.12.refs_2_, f32[128,128]{1,0:T(8,128)} %collective-permute-done.13.refs_3_, ...), custom_call_target="tpu_custom_call" | custom-call | bytes 10800000 | tf_op jit(solution)/shard_map/solve_sea/pallas_call | solution.py:610
  82.7 4.3 %all-to-all-done.1 = f32[64,8,128]{2,1,0:T(8,128)} async-done(((f32[64,8,128]{2,1,0:T(8,128)}), f32[64,8,128]{2,1,0:T(8,128)}, u32[]{:S(2)}, u32[]{:S(2)}) %all-to-all-start.1) | async-done | bytes 262176 | tf_op jit(solution)/shard_map/all_to_all | solution.py:765
  87.0 2.3 %last.1 = f32[1024,128]{1,0:T(8,128)} custom-call(f32[512,128]{1,0:T(8,128)} %bitcast.41.refs_0_, f32[64,128]{1,0:T(8,128)} %get-tuple-element.45.refs_1_, f32[1024,128]{1,0:T(8,128)} %get-tuple-element.50.refs_2_, f32[1024,128]{1,0:T(8,128)} %get-tuple-element.51.refs_3_), custom_call_target="tpu_custom_call" | custom-call | bytes 7200000 | tf_op jit(solution)/shard_map/last/pallas_call | solution.py:610
  (2 shorter events, 0.0 us)
Async XLA Ops:
  2.3 18.5 %collective-permute-start.1 = (f32[20,128]{1,0:T(8,128)}, f32[20,128]{1,0:T(8,128)}, u32[]{:S(2)}, u32[]{:S(2)}) collective-permute-start(f32[20,128]{1,0:T(8,128)} %get-tuple-element.28), channel_id=1, source_target_pairs={{0,252},{4,8},{8,4},{12,16},{16,12},{20,24},{24,20},{28,32},{32,28... | collective-permute-start | bytes 30728 | tf_op jit(solution)/shard_map/ppermute | solution.py:689
  13.7 7.1 %collective-permute-start = (f32[20,128]{1,0:T(8,128)}, f32[20,128]{1,0:T(8,128)}, u32[]{:S(2)}, u32[]{:S(2)}) collective-permute-start(f32[20,128]{1,0:T(8,128)} %get-tuple-element.27.refs_3_), channel_id=1, source_target_pairs={{0,4},{4,0},{8,12},{12,8},{16,20},{20,16},{24,28},{28,24},{32,36},... | collective-permute-start | bytes 30728 | tf_op jit(solution)/shard_map/ppermute | solution.py:688
  16.3 9.9 %collective-permute-start.2 = (f32[136,128]{1,0:T(8,128)}, f32[136,128]{1,0:T(8,128)}, u32[]{:S(2)}, u32[]{:S(2)}) collective-permute-start(f32[136,128]{1,0:T(8,128)} %get-tuple-element.30), channel_id=1, source_target_pairs={{0,1},{1,2},{2,3},{3,0},{4,5},{5,6},{6,7},{7,4},{8,9},{9,10},{10,1... | collective-permute-start | bytes 208904 | tf_op jit(solution)/shard_map/ppermute | solution.py:695
  17.5 8.7 %collective-permute-start.3 = (f32[136,128]{1,0:T(8,128)}, f32[136,128]{1,0:T(8,128)}, u32[]{:S(2)}, u32[]{:S(2)}) collective-permute-start(f32[136,128]{1,0:T(8,128)} %get-tuple-element.31), channel_id=1, source_target_pairs={{0,2},{1,3},{2,0},{3,1},{4,6},{5,7},{6,4},{7,5},{8,10},{9,11},{10,... | collective-permute-start | bytes 208904 | tf_op jit(solution)/shard_map/ppermute | solution.py:695
  18.7 8.1 %collective-permute-start.4 = (f32[136,128]{1,0:T(8,128)}, f32[136,128]{1,0:T(8,128)}, u32[]{:S(2)}, u32[]{:S(2)}) collective-permute-start(f32[136,128]{1,0:T(8,128)} %get-tuple-element.32), channel_id=1, source_target_pairs={{0,3},{1,0},{2,1},{3,2},{4,7},{5,4},{6,5},{7,6},{8,11},{9,8},{10,9... | collective-permute-start | bytes 208904 | tf_op jit(solution)/shard_map/ppermute | solution.py:695
  21.6 3.5 %copy-start = (f32[48,128]{1,0:T(8,128)}, f32[48,128]{1,0:T(8,128)S(1)}, u32[]{:S(2)}) copy-start(f32[48,128]{1,0:T(8,128)S(1)} %pad_maximum_fusion.refs_4_.refs_8_) | copy-start | bytes 73732
  21.6 3.5 %collective-permute-start.7 = (f32[48,128]{1,0:T(8,128)S(1)}, f32[48,128]{1,0:T(8,128)S(1)}, u32[]{:S(2)}, u32[]{:S(2)}) collective-permute-start(f32[48,128]{1,0:T(8,128)S(1)} %pad_maximum_fusion.refs_4_.refs_8_), channel_id=1, source_target_pairs={{0,3},{1,0},{2,1},{3,2},{4,7},{5,4},{6,5},{7,6},{8,11},{9,8},{10,9... | collective-permute-start | bytes 73736 | tf_op jit(solution)/shard_map/ppermute | solution.py:695
  22.3 2.8 %collective-permute-start.6 = (f32[48,128]{1,0:T(8,128)S(1)}, f32[48,128]{1,0:T(8,128)S(1)}, u32[]{:S(2)}, u32[]{:S(2)}) collective-permute-start(f32[48,128]{1,0:T(8,128)S(1)} %pad_maximum_fusion.refs_4_.refs_8_), channel_id=1, source_target_pairs={{0,2},{1,3},{2,0},{3,1},{4,6},{5,7},{6,4},{7,5},{8,10},{9,11},{10,... | collective-permute-start | bytes 73736 | tf_op jit(solution)/shard_map/ppermute | solution.py:695
  25.0 1.2 %copy-start.1 = (f32[48,128]{1,0:T(8,128)}, f32[48,128]{1,0:T(8,128)S(1)}, u32[]{:S(2)}) copy-start(f32[48,128]{1,0:T(8,128)S(1)} %collective-permute-done.7.refs_7_.refs_11_) | copy-start | bytes 73732
  25.0 1.2 %collective-permute-start.5 = (f32[48,128]{1,0:T(8,128)S(1)}, f32[48,128]{1,0:T(8,128)S(1)}, u32[]{:S(2)}, u32[]{:S(2)}) collective-permute-start(f32[48,128]{1,0:T(8,128)S(1)} %pad_maximum_fusion.refs_4_.refs_8_), channel_id=1, source_target_pairs={{0,1},{1,2},{2,3},{3,0},{4,5},{5,6},{6,7},{7,4},{8,9},{9,10},{10,1... | collective-permute-start | bytes 73736 | tf_op jit(solution)/shard_map/ppermute | solution.py:695
  25.1 1.1 %copy-start.2 = (f32[48,128]{1,0:T(8,128)}, f32[48,128]{1,0:T(8,128)S(1)}, u32[]{:S(2)}) copy-start(f32[48,128]{1,0:T(8,128)S(1)} %collective-permute-done.6.refs_6_.refs_10_) | copy-start | bytes 73732
  26.2 0.6 copy-start.3
  32.4 22.8 %all-to-all-start = ((f32[64,1,2176]{2,1,0:T(1,128)}), f32[64,1,2176]{2,1,0:T(1,128)}, u32[]{:S(2)}, u32[]{:S(2)}) async-start(f32[64,1,2176]{2,1,0:T(1,128)} %bitcast.60), calls=%async_computation | async-start | bytes 1114112 | tf_op jit(solution)/shard_map/all_to_all | solution.py:765
  42.0 7.1 %collective-permute-start.8 = (f32[256,128]{1,0:T(8,128)}, f32[256,128]{1,0:T(8,128)}, u32[]{:S(2)}, u32[]{:S(2)}) collective-permute-start(f32[256,128]{1,0:T(8,128)} %get-tuple-element.38), channel_id=1, source_target_pairs={{0,1},{1,2},{2,3},{3,0},{4,5},{5,6},{6,7},{7,4},{8,9},{9,10},{10,1... | collective-permute-start | bytes 393224 | tf_op jit(solution)/shard_map/ppermute | solution.py:695
  44.0 10.5 %collective-permute-start.9 = (f32[256,128]{1,0:T(8,128)}, f32[256,128]{1,0:T(8,128)}, u32[]{:S(2)}, u32[]{:S(2)}) collective-permute-start(f32[256,128]{1,0:T(8,128)} %get-tuple-element.39), channel_id=1, source_target_pairs={{0,2},{1,3},{2,0},{3,1},{4,6},{5,7},{6,4},{7,5},{8,10},{9,11},{10,... | collective-permute-start | bytes 393224 | tf_op jit(solution)/shard_map/ppermute | solution.py:695
  45.4 9.7 %collective-permute-start.10 = (f32[256,128]{1,0:T(8,128)}, f32[256,128]{1,0:T(8,128)}, u32[]{:S(2)}, u32[]{:S(2)}) collective-permute-start(f32[256,128]{1,0:T(8,128)} %get-tuple-element.40), channel_id=1, source_target_pairs={{0,3},{1,0},{2,1},{3,2},{4,7},{5,4},{6,5},{7,6},{8,11},{9,8},{10,9... | collective-permute-start | bytes 393224 | tf_op jit(solution)/shard_map/ppermute | solution.py:695
  60.4 26.6 %all-to-all-start.1 = ((f32[64,8,128]{2,1,0:T(8,128)}), f32[64,8,128]{2,1,0:T(8,128)}, u32[]{:S(2)}, u32[]{:S(2)}) async-start(f32[64,8,128]{2,1,0:T(8,128)} %bitcast.78), calls=%async_computation.1 | async-start | bytes 524288 | tf_op jit(solution)/shard_map/all_to_all | solution.py:765
  72.3 3.7 %collective-permute-start.11 = (f32[128,128]{1,0:T(8,128)}, f32[128,128]{1,0:T(8,128)}, u32[]{:S(2)}, u32[]{:S(2)}) collective-permute-start(f32[128,128]{1,0:T(8,128)} %get-tuple-element.47), channel_id=1, source_target_pairs={{0,1},{1,2},{2,3},{3,0},{4,5},{5,6},{6,7},{7,4},{8,9},{9,10},{10,1... | collective-permute-start | bytes 196616 | tf_op jit(solution)/shard_map/ppermute | solution.py:695
  72.4 4.4 %collective-permute-start.12 = (f32[128,128]{1,0:T(8,128)}, f32[128,128]{1,0:T(8,128)}, u32[]{:S(2)}, u32[]{:S(2)}) collective-permute-start(f32[128,128]{1,0:T(8,128)} %get-tuple-element.48), channel_id=1, source_target_pairs={{0,2},{1,3},{2,0},{3,1},{4,6},{5,7},{6,4},{7,5},{8,10},{9,11},{10,... | collective-permute-start | bytes 196616 | tf_op jit(solution)/shard_map/ppermute | solution.py:695
  73.1 6.1 %collective-permute-start.13 = (f32[128,128]{1,0:T(8,128)}, f32[128,128]{1,0:T(8,128)}, u32[]{:S(2)}, u32[]{:S(2)}) collective-permute-start(f32[128,128]{1,0:T(8,128)} %get-tuple-element.49), channel_id=1, source_target_pairs={{0,3},{1,0},{2,1},{3,2},{4,7},{5,4},{6,5},{7,6},{8,11},{9,8},{10,9... | collective-permute-start | bytes 196616 | tf_op jit(solution)/shard_map/ppermute | solution.py:695

commit v4 on v3

--- a/solution.py
+++ b/solution.py
@@ -684,10 +684,8 @@
     )
     pairs = [(i, i + 1 - 2 * (i % 2)) for i in range(tiles)]
     others = [(i, (i - 1 + 2 * (i % 2)) % tiles) for i in range(tiles)]
-    ends = (
-        lax.ppermute(to_pair, "tiles", pairs),
-        lax.ppermute(to_other, "tiles", others),
-    )
+    from_other = lax.ppermute(to_other, "tiles", others)
+    ends = (lax.ppermute(to_pair, "tiles", pairs), from_other)
     extended = pltpu.VMEM((rows + 16, LANES), F32)
 
     def around(parts):

time: 89.9 us -> 89.9 us (level)
  no operation moved by 1% of the time
where the time goes in v4:
time: 89.9 us; the launch traced here: 89.4 us
  starting transfers between devices  37.5 us (42%)
  Pallas kernels  29.8 us (33%)
  waiting for transfers between devices  19.8 us (22%)
  between operations  0.95 us (1%)
    pallas_call x9, Pallas kernels, call(): pl.pallas_call(body, out_shape=shapes, in_specs=[{'v': VMEM, 's': SMEM, '...  29.8 us
    all_to_all x2, starting transfers between devices, over_tiles(): y = lax.all_to_all(y, 'tiles', split_axis=0, concat_axis=0, tiled=True)  17.6 us
    ppermute x12, waiting for transfers between devices, around(): lax.ppermute(parts[d], 'lev', [(i, (i + d) % levs) for i in range(levs)])  15.5 us
    ppermute x1, starting transfers between devices, on_device(): from_other = lax.ppermute(to_other, 'tiles', others)  11.4 us
    ppermute x12, starting transfers between devices, around(): lax.ppermute(parts[d], 'lev', [(i, (i + d) % levs) for i in range(levs)])  8.53 us
    all_to_all x2, waiting for transfers between devices, over_tiles(): y = lax.all_to_all(y, 'tiles', split_axis=0, concat_axis=0, tiled=True)  4.29 us
  transfers between devices with their start and end apart: 16, of which 9 were waited for; matrix products, arithmetic and copies ran while one was open for 1% of the time, Pallas kernels for 17%

profile of v4, /device:TPU:1, one launch (start us, length us, event | category | flops | bytes accessed | tf_op | source)
XLA Modules:
  0.0 89.4 jit_solution(16162616507550639191)
XLA Ops:
  0.6 1.7 %edges.1 = (f32[20,128]{1,0:T(8,128)}, f32[20,128]{1,0:T(8,128)}) custom-call(f32[1024,128]{1,0:T(8,128)} %bitcast.61, f32[1024,128]{1,0:T(8,128)} %bitcast.66, f32[256,128]{1,0:T(8,128)} %bitcast.71, f32[256,128]{1,0:T(8,128)} %bitcast.76, s32[1]{0:T(128)} %bitcast.23.refs_4_.refs_2_.refs_12_.refs_7_.refs_8_.refs_6_.refs_14_), custom_call_target="tpu_custom_call" | custom-call | bytes 5400000 | tf_op jit(solution)/shard_map/edges/pallas_call | solution.py:610
  2.3 11.4 %collective-permute-start.1 = (f32[20,128]{1,0:T(8,128)}, f32[20,128]{1,0:T(8,128)}, u32[]{:S(2)}, u32[]{:S(2)}) collective-permute-start(f32[20,128]{1,0:T(8,128)} %get-tuple-element.28), channel_id=1, source_target_pairs={{0,252},{4,8},{8,4},{12,16},{16,12},{20,24},{24,20},{28,32},{32,28... | collective-permute-start | bytes 30728 | tf_op jit(solution)/shard_map/ppermute | solution.py:687
  13.7 0.0 collective-permute-start
  13.7 2.6 %sea.1 = (f32[136,128]{1,0:T(8,128)}, f32[136,128]{1,0:T(8,128)}, f32[136,128]{1,0:T(8,128)}, f32[136,128]{1,0:T(8,128)}) custom-call(f32[1024,128]{1,0:T(8,128)} %bitcast.62, f32[256,128]{1,0:T(8,128)} %bitcast.72, s32[1]{0:T(128)} %bitcast.23.refs_4_.refs_2_.refs_12_.refs_7_.refs_8_.refs_6_.refs_14_, f32[20,128]{1,0:T(8,128)} %get-tuple-element.27.refs_3_), custom_call_target="tpu_custom_call" | custom-call | bytes 10800000 | tf_op jit(solution)/shard_map/sea/pallas_call | solution.py:610
  16.3 1.2 %collective-permute-start.2 = (f32[136,128]{1,0:T(8,128)}, f32[136,128]{1,0:T(8,128)}, u32[]{:S(2)}, u32[]{:S(2)}) collective-permute-start(f32[136,128]{1,0:T(8,128)} %get-tuple-element.30), channel_id=1, source_target_pairs={{0,1},{1,2},{2,3},{3,0},{4,5},{5,6},{6,7},{7,4},{8,9},{9,10},{10,1... | collective-permute-start | bytes 208904 | tf_op jit(solution)/shard_map/ppermute | solution.py:693
  17.5 1.2 %collective-permute-start.3 = (f32[136,128]{1,0:T(8,128)}, f32[136,128]{1,0:T(8,128)}, u32[]{:S(2)}, u32[]{:S(2)}) collective-permute-start(f32[136,128]{1,0:T(8,128)} %get-tuple-element.31), channel_id=1, source_target_pairs={{0,2},{1,3},{2,0},{3,1},{4,6},{5,7},{6,4},{7,5},{8,10},{9,11},{10,... | collective-permute-start | bytes 208904 | tf_op jit(solution)/shard_map/ppermute | solution.py:693
  18.7 0.0 collective-permute-start.4
  18.7 2.1 %prepare.1 = (s32[2,512]{1,0:T(2,128)}, s32[2,512]{1,0:T(2,128)}, f32[64,128]{1,0:T(8,128)}, f32[128,128]{1,0:T(8,128)}, f32[8,128]{1,0:T(8,128)}) custom-call(s32[2,256]{1,0:T(2,128)} %bitcast.79, s32[2,256]{1,0:T(2,128)} %bitcast.80, s32[2,256]{1,0:T(2,128)} %bitcast.81, s32[2,256]{1,0:T(2,128)} %bitcast.82, s32[1,256]{1,0:T(1,128)} %bitcast.83, ...), custom_call_target="tpu_custom_call" | custom-call | bytes 9000000 | tf_op jit(solution)/shard_map/prepare/pallas_call | solution.py:610
  20.8 0.0 collective-permute-done.1.refs_6_
  20.8 0.0 collective-permute-done.refs_5_
  20.8 0.7 pad_maximum_fusion.refs_4_.refs_8_
  21.6 0.0 copy-start
  21.6 0.8 collective-permute-start.7
  22.3 1.2 %collective-permute-start.6 = (f32[48,128]{1,0:T(8,128)S(1)}, f32[48,128]{1,0:T(8,128)S(1)}, u32[]{:S(2)}, u32[]{:S(2)}) collective-permute-start(f32[48,128]{1,0:T(8,128)S(1)} %pad_maximum_fusion.refs_4_.refs_8_), channel_id=1, source_target_pairs={{0,2},{1,3},{2,0},{3,1},{4,6},{5,7},{6,4},{7,5},{8,10},{9,11},{10,... | collective-permute-start | bytes 73736 | tf_op jit(solution)/shard_map/ppermute | solution.py:693
  23.5 1.5 %collective-permute-done.7.refs_7_.refs_11_ = f32[48,128]{1,0:T(8,128)S(1)} collective-permute-done((f32[48,128]{1,0:T(8,128)S(1)}, f32[48,128]{1,0:T(8,128)S(1)}, u32[]{:S(2)}, u32[]{:S(2)}) %collective-permute-start.7) | collective-permute-done | bytes 24608 | tf_op jit(solution)/shard_map/ppermute | solution.py:693
  25.0 0.0 copy-done
  25.0 0.0 copy-start.1
  25.0 0.0 collective-permute-start.5
  25.0 0.1 collective-permute-done.6.refs_6_.refs_10_
  25.2 1.1 %collective-permute-done.5.refs_5_.refs_9_ = f32[48,128]{1,0:T(8,128)S(1)} collective-permute-done((f32[48,128]{1,0:T(8,128)S(1)}, f32[48,128]{1,0:T(8,128)S(1)}, u32[]{:S(2)}, u32[]{:S(2)}) %collective-permute-start.5) | collective-permute-done | bytes 24608 | tf_op jit(solution)/shard_map/ppermute | solution.py:693
  26.2 0.0 copy-done.1
  26.2 0.0 collective-permute-done.2.refs_1_.refs_5_
  26.2 0.0 copy-done.2
  26.2 0.0 collective-permute-done.3.refs_2_.refs_6_
  26.3 0.6 copy-done.3
  26.8 0.0 collective-permute-done.4.refs_3_.refs_7_
  26.8 5.5 %upward.1.refs_8_ = f32[1088,128]{1,0:T(8,128)} custom-call(f32[136,128]{1,0:T(8,128)} %get-tuple-element.29.refs_5_.refs_0_.refs_4_, f32[136,128]{1,0:T(8,128)} %collective-permute-done.2.refs_1_.refs_5_, f32[136,128]{1,0:T(8,128)} %collective-permute-done.3.refs_2_.refs_6_, f32[136,128]{1,0:T(8,128)} %collective-permute-done.4.refs_3_.refs_7_, ...), custom_call_target="tpu_custom_call" | custom-call | bytes 28800000 | tf_op jit(solution)/shard_map/upward/pallas_call | solution.py:610
  32.4 5.7 %all-to-all-start = ((f32[64,1,2176]{2,1,0:T(1,128)}), f32[64,1,2176]{2,1,0:T(1,128)}, u32[]{:S(2)}, u32[]{:S(2)}) async-start(f32[64,1,2176]{2,1,0:T(1,128)} %bitcast.60), calls=%async_computation | async-start | bytes 1114112 | tf_op jit(solution)/shard_map/all_to_all | solution.py:763
  38.0 4.0 %advect.1 = (f32[256,128]{1,0:T(8,128)}, f32[256,128]{1,0:T(8,128)}, f32[256,128]{1,0:T(8,128)}, f32[256,128]{1,0:T(8,128)}, f32[128,128]{1,0:T(8,128)}, /*index...) custom-call(f32[1024,128]{1,0:T(8,128)} %bitcast.63, f32[1024,128]{1,0:T(8,128)} %bitcast.67, ...), custom_call_target="tpu_custom_call" | custom-call | bytes 14400000 | tf_op jit(solution)/shard_map/advect/pallas_call | solution.py:610
  42.0 2.0 %collective-permute-start.8 = (f32[256,128]{1,0:T(8,128)}, f32[256,128]{1,0:T(8,128)}, u32[]{:S(2)}, u32[]{:S(2)}) collective-permute-start(f32[256,128]{1,0:T(8,128)} %get-tuple-element.38), channel_id=1, source_target_pairs={{0,1},{1,2},{2,3},{3,0},{4,5},{5,6},{6,7},{7,4},{8,9},{9,10},{10,1... | collective-permute-start | bytes 393224 | tf_op jit(solution)/shard_map/ppermute | solution.py:693
  44.0 1.4 %collective-permute-start.9 = (f32[256,128]{1,0:T(8,128)}, f32[256,128]{1,0:T(8,128)}, u32[]{:S(2)}, u32[]{:S(2)}) collective-permute-start(f32[256,128]{1,0:T(8,128)} %get-tuple-element.39), channel_id=1, source_target_pairs={{0,2},{1,3},{2,0},{3,1},{4,6},{5,7},{6,4},{7,5},{8,10},{9,11},{10,... | collective-permute-start | bytes 393224 | tf_op jit(solution)/shard_map/ppermute | solution.py:693
  45.4 0.0 collective-permute-start.10
  45.4 3.7 %collective-permute-done.8.refs_2_.refs_1_ = f32[256,128]{1,0:T(8,128)} collective-permute-done((f32[256,128]{1,0:T(8,128)}, f32[256,128]{1,0:T(8,128)}, u32[]{:S(2)}, u32[]{:S(2)}) %collective-permute-start.8) | collective-permute-done | bytes 131104 | tf_op jit(solution)/shard_map/ppermute | solution.py:693
  49.1 5.3 %collective-permute-done.9.refs_3_.refs_2_ = f32[256,128]{1,0:T(8,128)} collective-permute-done((f32[256,128]{1,0:T(8,128)}, f32[256,128]{1,0:T(8,128)}, u32[]{:S(2)}, u32[]{:S(2)}) %collective-permute-start.9) | collective-permute-done | bytes 131104 | tf_op jit(solution)/shard_map/ppermute | solution.py:693
  54.5 0.7 collective-permute-done.10.refs_4_.refs_3_
  55.1 0.0 all-to-all-done
  55.1 5.3 %middle.1 = (f32[128,128]{1,0:T(8,128)}, f32[512,128]{1,0:T(8,128)}, f32[64,128]{1,0:T(8,128)}) custom-call(f32[1088,128]{1,0:T(8,128)} %bitcast.33.refs_0_, f32[256,128]{1,0:T(8,128)} %get-tuple-element.37.refs_1_.refs_0_, f32[256,128]{1,0:T(8,128)} %collective-permute-done.8.refs_2_.refs_1_, f32[256,128]{1,0:T(8,128)} %collective-permute-done.9.refs_3_.refs_2_, ...), custom_call_target="tpu_custom_call" | custom-call | bytes 28800000 | tf_op jit(solution)/shard_map/middle/pallas_call | solution.py:610
  60.4 11.9 %all-to-all-start.1 = ((f32[64,8,128]{2,1,0:T(8,128)}), f32[64,8,128]{2,1,0:T(8,128)}, u32[]{:S(2)}, u32[]{:S(2)}) async-start(f32[64,8,128]{2,1,0:T(8,128)} %bitcast.78), calls=%async_computation.1 | async-start | bytes 524288 | tf_op jit(solution)/shard_map/all_to_all | solution.py:763
  72.3 0.1 collective-permute-start.11
  72.4 0.7 collective-permute-start.12
  73.1 0.1 collective-permute-start.13
  73.1 2.9 %solve_air.1.refs_15_ = f32[1024,128]{1,0:T(8,128)} custom-call(f32[256,128]{1,0:T(8,128)} %get-tuple-element.37.refs_1_.refs_0_, f32[256,128]{1,0:T(8,128)} %collective-permute-done.8.refs_2_.refs_1_, f32[256,128]{1,0:T(8,128)} %collective-permute-done.9.refs_3_.refs_2_, f32[256,128]{1,0:T(8,128)} %collective-permute-done.10.refs_4_.refs_3_, ...), custom_call_target="tpu_custom_call" | custom-call | bytes 10800000 | tf_op jit(solution)/shard_map/solve_air/pallas_call | solution.py:610
  76.0 0.0 collective-permute-done.11.refs_1_
  76.0 0.8 collective-permute-done.12.refs_2_
  76.8 2.4 %collective-permute-done.13.refs_3_ = f32[128,128]{1,0:T(8,128)} collective-permute-done((f32[128,128]{1,0:T(8,128)}, f32[128,128]{1,0:T(8,128)}, u32[]{:S(2)}, u32[]{:S(2)}) %collective-permute-start.13) | collective-permute-done | bytes 65568 | tf_op jit(solution)/shard_map/ppermute | solution.py:693
  79.2 3.5 %solve_sea.1 = (f32[1024,128]{1,0:T(8,128)}, f32[1024,128]{1,0:T(8,128)}) custom-call(f32[128,128]{1,0:T(8,128)} %get-tuple-element.46.refs_0_, f32[128,128]{1,0:T(8,128)} %collective-permute-done.11.refs_1_, f32[128,128]{1,0:T(8,128)} %collective-permute-done.12.refs_2_, f32[128,128]{1,0:T(8,128)} %collective-permute-done.13.refs_3_, ...), custom_call_target="tpu_custom_call" | custom-call | bytes 10800000 | tf_op jit(solution)/shard_map/solve_sea/pallas_call | solution.py:610
  82.7 4.3 %all-to-all-done.1 = f32[64,8,128]{2,1,0:T(8,128)} async-done(((f32[64,8,128]{2,1,0:T(8,128)}), f32[64,8,128]{2,1,0:T(8,128)}, u32[]{:S(2)}, u32[]{:S(2)}) %all-to-all-start.1) | async-done | bytes 262176 | tf_op jit(solution)/shard_map/all_to_all | solution.py:763
  87.0 2.3 %last.1 = f32[1024,128]{1,0:T(8,128)} custom-call(f32[512,128]{1,0:T(8,128)} %bitcast.41.refs_0_, f32[64,128]{1,0:T(8,128)} %get-tuple-element.45.refs_1_, f32[1024,128]{1,0:T(8,128)} %get-tuple-element.50.refs_2_, f32[1024,128]{1,0:T(8,128)} %get-tuple-element.51.refs_3_), custom_call_target="tpu_custom_call" | custom-call | bytes 7200000 | tf_op jit(solution)/shard_map/last/pallas_call | solution.py:610
  (2 shorter events, 0.0 us)
Async XLA Ops:
  2.3 18.5 %collective-permute-start.1 = (f32[20,128]{1,0:T(8,128)}, f32[20,128]{1,0:T(8,128)}, u32[]{:S(2)}, u32[]{:S(2)}) collective-permute-start(f32[20,128]{1,0:T(8,128)} %get-tuple-element.28), channel_id=1, source_target_pairs={{0,252},{4,8},{8,4},{12,16},{16,12},{20,24},{24,20},{28,32},{32,28... | collective-permute-start | bytes 30728 | tf_op jit(solution)/shard_map/ppermute | solution.py:687
  13.7 7.1 %collective-permute-start = (f32[20,128]{1,0:T(8,128)}, f32[20,128]{1,0:T(8,128)}, u32[]{:S(2)}, u32[]{:S(2)}) collective-permute-start(f32[20,128]{1,0:T(8,128)} %get-tuple-element.27.refs_3_), channel_id=1, source_target_pairs={{0,4},{4,0},{8,12},{12,8},{16,20},{20,16},{24,28},{28,24},{32,36},... | collective-permute-start | bytes 30728 | tf_op jit(solution)/shard_map/ppermute | solution.py:688
  16.3 9.9 %collective-permute-start.2 = (f32[136,128]{1,0:T(8,128)}, f32[136,128]{1,0:T(8,128)}, u32[]{:S(2)}, u32[]{:S(2)}) collective-permute-start(f32[136,128]{1,0:T(8,128)} %get-tuple-element.30), channel_id=1, source_target_pairs={{0,1},{1,2},{2,3},{3,0},{4,5},{5,6},{6,7},{7,4},{8,9},{9,10},{10,1... | collective-permute-start | bytes 208904 | tf_op jit(solution)/shard_map/ppermute | solution.py:693
  17.5 8.7 %collective-permute-start.3 = (f32[136,128]{1,0:T(8,128)}, f32[136,128]{1,0:T(8,128)}, u32[]{:S(2)}, u32[]{:S(2)}) collective-permute-start(f32[136,128]{1,0:T(8,128)} %get-tuple-element.31), channel_id=1, source_target_pairs={{0,2},{1,3},{2,0},{3,1},{4,6},{5,7},{6,4},{7,5},{8,10},{9,11},{10,... | collective-permute-start | bytes 208904 | tf_op jit(solution)/shard_map/ppermute | solution.py:693
  18.7 8.1 %collective-permute-start.4 = (f32[136,128]{1,0:T(8,128)}, f32[136,128]{1,0:T(8,128)}, u32[]{:S(2)}, u32[]{:S(2)}) collective-permute-start(f32[136,128]{1,0:T(8,128)} %get-tuple-element.32), channel_id=1, source_target_pairs={{0,3},{1,0},{2,1},{3,2},{4,7},{5,4},{6,5},{7,6},{8,11},{9,8},{10,9... | collective-permute-start | bytes 208904 | tf_op jit(solution)/shard_map/ppermute | solution.py:693
  21.6 3.5 %copy-start = (f32[48,128]{1,0:T(8,128)}, f32[48,128]{1,0:T(8,128)S(1)}, u32[]{:S(2)}) copy-start(f32[48,128]{1,0:T(8,128)S(1)} %pad_maximum_fusion.refs_4_.refs_8_) | copy-start | bytes 73732
  21.6 3.5 %collective-permute-start.7 = (f32[48,128]{1,0:T(8,128)S(1)}, f32[48,128]{1,0:T(8,128)S(1)}, u32[]{:S(2)}, u32[]{:S(2)}) collective-permute-start(f32[48,128]{1,0:T(8,128)S(1)} %pad_maximum_fusion.refs_4_.refs_8_), channel_id=1, source_target_pairs={{0,3},{1,0},{2,1},{3,2},{4,7},{5,4},{6,5},{7,6},{8,11},{9,8},{10,9... | collective-permute-start | bytes 73736 | tf_op jit(solution)/shard_map/ppermute | solution.py:693
  22.3 2.8 %collective-permute-start.6 = (f32[48,128]{1,0:T(8,128)S(1)}, f32[48,128]{1,0:T(8,128)S(1)}, u32[]{:S(2)}, u32[]{:S(2)}) collective-permute-start(f32[48,128]{1,0:T(8,128)S(1)} %pad_maximum_fusion.refs_4_.refs_8_), channel_id=1, source_target_pairs={{0,2},{1,3},{2,0},{3,1},{4,6},{5,7},{6,4},{7,5},{8,10},{9,11},{10,... | collective-permute-start | bytes 73736 | tf_op jit(solution)/shard_map/ppermute | solution.py:693
  25.0 1.2 %copy-start.1 = (f32[48,128]{1,0:T(8,128)}, f32[48,128]{1,0:T(8,128)S(1)}, u32[]{:S(2)}) copy-start(f32[48,128]{1,0:T(8,128)S(1)} %collective-permute-done.7.refs_7_.refs_11_) | copy-start | bytes 73732
  25.0 1.2 %collective-permute-start.5 = (f32[48,128]{1,0:T(8,128)S(1)}, f32[48,128]{1,0:T(8,128)S(1)}, u32[]{:S(2)}, u32[]{:S(2)}) collective-permute-start(f32[48,128]{1,0:T(8,128)S(1)} %pad_maximum_fusion.refs_4_.refs_8_), channel_id=1, source_target_pairs={{0,1},{1,2},{2,3},{3,0},{4,5},{5,6},{6,7},{7,4},{8,9},{9,10},{10,1... | collective-permute-start | bytes 73736 | tf_op jit(solution)/shard_map/ppermute | solution.py:693
  25.1 1.1 %copy-start.2 = (f32[48,128]{1,0:T(8,128)}, f32[48,128]{1,0:T(8,128)S(1)}, u32[]{:S(2)}) copy-start(f32[48,128]{1,0:T(8,128)S(1)} %collective-permute-done.6.refs_6_.refs_10_) | copy-start | bytes 73732
  26.2 0.6 copy-start.3
  32.4 22.8 %all-to-all-start = ((f32[64,1,2176]{2,1,0:T(1,128)}), f32[64,1,2176]{2,1,0:T(1,128)}, u32[]{:S(2)}, u32[]{:S(2)}) async-start(f32[64,1,2176]{2,1,0:T(1,128)} %bitcast.60), calls=%async_computation | async-start | bytes 1114112 | tf_op jit(solution)/shard_map/all_to_all | solution.py:763
  42.0 7.1 %collective-permute-start.8 = (f32[256,128]{1,0:T(8,128)}, f32[256,128]{1,0:T(8,128)}, u32[]{:S(2)}, u32[]{:S(2)}) collective-permute-start(f32[256,128]{1,0:T(8,128)} %get-tuple-element.38), channel_id=1, source_target_pairs={{0,1},{1,2},{2,3},{3,0},{4,5},{5,6},{6,7},{7,4},{8,9},{9,10},{10,1... | collective-permute-start | bytes 393224 | tf_op jit(solution)/shard_map/ppermute | solution.py:693
  44.0 10.5 %collective-permute-start.9 = (f32[256,128]{1,0:T(8,128)}, f32[256,128]{1,0:T(8,128)}, u32[]{:S(2)}, u32[]{:S(2)}) collective-permute-start(f32[256,128]{1,0:T(8,128)} %get-tuple-element.39), channel_id=1, source_target_pairs={{0,2},{1,3},{2,0},{3,1},{4,6},{5,7},{6,4},{7,5},{8,10},{9,11},{10,... | collective-permute-start | bytes 393224 | tf_op jit(solution)/shard_map/ppermute | solution.py:693
  45.4 9.7 %collective-permute-start.10 = (f32[256,128]{1,0:T(8,128)}, f32[256,128]{1,0:T(8,128)}, u32[]{:S(2)}, u32[]{:S(2)}) collective-permute-start(f32[256,128]{1,0:T(8,128)} %get-tuple-element.40), channel_id=1, source_target_pairs={{0,3},{1,0},{2,1},{3,2},{4,7},{5,4},{6,5},{7,6},{8,11},{9,8},{10,9... | collective-permute-start | bytes 393224 | tf_op jit(solution)/shard_map/ppermute | solution.py:693
  60.4 26.6 %all-to-all-start.1 = ((f32[64,8,128]{2,1,0:T(8,128)}), f32[64,8,128]{2,1,0:T(8,128)}, u32[]{:S(2)}, u32[]{:S(2)}) async-start(f32[64,8,128]{2,1,0:T(8,128)} %bitcast.78), calls=%async_computation.1 | async-start | bytes 524288 | tf_op jit(solution)/shard_map/all_to_all | solution.py:763
  72.3 3.7 %collective-permute-start.11 = (f32[128,128]{1,0:T(8,128)}, f32[128,128]{1,0:T(8,128)}, u32[]{:S(2)}, u32[]{:S(2)}) collective-permute-start(f32[128,128]{1,0:T(8,128)} %get-tuple-element.47), channel_id=1, source_target_pairs={{0,1},{1,2},{2,3},{3,0},{4,5},{5,6},{6,7},{7,4},{8,9},{9,10},{10,1... | collective-permute-start | bytes 196616 | tf_op jit(solution)/shard_map/ppermute | solution.py:693
  72.4 4.4 %collective-permute-start.12 = (f32[128,128]{1,0:T(8,128)}, f32[128,128]{1,0:T(8,128)}, u32[]{:S(2)}, u32[]{:S(2)}) collective-permute-start(f32[128,128]{1,0:T(8,128)} %get-tuple-element.48), channel_id=1, source_target_pairs={{0,2},{1,3},{2,0},{3,1},{4,6},{5,7},{6,4},{7,5},{8,10},{9,11},{10,... | collective-permute-start | bytes 196616 | tf_op jit(solution)/shard_map/ppermute | solution.py:693
  73.1 6.1 %collective-permute-start.13 = (f32[128,128]{1,0:T(8,128)}, f32[128,128]{1,0:T(8,128)}, u32[]{:S(2)}, u32[]{:S(2)}) collective-permute-start(f32[128,128]{1,0:T(8,128)} %get-tuple-element.49), channel_id=1, source_target_pairs={{0,3},{1,0},{2,1},{3,2},{4,7},{5,4},{6,5},{7,6},{8,11},{9,8},{10,9... | collective-permute-start | bytes 196616 | tf_op jit(solution)/shard_map/ppermute | solution.py:693
